TPU v7x, 256 devices: a whole 4x4x8 slice. The times are simulated.
256 devices in a mesh: dp: 8 (over z_hi, y), tensor: 8 (over z_lo, core), section: 4 (over x).
Axes of the slice: x: 4, y: 4, z: 8 (z_hi: 2, z_lo: 4; z = z_hi * 4 + z_lo), core: 2. Of those that a mesh axis runs over, the one named last changes fastest.
Arguments:
- tokens_in: bfloat16 [40960, 5120], P(('section', 'dp', 'tensor')), parts along dimension 0, may hold values from -4 to 4
- key_cot: bfloat16 [40960, 1024], P(('section', 'dp'), 'tensor'), parts along dimension 0, may hold values from -3 to 3, as said below
- row_mask: int32 [40960], P(('section', 'dp', 'tensor')), parts along dimension 0, may hold values 0 or 1
- w_key: bfloat16 [20480, 1024], P('section', 'tensor'), parts along dimension 0, may hold values from -0.078125 to 0.078125
- momentum: bfloat16 [8, 20480, 1024], P('dp', 'section', 'tensor'), parts along dimension 1, may hold values from -4 to 4
Outputs:
- input_grad: bfloat16 [40960, 5120], P(('section', 'dp', 'tensor')), parts along dimension 0
- new_momentum: bfloat16 [8, 20480, 1024], P('dp', 'section', 'tensor'), parts along dimension 1
- rollout_weight: bfloat16 [8, 20480, 256], P('tensor', 'section'), parts along dimension 1
There are 4 independent parts, one for each index of `section`. A program takes and returns all parts, laid end to end along the dimension named above; each array names one. Nothing has to cross between parts.
Inputs may be any that keep to these rules, and one draw needn't show every extreme that they name: `key_cot`: every entry is a multiple of 0.125.
All inputs are finite; a program needn't handle non-finite values. No bound on the sum of `row_mask` on one device may be relied on, other than what follows from the above.
Results may differ from a plain program's by a relative error of at most 0.017.
Values may be sent and summed in bfloat16 or wider, within the bound.
No kernel may reach another device: no remote copies, remote signals or barrier semaphores. Data moves between devices by JAX's collectives and lax.ppermute only.
A program may use at most 128 MiB of HBM per device.

v0:
```python
import jax
import jax.numpy as jnp
from jax import lax
from jax.sharding import PartitionSpec as P

beta_slow = 0.99
beta_vote = 0.9
step_rate = 0.02


def swapped(array, axis, stride):
    return lax.ppermute(array, axis, [(i, i ^ 1 << stride) for i in range(lax.axis_size(axis))])


def unpack_words(packed):
    bit_shifts = jnp.arange(32, dtype=jnp.int32)[:, None]
    return jnp.bitwise_and(jnp.right_shift(packed[..., None, :], bit_shifts), 1)


def per_device(tokens_in, key_cot, row_mask, w_key, momentum):
    features = w_key.shape[0]
    head_cols = w_key.shape[1]
    worker_count = lax.axis_size("dp")
    mask_half = row_mask.astype(jnp.bfloat16)
    token_block = lax.all_gather(tokens_in, "tensor", axis=0, tiled=True)
    mask_block = lax.all_gather(mask_half, "tensor", axis=0, tiled=True)
    cot_block = key_cot * mask_block[:, None]
    key_grad = lax.dot_general(
        token_block, cot_block, (((0,), (0,)), ((), ())), preferred_element_type=jnp.float32
    )
    prior_momentum = momentum[0].astype(jnp.float32)
    new_momentum = (beta_slow * prior_momentum + (1.0 - beta_slow) * key_grad).astype(jnp.bfloat16)[
        None
    ]
    interp = beta_vote * prior_momentum + (1.0 - beta_vote) * key_grad
    positive = (interp > 0).astype(jnp.int32).reshape(features // 32, 32, head_cols)
    bit_shifts = jnp.arange(32, dtype=jnp.int32)[:, None]
    packed_signs = jnp.sum(jnp.left_shift(positive, bit_shifts), axis=1, dtype=jnp.int32)
    vote_count = jnp.sum(
        unpack_words(lax.all_gather(packed_signs[None], "dp", axis=0, tiled=True)),
        axis=0,
        dtype=jnp.int32,
    ).reshape(features, head_cols)
    direction = jnp.sign((2 * vote_count - worker_count).astype(jnp.float32))
    updated = (w_key.astype(jnp.float32) - step_rate * direction).astype(jnp.bfloat16)
    column_block = updated
    position = lax.axis_index("tensor")
    partner = swapped(column_block, "tensor", 0)
    lower_half = jnp.bitwise_and(jnp.right_shift(position, 0), 1) == 0
    column_block = jnp.where(
        lower_half,
        jnp.concatenate([column_block, partner], 1),
        jnp.concatenate([partner, column_block], 1),
    )
    rollout_weight = column_block[None]
    product = lax.dot_general(
        key_cot, w_key, (((1,), (1,)), ((), ())), preferred_element_type=jnp.float32
    )
    summed_grad = lax.psum_scatter(
        lax.optimization_barrier(product.astype(jnp.bfloat16))
        .astype(jnp.float32)
        .astype(jnp.bfloat16),
        "tensor",
        scatter_dimension=0,
        tiled=True,
    ).astype(jnp.float32)
    input_grad = (summed_grad * row_mask.astype(jnp.float32)[:, None]).astype(jnp.bfloat16)
    return (input_grad, new_momentum, rollout_weight)


def solution(mesh):
    return jax.shard_map(
        per_device,
        mesh=mesh,
        in_specs=(
            P(("section", "dp", "tensor"), None),
            P(("section", "dp"), "tensor"),
            P(("section", "dp", "tensor")),
            P("section", "tensor"),
            P("dp", "section", "tensor"),
        ),
        out_specs=(
            P(("section", "dp", "tensor"), None),
            P("dp", "section", "tensor"),
            P("tensor", "section", None),
        ),
        check_vma=False,
    )
```

profile of v0, /device:TPU:1, one launch (start us, length us, event | category | flops | bytes accessed | tf_op | source)
XLA Modules:
  0.0 312.5 jit_solution(4321463678229362600)
XLA Ops:
  7.2 0.0 all-gather.3.cloned.1.call-start
  7.2 0.7 all-gather.3.cloned.1.call-update
  7.9 0.0 reduce-scatter.2.cloned.1.call-start
  7.9 9.7 %convolution_convert_fusion = bf16[1280,5120]{1,0:T(8,128)(2,1)} fusion(bf16[1280,128]{1,0:T(8,128)(2,1)} %param.6, bf16[5120,128]{1,0:T(8,128)(2,1)} %param.8), kind=kOutput, calls=%fused_computation.1 | convolution fusion | flops 1684275200 | bytes 14745600 | tf_op jit(solution)/shard_map/dot_general | solution.py:56
  17.6 0.0 copy-start.2
  17.6 0.0 reduce-scatter.2.cloned.1.call-update
  17.6 0.0 copy-start.4
  17.7 0.0 copy-start.3
  17.7 0.0 copy-start.1
  17.7 1.2 copy-done.2
  18.9 0.6 copy.13
  19.6 0.0 copy-done.4
  19.6 0.6 dynamic-slice
  20.8 0.0 copy-done.3
  20.8 0.2 dynamic-update-slice
  21.1 16.3 %all-reduce = bf16[1280]{0:T(1024)(128)(2,1)S(1)} all-reduce(bf16[1280]{0:T(1024)(128)(2,1)S(1)} %dynamic-update-slice), channel_id=1, replica_groups=mesh['dp'=8,'tensor'=8,'section'=4] {'tensor'}, use_global_device_ids=true, to_apply=%add | all-reduce | flops 1280 | bytes 5120
  37.4 112.4 %all-gather.3.cloned.1.call-done = bf16[1280,5120]{1,0:T(8,128)(2,1)} async-done(((bf16[160,5120]{1,0:T(8,128)(2,1)}), bf16[1280,5120]{1,0:T(8,128)(2,1)}) %all-gather.3.cloned.1.call-update) | async-done | bytes 13107216 | tf_op jit(solution)/shard_map/all_gather | solution.py:25
  149.8 0.0 copy-done.1
  149.8 9.7 %fusion.7 = (s32[5120,128]{0,1:T(8,128)}, f32[128,5120]{1,0:T(8,128)}) fusion(bf16[1,5120,128]{1,2,0:T(8,128)(2,1)S(1)} %copy.13, bf16[1280,5120]{1,0:T(8,128)(2,1)} %all-gather.3.cloned.1.call-done, bf16[1280,128]{1,0:T(8,128)(2,1)S(1)} %copy-done.1, bf16[1280]{0:T(1024)(128)(2,1)S(1)} %all-reduce), kind=kOutput, calls=%fused_computation.16 | convolution fusion | flops 1681817600 | bytes 19991040 | tf_op jit(solution)/shard_map/dot_general | solution.py:28
  159.5 3.2 %copy.14 = s32[5120,128]{1,0:T(8,128)} copy(s32[5120,128]{0,1:T(8,128)} %get-tuple-element.14) | data formatting | bytes 5242880 | tf_op jit(solution)/shard_map/reshape | solution.py:36
  162.7 2.3 shift-left_reduce_fusion
  165.0 46.3 %all-gather = s32[1280,128]{1,0:T(8,128)S(1)} all-gather(s32[160,128]{1,0:T(8,128)S(1)} %shift-left_reduce_fusion), channel_id=2, replica_groups=mesh['dp'=8,'tensor'=8,'section'=4] {'dp'}, dimensions={0}, use_global_device_ids=true | all-gather | bytes 737280 | tf_op jit(solution)/shard_map/all_gather | solution.py:40
  211.3 3.2 %and_reduce_fusion = s32[160,32,128]{2,1,0:T(8,128)S(1)} fusion(s32[8,160,128]{2,1,0:T(8,128)S(1)} %bitcast.39), kind=kLoop, calls=%fused_computation | loop fusion | flops 15073280 | bytes 3276800 | tf_op jit(solution)/shard_map/reduce_sum | solution.py:39
  214.4 0.0 copy-start
  214.5 0.9 sign_multiply_fusion
  215.4 0.4 copy-done
  215.8 1.3 fusion.6
  217.1 6.7 %collective-permute-start = (bf16[5120,128]{1,0:T(8,128)(2,1)}, bf16[5120,128]{1,0:T(8,128)(2,1)}, u32[]{:S(2)}, u32[]{:S(2)}) collective-permute-start(bf16[5120,128]{1,0:T(8,128)(2,1)} %fusion.6), channel_id=1, source_target_pairs={{0,4},{4,0},{8,12},{12,8},{16,20},{20,16},{24,28},{28,24},{1,5},{5... | collective-permute-start | bytes 3932168 | tf_op jit(solution)/shard_map/ppermute | solution.py:12
  223.7 2.2 fusion.8
  225.9 1.4 copy.15
  227.3 0.0 collective-permute-done
  227.3 4.3 %maximum_select_fusion = bf16[1,5120,256]{2,1,0:T(8,128)(2,1)} fusion(bf16[1,5120,128]{2,1,0:T(8,128)(2,1)} %bitcast.10, bf16[1,5120,128]{2,1,0:T(8,128)(2,1)} %bitcast.9, pred[]{:T(512)S(6)} %eq.3), kind=kLoop, calls=%fused_computation.11 | loop fusion | flops 11796480 | bytes 5242881 | tf_op jit(solution)/shard_map/jit(_where)/select_n | solution.py:50
  231.7 71.1 %reduce-scatter.2.cloned.1.call-done = bf16[160,5120]{1,0:T(8,128)(2,1)} async-done(((bf16[1280,5120]{1,0:T(8,128)(2,1)}), bf16[160,5120]{1,0:T(8,128)(2,1)}) %reduce-scatter.2.cloned.1.call-update) | async-done | bytes 1638416 | tf_op jit(solution)/shard_map/reduce_scatter | solution.py:59
  302.7 3.0 multiply_convert_fusion
  (2 shorter events, 0.0 us)
Async XLA Ops:
  7.2 142.6 %all-gather.3.cloned.1.call-start = ((), (), s32[]{:S(2)}) async-start(), calls=%async_computation.2 | async-start | bytes 14745600 | tf_op jit(solution)/shard_map/all_gather | solution.py:25
  7.9 294.8 %reduce-scatter.2.cloned.1.call-start = ((), (), s32[]{:S(2)}) async-start(), calls=%async_computation.1 | async-start | bytes 14745600 | tf_op jit(solution)/shard_map/reduce_scatter | solution.py:59
  17.6 1.3 copy-start.2
  17.6 1.9 copy-start.4
  17.7 3.2 %copy-start.3 = (s32[160]{0:T(256)S(1)}, s32[160]{0:T(256)}, u32[]{:S(2)}) copy-start(s32[160]{0:T(256)} %param.7) | copy-start | bytes 1924
  17.7 132.1 %copy-start.1 = (bf16[1280,128]{1,0:T(8,128)(2,1)S(1)}, bf16[1280,128]{1,0:T(8,128)(2,1)}, u32[]{:S(2)}) copy-start(bf16[1280,128]{1,0:T(8,128)(2,1)} %param.6) | copy-start | bytes 983044
  214.4 1.3 copy-start
  217.1 10.3 %collective-permute-start = (bf16[5120,128]{1,0:T(8,128)(2,1)}, bf16[5120,128]{1,0:T(8,128)(2,1)}, u32[]{:S(2)}, u32[]{:S(2)}) collective-permute-start(bf16[5120,128]{1,0:T(8,128)(2,1)} %fusion.6), channel_id=1, source_target_pairs={{0,4},{4,0},{8,12},{12,8},{16,20},{20,16},{24,28},{28,24},{1,5},{5... | collective-permute-start | bytes 3932168 | tf_op jit(solution)/shard_map/ppermute | solution.py:12
Sparse Core Ops, SparseCore 0:
  9.8 139.9 all-gather.2
  152.4 150.3 reduce-scatter.1
where the time goes:
time: 314 us; the launch traced here: 313 us
  waiting for transfers between devices  184 us (59%)
  blocking collectives  62.6 us (20%)
  matrix products  19.3 us (6%)
  other arithmetic  17.2 us (5%)
  between operations  14.8 us (5%)
  local copies, waits for them, and re-layouts  7.73 us (2%)
  starting transfers between devices  6.74 us (2%)
    all_gather x1, waiting for transfers between devices, per_device(): token_block = lax.all_gather(tokens_in, 'tensor', axis=0, tiled=True)  112 us
    reduce_scatter x1, waiting for transfers between devices, per_device(): lax.psum_scatter(lax.optimization_barrier(product.astype(jnp.bfloat16)).a...  71.1 us
    all_gather x1, blocking collectives, per_device(): lax.all_gather(packed_signs[None], 'dp', axis=0, tiled=True)  46.3 us
    unnamed x1, blocking collectives  16.3 us
    dot_general x1, matrix products, per_device(): lax.dot_general(key_cot, w_key, (((1,), (1,)), ((), ())), preferred_eleme...  9.67 us
    dot_general x1, matrix products, per_device(): lax.dot_general(token_block, cot_block, (((0,), (0,)), ((), ())), preferr...  9.66 us
    ppermute x1, starting transfers between devices, swapped(): lax.ppermute(array, axis, [(i, i ^ 1 << stride) for i in range(lax.axis_s...  6.66 us
  transfers between devices with their start and end apart: 3, of which 2 were waited for; matrix products, arithmetic and copies ran while one was open for 13% of the time, Pallas kernels for 0%

commit v1 on v0

v1 whole, which is shorter than its diff:
```python
import jax
import jax.numpy as jnp
from jax import lax
from jax.experimental import pallas as pl
from jax.experimental.pallas import tpu as pltpu
from jax.sharding import PartitionSpec as P

beta_slow = 0.99
beta_vote = 0.9
step_rate = 0.02

AXES = ("dp", "tensor")
HI, YS, LINE, CORES = 2, 4, 4, 2
WIDTH = 512
VMEM = 48 * 1024 * 1024


def permute(array, place):
    pairs = []
    for hi in range(HI):
        for y in range(YS):
            for c in range(LINE):
                for k in range(CORES):
                    to = place(hi, y, c, k)
                    if to is not None:
                        h2, y2, c2, k2 = to
                        source = ((hi * YS + y) * LINE + c) * CORES + k
                        target = ((h2 % HI * YS + y2 % YS) * LINE + c2) * CORES + k2
                        pairs.append((source, target))
    return lax.ppermute(array, AXES, pairs)


def core_swap(array):
    return permute(array, lambda h, y, c, k: (h, y, c, 1 - k))


def along_y(array, step):
    return permute(array, lambda h, y, c, k: (h, y - step, c, k))


def along_z(array, step):
    def place(h, y, c, k):
        z = (h * LINE + c - step) % (HI * LINE)
        return z // LINE, y, z % LINE, k

    return permute(array, place)


def opposite_heads(array):
    def place(h, y, c, k):
        z = (h * LINE + c + (2 if c >= 2 else -2)) % (HI * LINE)
        return z // LINE, y, z % LINE, k

    return permute(array, place)


def inward(array):
    return permute(array, lambda h, y, c, k: (h, y, c ^ 1, k) if c in (0, 3) else None)


def outward(array, flip=0):
    return permute(array, lambda h, y, c, k: (h ^ flip, y, c ^ 1, k) if c in (1, 2) else None)


def across(array):
    return permute(array, lambda h, y, c, k: (h, y, 3 - c, k) if c in (1, 2) else None)


def inner_flip(array):
    return permute(array, lambda h, y, c, k: (h ^ 1, y, c, k) if c in (1, 2) else None)


def params():
    return pltpu.CompilerParams(vmem_limit_bytes=VMEM)


def momentum_kernel(*refs):
    tokens = refs[:8]
    cot, prior_own, prior_side, new_own, new_side, words_own, words_side = refs[8:]
    rows = jnp.concatenate([ref[...] for ref in tokens], 0)
    grad = lax.dot_general(
        cot[...], rows, (((1,), (0,)), ((), ())), preferred_element_type=jnp.float32
    ).T
    for i, (prior, new, words) in enumerate(
        ((prior_own, new_own, words_own), (prior_side, new_side, words_side))
    ):
        part = grad[:, i * 128 : (i + 1) * 128]
        before = prior[...].astype(jnp.float32)
        new[...] = (beta_slow * before + (1.0 - beta_slow) * part).astype(jnp.bfloat16)
        positive = (beta_vote * before + (1.0 - beta_vote) * part > 0).astype(jnp.int32)
        step = WIDTH // 32
        packed = positive[:step]
        for bit in range(1, 32):
            packed = packed | (positive[bit * step : (bit + 1) * step] << bit)
        words[...] = packed


def momentum_step(tokens, cot, prior_own, prior_side, start, size):
    first = start // WIDTH
    token_specs = [
        pl.BlockSpec((160, WIDTH), (lambda i: (0, i + first)) if whole else (lambda i: (0, i)))
        for _, whole in tokens
    ]
    prior_spec = pl.BlockSpec((WIDTH, 128), lambda i: (i + first, 0))
    grad_spec = pl.BlockSpec((WIDTH, 128), lambda i: (i, 0))
    word_spec = pl.BlockSpec((WIDTH // 32, 128), lambda i: (i, 0))
    return pl.pallas_call(
        momentum_kernel,
        grid=(size // WIDTH,),
        in_specs=token_specs
        + [pl.BlockSpec((256, 1280), lambda i: (0, 0)), prior_spec, prior_spec],
        out_specs=[grad_spec, grad_spec, word_spec, word_spec],
        out_shape=[jax.ShapeDtypeStruct((size, 128), jnp.bfloat16)] * 2
        + [jax.ShapeDtypeStruct((size // 32, 128), jnp.int32)] * 2,
        compiler_params=params(),
        cost_estimate=pl.CostEstimate(
            flops=2 * size * 1280 * 256, bytes_accessed=size * 1280 * 2 + size * 1024, transcendentals=0
        ),
        name="momentum_step",
    )(*[array for array, _ in tokens], cot, prior_own, prior_side)


def majority(words):
    def half(a, b):
        return a ^ b, a & b

    def full(a, b, c):
        x = a ^ b
        return x ^ c, (a & b) | (x & c)

    s0, c0 = full(words[0], words[1], words[2])
    s1, c1 = full(words[3], words[4], words[5])
    s2, c2 = half(words[6], words[7])
    ones, c3 = full(s0, s1, s2)
    t0, d0 = full(c0, c1, c2)
    twos, d1 = half(t0, c3)
    fours, eights = half(d0, d1)
    more = eights | (fours & (ones | twos))
    fewer = ~(eights | fours)
    return more, fewer


def vote_kernel(core, words_own, words_other, w_own, w_other, out):
    is_low = core[0] == 0
    step = WIDTH // 32
    updated = []
    for words, weights in ((words_own, w_own), (words_other, w_other)):
        more, fewer = majority([words[i] for i in range(8)])
        direction = jnp.concatenate(
            [((more >> bit) & 1) - ((fewer >> bit) & 1) for bit in range(32)], 0
        ).astype(jnp.float32)
        updated.append((weights[...].astype(jnp.float32) - step_rate * direction).astype(jnp.bfloat16))
    out[:, :128] = jnp.where(is_low, updated[0], updated[1])
    out[:, 128:] = jnp.where(is_low, updated[1], updated[0])


def vote_step(core, words_own, words_other, w_own, w_other):
    features = w_own.shape[0]
    word_spec = pl.BlockSpec((8, WIDTH // 32, 128), lambda i, core: (0, i, 0))
    weight_spec = pl.BlockSpec((WIDTH, 128), lambda i, core: (i, 0))
    return pl.pallas_call(
        vote_kernel,
        grid_spec=pltpu.PrefetchScalarGridSpec(
            num_scalar_prefetch=1,
            grid=(features // WIDTH,),
            in_specs=[word_spec, word_spec, weight_spec, weight_spec],
            out_specs=pl.BlockSpec((WIDTH, 256), lambda i, core: (i, 0)),
        ),
        out_shape=jax.ShapeDtypeStruct((features, 256), jnp.bfloat16),
        compiler_params=params(),
        cost_estimate=pl.CostEstimate(flops=features * 256 * 8, bytes_accessed=features * 1280, transcendentals=0),
        name="vote_step",
    )(core, words_own, words_other, w_own, w_other)


def partial_kernel(place, cot, weights, out):
    out[...] = lax.dot_general(
        cot[...], weights[0], (((1,), (1,)), ((), ())), preferred_element_type=jnp.float32
    ).astype(jnp.bfloat16)


def total_kernel(place, cot, weights, other, mask, out):
    total = lax.dot_general(
        cot[...], weights[0], (((1,), (1,)), ((), ())), preferred_element_type=jnp.float32
    ) + other[...].astype(jnp.float32)
    out[...] = (total * mask[...]).astype(jnp.bfloat16)


def input_step(place, cot, weights, other=None, mask=None):
    blocks, width, depth = weights.shape
    rows = cot.shape[0]
    out_spec = pl.BlockSpec((rows, width), lambda i, place: (0, place[i]))
    in_specs = [
        pl.BlockSpec((rows, depth), lambda i, place: (0, 0)),
        pl.BlockSpec((1, width, depth), lambda i, place: (i, 0, 0)),
    ]
    args = [cot, weights]
    if other is not None:
        in_specs += [out_spec, pl.BlockSpec((rows, 1), lambda i, place: (0, 0))]
        args += [other, mask]
    return pl.pallas_call(
        partial_kernel if other is None else total_kernel,
        grid_spec=pltpu.PrefetchScalarGridSpec(
            num_scalar_prefetch=1, grid=(blocks,), in_specs=in_specs, out_specs=out_spec
        ),
        out_shape=jax.ShapeDtypeStruct((rows, blocks * width), jnp.bfloat16),
        compiler_params=params(),
        cost_estimate=pl.CostEstimate(
            flops=2 * rows * depth * blocks * width,
            bytes_accessed=2 * (depth + 2 * rows) * blocks * width,
            transcendentals=0,
        ),
        name="input_step",
    )(place, *args)


def after(array, *others):
    return lax.optimization_barrier((array, *others))[0]


def per_device(tokens_in, key_cot, row_mask, w_key, momentum):
    position = lax.axis_index("tensor")
    chip, core = position // CORES, position % CORES
    y = lax.axis_index("dp") % YS
    inner = (chip == 1) | (chip == 2)
    features = w_key.shape[0]
    share = tokens_in.shape[0]
    quarter = features // YS
    cut = 2560

    tokens = jnp.where(row_mask[:, None] != 0, tokens_in, jnp.zeros_like(tokens_in))
    low, high = tokens[:, :cut], tokens[:, cut:]
    prior = momentum[0]

    def cot_rows(array, of_chip, of_core):
        return lax.dynamic_slice(array, ((of_chip * CORES + of_core) * share, 0), (share, 128))

    w_part = lax.dynamic_slice(w_key, (y * quarter, 0), (quarter, 128))
    w_up, w_down = along_z(w_part, 1), along_z(w_part, -1)
    w_far = opposite_heads(w_part)
    cot_pieces = []
    for step in (0, 1, 3, 2):
        rows = lax.dynamic_slice(
            key_cot, ((chip - step) % LINE * CORES * share, 0), (CORES * share, 128)
        )
        if step:
            rows = permute(rows, lambda h, y, c, k, step=step: (h, y, (c - step) % LINE, k))
        cot_pieces.append(rows)
    cot_mine = jnp.concatenate(cot_pieces, 1)
    cot_side = inward(key_cot)
    w_other = core_swap(w_key)

    from_across = across(tokens)
    from_side = [inward(low), inward(high)]
    w_here = jnp.concatenate([w_part, w_up, w_down, w_far], 1)
    w_next, w_before = along_y(w_here, 1), along_y(w_here, -1)
    w_next_far = along_y(w_next[: quarter // 2], 1)
    w_before_far = along_y(w_before[quarter // 2 :], -1)
    weights = jnp.concatenate([w_here, w_next, w_before, w_next_far, w_before_far], 0).reshape(
        8, quarter // 2, 512
    )
    from_far = [across(part) for part in from_side]
    prior_side = inward(prior)

    own_swapped = core_swap(tokens)
    across_swapped = core_swap(from_across)
    side_swapped = [core_swap(part) for part in from_side]
    far_swapped = [core_swap(part) for part in from_far]

    both = jnp.concatenate([key_cot, cot_side], 1)
    order = [chip, chip ^ 1, 3 - chip, (3 - chip) ^ 1]
    cot_all = jnp.concatenate(
        [
            lax.dynamic_slice(both, ((of_chip * CORES + of_core) * share, 0), (share, 256))
            for of_chip in order
            for of_core in (core, 1 - core)
        ],
        0,
    ).T
    new_own, new_side, words_own, words_side = [], [], [], []
    for i, (start, size) in enumerate(((0, cut), (cut, features - cut))):
        parts = [
            (tokens, True),
            (own_swapped, True),
            (from_side[i], False),
            (side_swapped[i], False),
            (from_across, True),
            (across_swapped, True),
            (from_far[i], False),
            (far_swapped[i], False),
        ]
        results = momentum_step(parts, cot_all, prior, prior_side, start, size)
        new_own.append(results[0])
        new_side.append(outward(results[1]))
        words_own.append(results[2])
        words_side.append(results[3])
    new_momentum = jnp.where(
        inner, jnp.concatenate(new_own, 0), jnp.concatenate(new_side, 0)
    )[None]

    mine, side = jnp.concatenate(words_own, 0), jnp.concatenate(words_side, 0)
    mine_flip = inner_flip(mine)
    side_here = outward(side)
    side_flip = outward(side, 1)
    pair = jnp.where(inner, jnp.stack([mine, mine_flip]), jnp.stack([side_here, side_flip]))
    words = jnp.concatenate([pair, along_y(pair, 1), along_y(pair, -1), along_y(pair, 2)], 0)
    words_other = core_swap(words)
    rollout_weight = vote_step(core[None], words, words_other, w_key, w_other)[None]

    quarters = jnp.stack([y, (y + 1) % YS, (y + 3) % YS, (y + 2) % YS])
    place = (quarters[:, None] * 2 + jnp.arange(2)[None, :]).reshape(8).astype(jnp.int32)
    theirs = lax.dynamic_slice(cot_mine, ((1 - core) * share, 0), (share, 512))
    ours = lax.dynamic_slice(cot_mine, (core * share, 0), (share, 512))
    other = core_swap(input_step(place, theirs, weights))
    input_grad = input_step(place, ours, weights, other, row_mask.astype(jnp.float32)[:, None])
    return (input_grad, new_momentum, rollout_weight)


def solution(mesh):
    return jax.shard_map(
        per_device,
        mesh=mesh,
        in_specs=(
            P(("section", "dp", "tensor"), None),
            P(("section", "dp"), "tensor"),
            P(("section", "dp", "tensor")),
            P("section", "tensor"),
            P("dp", "section", "tensor"),
        ),
        out_specs=(
            P(("section", "dp", "tensor"), None),
            P("dp", "section", "tensor"),
            P("tensor", "section", None),
        ),
        check_vma=False,
    )
```

time: 314 us -> 235 us (0.75)
  waiting for transfers between devices: 184 us -> 102 us
  blocking collectives: 62.6 us -> 0 us
  starting transfers between devices: 6.74 us -> 62.9 us
  Pallas kernels: 0 us -> 34.3 us
  matrix products: 19.3 us -> 0 us
  local copies, waits for them, and re-layouts: 7.73 us -> 21.7 us
  between operations: 14.8 us -> 1.09 us
  other arithmetic: 17.2 us -> 11.2 us
    all_gather x1 -> x0, waiting for transfers between devices: 112 us -> none  [per_device(): token_block = lax.all_gather(tokens_in, 'tensor', axis=0, tiled=True)]
    ppermute x1 -> x34, waiting for transfers between devices: 0.01 us -> 102 us  [permute(): return lax.ppermute(array, AXES, pairs)]
    reduce_scatter x1 -> x0, waiting for transfers between devices: 71.1 us -> none  [per_device(): lax.psum_scatter(lax.optimization_barrier(product.astype(jnp.bfloat16)).a...]
    ppermute x1 -> x34, starting transfers between devices: 6.66 us -> 62.9 us  [permute(): return lax.ppermute(array, AXES, pairs)]
    all_gather x1 -> x0, blocking collectives: 46.3 us -> none  [per_device(): lax.all_gather(packed_signs[None], 'dp', axis=0, tiled=True)]
    pallas_call x0 -> x5, Pallas kernels: none -> 34.3 us  [the longest x2 16.3 us: input_step(): pl.pallas_call(partial_kernel if other is None else total_kernel, grid_sp...]
    dot_general x2 -> x0, matrix products: 19.3 us -> none  [the longest x1 9.67 us: per_device(): lax.dot_general(key_cot, w_key, (((1,), (1,)), ((), ())), preferred_eleme...]
    unnamed x1 -> x0, blocking collectives: 16.3 us -> none
  transfers between devices with their start and end apart: 3 -> 34, of which waited for: 2 -> 13; matrix products, arithmetic and copies ran while one was open for 13% -> 12% of each run, Pallas kernels for 0% -> 13%
where the time goes in v1:
time: 235 us; the launch traced here: 233 us
  waiting for transfers between devices  102 us (43%)
  starting transfers between devices  62.9 us (27%)
  Pallas kernels  34.3 us (15%)
  local copies, waits for them, and re-layouts  21.7 us (9%)
  other arithmetic  11.2 us (5%)
    ppermute x34, waiting for transfers between devices, permute(): return lax.ppermute(array, AXES, pairs)  102 us
    ppermute x34, starting transfers between devices, permute(): return lax.ppermute(array, AXES, pairs)  62.9 us
    pallas_call x2, Pallas kernels, input_step(): pl.pallas_call(partial_kernel if other is None else total_kernel, grid_sp...  16.3 us
    pallas_call x2, Pallas kernels, momentum_step(): pl.pallas_call(momentum_kernel, grid=(size // WIDTH,), in_specs=token_spe...  13.1 us
    unnamed x42, local copies, waits for them, and re-layouts  11 us
    pallas_call x1, Pallas kernels, vote_step(): pl.pallas_call(vote_kernel, grid_spec=pltpu.PrefetchScalarGridSpec(num_sc...  4.85 us
  transfers between devices with their start and end apart: 34, of which 13 were waited for; matrix products, arithmetic and copies ran while one was open for 12% of the time, Pallas kernels for 13%

profile of v1, /device:TPU:1, one launch (start us, length us, event | category | flops | bytes accessed | tf_op | source)
XLA Modules:
  0.0 232.8 jit_solution(1956052272825594954)
XLA Ops:
  0.7 1.7 constant_dynamic-slice_fusion.6
  2.4 3.8 %collective-permute-start.2 = (bf16[320,128]{1,0:T(8,128)(2,1)}, bf16[320,128]{1,0:T(8,128)(2,1)S(1)}, u32[]{:S(2)}, u32[]{:S(2)}) collective-permute-start(bf16[320,128]{1,0:T(8,128)(2,1)} %get-tuple-element.36), channel_id=1, source_target_pairs={{0,16},{4,20},{8,24},{12,28},{16,0},{20,4},{24,8},{28,12},{32,48},... | collective-permute-start | bytes 245768 | tf_op jit(solution)/shard_map/ppermute | solution.py:30
  6.3 1.6 collective-permute-start.1
  7.9 1.6 collective-permute-start
  9.5 0.7 broadcast_compare_fusion
  10.2 1.6 broadcast_select_fusion.refs_0_
  11.9 1.3 fusion.8
  13.5 1.8 collective-permute-start.20
  15.4 2.0 collective-permute-start.5
  17.4 2.1 collective-permute-start.4
  20.7 3.7 %collective-permute-start.12 = (bf16[160,2560]{1,0:T(8,128)(2,1)}, bf16[160,2560]{1,0:T(8,128)(2,1)}, u32[]{:S(2)}, u32[]{:S(2)}) collective-permute-start(bf16[160,2560]{1,0:T(8,128)(2,1)} %get-tuple-element.19), channel_id=1, source_target_pairs={{0,8},{4,12},{24,16},{28,20},{32,40},{36,44},{56,48},{60,52},{64,7... | collective-permute-start | bytes 2457608 | tf_op jit(solution)/shard_map/ppermute | solution.py:30
  24.6 5.2 %collective-permute-done.5 = bf16[1280,128]{1,0:T(8,128)(2,1)S(1)} collective-permute-done((bf16[1280,128]{1,0:T(8,128)(2,1)S(1)}, bf16[1280,128]{1,0:T(8,128)(2,1)S(1)}, u32[]{:S(2)}, u32[]{:S(2)}) %collective-permute-start.5) | collective-permute-done | bytes 327712 | tf_op jit(solution)/shard_map/ppermute | solution.py:30
  29.8 4.6 %collective-permute-start.11 = (bf16[160,5120]{1,0:T(8,128)(2,1)}, bf16[160,5120]{1,0:T(8,128)(2,1)}, u32[]{:S(2)}, u32[]{:S(2)}) collective-permute-start(bf16[160,5120]{1,0:T(8,128)(2,1)} %copy-done.9), channel_id=1, source_target_pairs={{0,4},{4,0},{8,12},{12,8},{16,20},{20,16},{24,28},{28,24},{32,36},... | collective-permute-start | bytes 4915208 | tf_op jit(solution)/shard_map/ppermute | solution.py:30
  34.3 11.2 %collective-permute-done.4 = bf16[1280,128]{1,0:T(8,128)(2,1)} collective-permute-done((bf16[1280,128]{1,0:T(8,128)(2,1)S(1)}, bf16[1280,128]{1,0:T(8,128)(2,1)}, u32[]{:S(2)}, u32[]{:S(2)}) %collective-permute-start.4) | collective-permute-done | bytes 327712 | tf_op jit(solution)/shard_map/ppermute | solution.py:30
  45.5 1.9 collective-permute-start.14
  47.4 4.3 %collective-permute-start.18 = (bf16[1280,128]{0,1:T(8,128)(2,1)S(1)}, bf16[1280,128]{0,1:T(8,128)(2,1)S(1)}, u32[]{:S(2)}, u32[]{:S(2)}) collective-permute-start(bf16[1280,128]{0,1:T(8,128)(2,1)S(1)} %copy.12), channel_id=1, source_target_pairs={{0,8},{4,12},{24,16},{28,20},{32,40},{36,44},{56,48},{60,52},{64,7... | collective-permute-start | bytes 983048 | tf_op jit(solution)/shard_map/ppermute | solution.py:30
  51.7 2.4 %pad_maximum_fusion = (bf16[1280,512]{1,0:T(8,128)(2,1)S(1)}, bf16[5120,512]{1,0:T(8,128)(2,1)}) fusion(bf16[1280,128]{1,0:T(8,128)(2,1)S(1)} %collective-permute-done.5, bf16[1280,128]{1,0:T(8,128)(2,1)} %collective-permute-done.4, bf16[1280,128]{1,0:T(8,128)(2,1)} %collective-permute-done.3, bf16[1280,128]{1,0:T(8,128)(2,1)S(1)} %constant_dynamic-slice_fusion.1), kind=kLoop, calls=%fused_computation.1 | loop fusion | flops 5242879 | bytes 3932160 | tf_op jit(solution)/shard_map/concatenate | solution.py:255
  54.0 16.1 %collective-permute-done.18 = bf16[1280,128]{0,1:T(8,128)(2,1)S(1)} collective-permute-done((bf16[1280,128]{0,1:T(8,128)(2,1)S(1)}, bf16[1280,128]{0,1:T(8,128)(2,1)S(1)}, u32[]{:S(2)}, u32[]{:S(2)}) %collective-permute-start.18) | collective-permute-done | bytes 327712 | tf_op jit(solution)/shard_map/ppermute | solution.py:30
  70.1 2.7 %collective-permute-start.6 = (bf16[1280,512]{1,0:T(8,128)(2,1)S(1)}, bf16[1280,512]{1,0:T(8,128)(2,1)}, u32[]{:S(2)}, u32[]{:S(2)}) collective-permute-start(bf16[1280,512]{1,0:T(8,128)(2,1)S(1)} %get-tuple-element.21), channel_id=1, source_target_pairs={{0,96},{4,100},{8,104},{12,108},{16,112},{20,116},{24,120},{28,124... | collective-permute-start | bytes 3932168 | tf_op jit(solution)/shard_map/ppermute | solution.py:30
  72.8 5.3 %collective-permute-start.19 = (bf16[5120,128]{1,0:T(8,128)(2,1)}, bf16[5120,128]{1,0:T(8,128)(2,1)}, u32[]{:S(2)}, u32[]{:S(2)}) collective-permute-start(bf16[5120,128]{1,0:T(8,128)(2,1)} %bitcast.7.refs_9_), channel_id=1, source_target_pairs={{0,8},{4,12},{24,16},{28,20},{32,40},{36,44},{56,48},{60,52},{64,7... | collective-permute-start | bytes 3932168 | tf_op jit(solution)/shard_map/ppermute | solution.py:30
  78.1 20.3 %collective-permute-done.6 = bf16[1280,512]{1,0:T(8,128)(2,1)} collective-permute-done((bf16[1280,512]{1,0:T(8,128)(2,1)S(1)}, bf16[1280,512]{1,0:T(8,128)(2,1)}, u32[]{:S(2)}, u32[]{:S(2)}) %collective-permute-start.6) | collective-permute-done | bytes 1310752 | tf_op jit(solution)/shard_map/ppermute | solution.py:30
  98.5 1.6 collective-permute-start.22
  100.0 1.7 collective-permute-done.7
  101.7 1.5 collective-permute-start.16
  103.2 3.6 %collective-permute-start.15 = (bf16[160,5120]{1,0:T(8,128)(2,1)}, bf16[160,5120]{1,0:T(8,128)(2,1)}, u32[]{:S(2)}, u32[]{:S(2)}) collective-permute-start(bf16[160,5120]{1,0:T(8,128)(2,1)} %collective-permute-done.14.refs_4_), channel_id=1, source_target_pairs={{0,4},{4,0},{8,12},{12,8},{16,20},{20,16},{24,28},{28,24},{32,36},... | collective-permute-start | bytes 4915208 | tf_op jit(solution)/shard_map/ppermute | solution.py:30
  107.0 2.0 slice.16
  108.9 2.0 slice.17
  110.9 1.6 collective-permute-start.8
  112.7 1.7 fusion
  115.2 2.5 %constant_dynamic-update-slice_fusion.3 = bf16[5120,512]{1,0:T(8,128)(2,1)} fusion(bf16[5120,512]{1,0:T(8,128)(2,1)} %get-tuple-element.22, bf16[1280,512]{1,0:T(8,128)(2,1)} %collective-permute-done.6), kind=kLoop, calls=%fused_computation.33 | loop fusion | bytes 2621440
  117.7 9.9 %collective-permute-done.8 = bf16[640,512]{1,0:T(8,128)(2,1)} collective-permute-done((bf16[640,512]{1,0:T(8,128)(2,1)}, bf16[640,512]{1,0:T(8,128)(2,1)}, u32[]{:S(2)}, u32[]{:S(2)}) %collective-permute-start.8) | collective-permute-done | bytes 655392 | tf_op jit(solution)/shard_map/ppermute | solution.py:30
  127.6 0.8 collective-permute-start.21
  128.4 1.7 collective-permute-done.9
  130.0 1.1 collective-permute-start.23
  131.1 2.5 %constant_dynamic-update-slice_fusion.2 = bf16[5120,512]{1,0:T(8,128)(2,1)} fusion(bf16[5120,512]{1,0:T(8,128)(2,1)} %constant_dynamic-update-slice_fusion.3, bf16[1280,512]{1,0:T(8,128)(2,1)} %collective-permute-done.7), kind=kLoop, calls=%fused_computation.32 | loop fusion | bytes 2621440
  133.6 2.0 constant_dynamic-update-slice_fusion.1
  135.6 2.0 constant_dynamic-update-slice_fusion
  137.6 8.1 %input_step.2 = bf16[160,5120]{1,0:T(8,128)(2,1)} custom-call(s32[8]{0:T(128)S(1)} %add.137.place, bf16[160,512]{1,0:T(8,128)(2,1)S(1)} %get-tuple-element.31.cot, bf16[8,640,512]{2,1,0:T(8,128)(2,1)} %bitcast.22), custom_call_target="tpu_custom_call" | custom-call | flops 838860800 | bytes 8519680 | tf_op jit(solution)/shard_map/input_step/pallas_call | solution.py:201
  145.6 1.0 fusion.7
  146.7 1.5 concatenate.60
  148.2 1.1 copy-done.2
  149.4 6.3 %momentum_step.2 = (bf16[2560,128]{1,0:T(8,128)(2,1)S(1)}, bf16[2560,128]{1,0:T(8,128)(2,1)S(1)}, s32[80,128]{1,0:T(8,128)S(1)}, s32[80,128]{1,0:T(8,128)S(1)}) custom-call(bf16[160,5120]{1,0:T(8,128)(2,1)} %copy-done.9, bf16[160,5120]{1,0:T(8,128)(2,1)} %collective-permute-done.11.refs_1_, bf16[160,2560]{1,0:T(8,128)(2,1)} %collective-permute-done.12.refs_2_, ...), custom_call_target="tpu_custom_call" | custom-call | flops 1677721600 | bytes 9175040 | tf_op jit(solution)/shard_map/momentum_step/pallas_call | solution.py:107
  155.8 6.8 %momentum_step.3 = (bf16[2560,128]{1,0:T(8,128)(2,1)S(1)}, bf16[2560,128]{1,0:T(8,128)(2,1)S(1)}, s32[80,128]{1,0:T(8,128)S(1)}, s32[80,128]{1,0:T(8,128)S(1)}) custom-call(bf16[160,5120]{1,0:T(8,128)(2,1)} %copy-done.9, bf16[160,5120]{1,0:T(8,128)(2,1)} %collective-permute-done.11.refs_1_, bf16[160,2560]{1,0:T(8,128)(2,1)S(1)} %collective-permute-done.20.refs_2_, ...), custom_call_target="tpu_custom_call" | custom-call | flops 1677721600 | bytes 9175040 | tf_op jit(solution)/shard_map/momentum_step/pallas_call | solution.py:107
  162.6 0.8 copy-done.5
  163.4 0.8 copy-done.8
  164.3 0.7 collective-permute-start.26
  165.0 1.3 collective-permute-start.28
  166.3 1.3 collective-permute-start.27
  168.1 20.1 %collective-permute-done.28 = s32[160,128]{1,0:T(8,128)S(1)} collective-permute-done((s32[160,128]{1,0:T(8,128)S(1)}, s32[160,128]{1,0:T(8,128)S(1)}, u32[]{:S(2)}, u32[]{:S(2)}) %collective-permute-start.28) | collective-permute-done | bytes 81952 | tf_op jit(solution)/shard_map/ppermute | solution.py:30
  188.2 3.2 %collective-permute-done.27 = s32[160,128]{1,0:T(8,128)S(1)} collective-permute-done((s32[160,128]{1,0:T(8,128)S(1)}, s32[160,128]{1,0:T(8,128)S(1)}, u32[]{:S(2)}, u32[]{:S(2)}) %collective-permute-start.27) | collective-permute-done | bytes 81952 | tf_op jit(solution)/shard_map/ppermute | solution.py:30
  191.5 2.6 %collective-permute-start.31 = (s32[2,160,128]{2,1,0:T(8,128)S(1)}, s32[2,160,128]{2,1,0:T(8,128)S(1)}, u32[]{:S(2)}, u32[]{:S(2)}) collective-permute-start(s32[2,160,128]{2,1,0:T(8,128)S(1)} %add_select_fusion), channel_id=1, source_target_pairs={{0,64},{4,68},{8,72},{12,76},{16,80},{20,84},{24,88},{28,92},{32,9... | collective-permute-start | bytes 491528 | tf_op jit(solution)/shard_map/ppermute | solution.py:30
  194.1 1.3 collective-permute-start.25
  195.4 1.3 collective-permute-start.24
  196.7 1.1 collective-permute-done.31
  197.7 1.4 collective-permute-start.30
  199.2 4.8 %collective-permute-done.30 = s32[2,160,128]{2,1,0:T(8,128)S(1)} collective-permute-done((s32[2,160,128]{2,1,0:T(8,128)S(1)}, s32[2,160,128]{2,1,0:T(8,128)S(1)}, u32[]{:S(2)}, u32[]{:S(2)}) %collective-permute-start.30) | collective-permute-done | bytes 163872 | tf_op jit(solution)/shard_map/ppermute | solution.py:30
  203.9 1.9 collective-permute-start.29
  205.9 2.6 %collective-permute-done.29 = s32[2,160,128]{2,1,0:T(8,128)} collective-permute-done((s32[2,160,128]{2,1,0:T(8,128)S(1)}, s32[2,160,128]{2,1,0:T(8,128)}, u32[]{:S(2)}, u32[]{:S(2)}) %collective-permute-start.29) | collective-permute-done | bytes 163872 | tf_op jit(solution)/shard_map/ppermute | solution.py:30
  208.5 1.0 pad_add_fusion.words_own
  209.5 3.8 %collective-permute-start.32 = (s32[8,160,128]{2,1,0:T(8,128)S(1)}, s32[8,160,128]{2,1,0:T(8,128)S(1)}, u32[]{:S(2)}, u32[]{:S(2)}) collective-permute-start(s32[8,160,128]{2,1,0:T(8,128)S(1)} %pad_add_fusion.words_own), channel_id=1, source_target_pairs={{0,4},{4,0},{8,12},{12,8},{16,20},{20,16},{24,28},{28,24},{32,36},... | collective-permute-start | bytes 1966088 | tf_op jit(solution)/shard_map/ppermute | solution.py:30
  213.3 8.3 %input_step.3 = bf16[160,5120]{1,0:T(8,128)(2,1)} custom-call(s32[8]{0:T(128)S(1)} %add.137.place, bf16[160,512]{1,0:T(8,128)(2,1)S(1)} %get-tuple-element.32.cot, bf16[8,640,512]{2,1,0:T(8,128)(2,1)} %bitcast.23, bf16[160,5120]{1,0:T(8,128)(2,1)} %collective-permute-done.10.other, f32[160,1]{1,0:T(8,128)S(1)} %copy.10.mask), custom_call_target="tpu_custom_call" | custom-call | flops 838860800 | bytes 8519680 | tf_op jit(solution)/shard_map/input_step/pallas_call | solution.py:201
  221.5 3.7 %collective-permute-done.24 = bf16[2560,128]{1,0:T(8,128)(2,1)} collective-permute-done((bf16[2560,128]{1,0:T(8,128)(2,1)}, bf16[2560,128]{1,0:T(8,128)(2,1)}, u32[]{:S(2)}, u32[]{:S(2)}) %collective-permute-start.24) | collective-permute-done | bytes 655392 | tf_op jit(solution)/shard_map/ppermute | solution.py:30
  225.3 2.7 %maximum_select_fusion = bf16[1,5120,128]{2,1,0:T(8,128)(2,1)} fusion(bf16[1,2560,128]{2,1,0:T(8,128)(2,1)S(1)} %bitcast.21, bf16[1,2560,128]{2,1,0:T(8,128)(2,1)S(1)} %bitcast.20, bf16[1,2560,128]{2,1,0:T(8,128)(2,1)} %bitcast.11, bf16[1,2560,128]{2,1,0:T(8,128)(2,1)} %bitcast.10, pred[]{:T(512)S(6)} %or.3), kind=kLoop, calls=%fused_computation.2 | loop fusion | flops 5898240 | bytes 3932161 | tf_op jit(solution)/shard_map/jit(_where)/select_n | solution.py:297
  228.0 4.9 %vote_step.1 = bf16[5120,256]{1,0:T(8,128)(2,1)} custom-call(s32[1]{0:T(128)} %bitcast.12.core, s32[8,160,128]{2,1,0:T(8,128)S(1)} %pad_add_fusion.words_own, s32[8,160,128]{2,1,0:T(8,128)S(1)} %collective-permute-done.32.words_other, bf16[5120,128]{1,0:T(8,128)(2,1)S(1)} %copy-done, bf16[5120,128]{1,0:T(8,128)(2,1)S(1)} %collective-permute-done.33.w_other), custom_call_target="tpu_custom_call" | custom-call | flops 10485760 | bytes 6553600 | tf_op jit(solution)/shard_map/vote_step/pallas_call | solution.py:161
  (75 shorter events, 3.7 us)
Async XLA Ops:
  2.4 14.9 %collective-permute-start.2 = (bf16[320,128]{1,0:T(8,128)(2,1)}, bf16[320,128]{1,0:T(8,128)(2,1)S(1)}, u32[]{:S(2)}, u32[]{:S(2)}) collective-permute-start(bf16[320,128]{1,0:T(8,128)(2,1)} %get-tuple-element.36), channel_id=1, source_target_pairs={{0,16},{4,20},{8,24},{12,28},{16,0},{20,4},{24,8},{28,12},{32,48},... | collective-permute-start | bytes 245768 | tf_op jit(solution)/shard_map/ppermute | solution.py:30
  6.3 13.2 %collective-permute-start.1 = (bf16[320,128]{1,0:T(8,128)(2,1)}, bf16[320,128]{1,0:T(8,128)(2,1)S(1)}, u32[]{:S(2)}, u32[]{:S(2)}) collective-permute-start(bf16[320,128]{1,0:T(8,128)(2,1)} %get-tuple-element.34), channel_id=1, source_target_pairs={{0,8},{4,12},{8,16},{12,20},{16,24},{20,28},{24,0},{28,4},{32,40},... | collective-permute-start | bytes 245768 | tf_op jit(solution)/shard_map/ppermute | solution.py:30
  7.9 12.2 %collective-permute-start = (bf16[320,128]{1,0:T(8,128)(2,1)S(1)}, bf16[320,128]{1,0:T(8,128)(2,1)S(1)}, u32[]{:S(2)}, u32[]{:S(2)}) collective-permute-start(bf16[320,128]{1,0:T(8,128)(2,1)S(1)} %get-tuple-element.35), channel_id=1, source_target_pairs={{0,24},{4,28},{8,0},{12,4},{16,8},{20,12},{24,16},{28,20},{32,56},... | collective-permute-start | bytes 245768 | tf_op jit(solution)/shard_map/ppermute | solution.py:30
  11.8 1.7 copy-start.9
  11.8 3.5 %copy-start = (bf16[5120,128]{1,0:T(8,128)(2,1)S(1)}, bf16[5120,128]{1,0:T(8,128)(2,1)}, u32[]{:S(2)}) copy-start(bf16[5120,128]{1,0:T(8,128)(2,1)} %w_own.1) | copy-start | bytes 3932164
  11.8 12.6 %copy-start.10 = (bf16[1280,128]{1,0:T(8,128)(2,1)S(1)}, bf16[1280,128]{1,0:T(8,128)(2,1)}, u32[]{:S(2)}) copy-start(bf16[1280,128]{1,0:T(8,128)(2,1)} %param.6) | copy-start | bytes 983044
  13.5 59.3 %collective-permute-start.20 = (bf16[160,2560]{1,0:T(8,128)(2,1)}, bf16[160,2560]{1,0:T(8,128)(2,1)S(1)}, u32[]{:S(2)}, u32[]{:S(2)}) collective-permute-start(bf16[160,2560]{1,0:T(8,128)(2,1)} %get-tuple-element.20), channel_id=1, source_target_pairs={{0,8},{4,12},{24,16},{28,20},{32,40},{36,44},{56,48},{60,52},{64,7... | collective-permute-start | bytes 2457608 | tf_op jit(solution)/shard_map/ppermute | solution.py:30
  15.4 14.4 %collective-permute-start.5 = (bf16[1280,128]{1,0:T(8,128)(2,1)S(1)}, bf16[1280,128]{1,0:T(8,128)(2,1)S(1)}, u32[]{:S(2)}, u32[]{:S(2)}) collective-permute-start(bf16[1280,128]{1,0:T(8,128)(2,1)S(1)} %constant_dynamic-slice_fusion.1), channel_id=1, source_target_pairs={{0,144},{4,148},{8,152},{12,156},{16,128},{20,132},{24,136},{28,14... | collective-permute-start | bytes 983048 | tf_op jit(solution)/shard_map/ppermute | solution.py:30
  17.4 2.7 %copy-start.11 = (bf16[320,128]{1,0:T(8,128)(2,1)}, bf16[320,128]{1,0:T(8,128)(2,1)S(1)}, u32[]{:S(2)}) copy-start(bf16[320,128]{1,0:T(8,128)(2,1)S(1)} %collective-permute-done.2) | copy-start | bytes 245764
  17.4 28.1 %collective-permute-start.4 = (bf16[1280,128]{1,0:T(8,128)(2,1)S(1)}, bf16[1280,128]{1,0:T(8,128)(2,1)}, u32[]{:S(2)}, u32[]{:S(2)}) collective-permute-start(bf16[1280,128]{1,0:T(8,128)(2,1)S(1)} %constant_dynamic-slice_fusion.1), channel_id=1, source_target_pairs={{0,8},{4,12},{8,16},{12,20},{16,24},{20,28},{24,128},{28,132},{32,... | collective-permute-start | bytes 983048 | tf_op jit(solution)/shard_map/ppermute | solution.py:30
  19.5 0.6 copy-start.13
  19.5 27.9 %collective-permute-start.3 = (bf16[1280,128]{1,0:T(8,128)(2,1)S(1)}, bf16[1280,128]{1,0:T(8,128)(2,1)}, u32[]{:S(2)}, u32[]{:S(2)}) collective-permute-start(bf16[1280,128]{1,0:T(8,128)(2,1)S(1)} %constant_dynamic-slice_fusion.1), channel_id=1, source_target_pairs={{0,152},{4,156},{8,0},{12,4},{16,8},{20,12},{24,16},{28,20},{32,18... | collective-permute-start | bytes 983048 | tf_op jit(solution)/shard_map/ppermute | solution.py:30
  20.1 0.7 copy-start.15
  20.7 52.1 %collective-permute-start.12 = (bf16[160,2560]{1,0:T(8,128)(2,1)}, bf16[160,2560]{1,0:T(8,128)(2,1)}, u32[]{:S(2)}, u32[]{:S(2)}) collective-permute-start(bf16[160,2560]{1,0:T(8,128)(2,1)} %get-tuple-element.19), channel_id=1, source_target_pairs={{0,8},{4,12},{24,16},{28,20},{32,40},{36,44},{56,48},{60,52},{64,7... | collective-permute-start | bytes 2457608 | tf_op jit(solution)/shard_map/ppermute | solution.py:30
  29.8 82.7 %collective-permute-start.11 = (bf16[160,5120]{1,0:T(8,128)(2,1)}, bf16[160,5120]{1,0:T(8,128)(2,1)}, u32[]{:S(2)}, u32[]{:S(2)}) collective-permute-start(bf16[160,5120]{1,0:T(8,128)(2,1)} %copy-done.9), channel_id=1, source_target_pairs={{0,4},{4,0},{8,12},{12,8},{16,20},{20,16},{24,28},{28,24},{32,36},... | collective-permute-start | bytes 4915208 | tf_op jit(solution)/shard_map/ppermute | solution.py:30
  45.5 57.7 %collective-permute-start.14 = (bf16[160,5120]{1,0:T(8,128)(2,1)}, bf16[160,5120]{1,0:T(8,128)(2,1)}, u32[]{:S(2)}, u32[]{:S(2)}) collective-permute-start(bf16[160,5120]{1,0:T(8,128)(2,1)} %copy-done.9), channel_id=1, source_target_pairs={{8,16},{12,20},{16,8},{20,12},{40,48},{44,52},{48,40},{52,44},{72,... | collective-permute-start | bytes 4915208 | tf_op jit(solution)/shard_map/ppermute | solution.py:30
  47.4 22.7 %collective-permute-start.18 = (bf16[1280,128]{0,1:T(8,128)(2,1)S(1)}, bf16[1280,128]{0,1:T(8,128)(2,1)S(1)}, u32[]{:S(2)}, u32[]{:S(2)}) collective-permute-start(bf16[1280,128]{0,1:T(8,128)(2,1)S(1)} %copy.12), channel_id=1, source_target_pairs={{0,8},{4,12},{24,16},{28,20},{32,40},{36,44},{56,48},{60,52},{64,7... | collective-permute-start | bytes 983048 | tf_op jit(solution)/shard_map/ppermute | solution.py:30
  54.0 58.6 %copy-start.12 = (bf16[320,128]{1,0:T(8,128)(2,1)S(1)}, bf16[320,128]{1,0:T(8,128)(2,1)}, u32[]{:S(2)}) copy-start(bf16[320,128]{1,0:T(8,128)(2,1)} %copy-done.11) | copy-start | bytes 245764
  54.0 58.6 %copy-start.14 = (bf16[320,128]{1,0:T(8,128)(2,1)S(1)}, bf16[320,128]{1,0:T(8,128)(2,1)}, u32[]{:S(2)}) copy-start(bf16[320,128]{1,0:T(8,128)(2,1)} %copy-done.13) | copy-start | bytes 245764
  54.0 58.6 %copy-start.16 = (bf16[320,128]{1,0:T(8,128)(2,1)S(1)}, bf16[320,128]{1,0:T(8,128)(2,1)}, u32[]{:S(2)}) copy-start(bf16[320,128]{1,0:T(8,128)(2,1)} %copy-done.15) | copy-start | bytes 245764
  70.1 28.4 %collective-permute-start.6 = (bf16[1280,512]{1,0:T(8,128)(2,1)S(1)}, bf16[1280,512]{1,0:T(8,128)(2,1)}, u32[]{:S(2)}, u32[]{:S(2)}) collective-permute-start(bf16[1280,512]{1,0:T(8,128)(2,1)S(1)} %get-tuple-element.21), channel_id=1, source_target_pairs={{0,96},{4,100},{8,104},{12,108},{16,112},{20,116},{24,120},{28,124... | collective-permute-start | bytes 3932168 | tf_op jit(solution)/shard_map/ppermute | solution.py:30
  72.8 28.9 %collective-permute-start.7 = (bf16[1280,512]{1,0:T(8,128)(2,1)S(1)}, bf16[1280,512]{1,0:T(8,128)(2,1)}, u32[]{:S(2)}, u32[]{:S(2)}) collective-permute-start(bf16[1280,512]{1,0:T(8,128)(2,1)S(1)} %get-tuple-element.21), channel_id=1, source_target_pairs={{0,32},{4,36},{8,40},{12,44},{16,48},{20,52},{24,56},{28,60},{32,6... | collective-permute-start | bytes 3932168 | tf_op jit(solution)/shard_map/ppermute | solution.py:30
  72.8 38.1 %collective-permute-start.19 = (bf16[5120,128]{1,0:T(8,128)(2,1)}, bf16[5120,128]{1,0:T(8,128)(2,1)}, u32[]{:S(2)}, u32[]{:S(2)}) collective-permute-start(bf16[5120,128]{1,0:T(8,128)(2,1)} %bitcast.7.refs_9_), channel_id=1, source_target_pairs={{0,8},{4,12},{24,16},{28,20},{32,40},{36,44},{56,48},{60,52},{64,7... | collective-permute-start | bytes 3932168 | tf_op jit(solution)/shard_map/ppermute | solution.py:30
  98.5 16.0 %collective-permute-start.22 = (bf16[160,2560]{1,0:T(8,128)(2,1)S(1)}, bf16[160,2560]{1,0:T(8,128)(2,1)}, u32[]{:S(2)}, u32[]{:S(2)}) collective-permute-start(bf16[160,2560]{1,0:T(8,128)(2,1)S(1)} %collective-permute-done.20.refs_2_), channel_id=1, source_target_pairs={{8,16},{12,20},{16,8},{20,12},{40,48},{44,52},{48,40},{52,44},{72,... | collective-permute-start | bytes 2457608 | tf_op jit(solution)/shard_map/ppermute | solution.py:30
  101.7 13.2 %collective-permute-start.16 = (bf16[160,2560]{1,0:T(8,128)(2,1)}, bf16[160,2560]{1,0:T(8,128)(2,1)}, u32[]{:S(2)}, u32[]{:S(2)}) collective-permute-start(bf16[160,2560]{1,0:T(8,128)(2,1)} %collective-permute-done.12.refs_2_), channel_id=1, source_target_pairs={{8,16},{12,20},{16,8},{20,12},{40,48},{44,52},{48,40},{52,44},{72,... | collective-permute-start | bytes 2457608 | tf_op jit(solution)/shard_map/ppermute | solution.py:30
  103.2 45.0 %collective-permute-start.15 = (bf16[160,5120]{1,0:T(8,128)(2,1)}, bf16[160,5120]{1,0:T(8,128)(2,1)}, u32[]{:S(2)}, u32[]{:S(2)}) collective-permute-start(bf16[160,5120]{1,0:T(8,128)(2,1)} %collective-permute-done.14.refs_4_), channel_id=1, source_target_pairs={{0,4},{4,0},{8,12},{12,8},{16,20},{20,16},{24,28},{28,24},{32,36},... | collective-permute-start | bytes 4915208 | tf_op jit(solution)/shard_map/ppermute | solution.py:30
  110.9 16.7 %collective-permute-start.8 = (bf16[640,512]{1,0:T(8,128)(2,1)}, bf16[640,512]{1,0:T(8,128)(2,1)}, u32[]{:S(2)}, u32[]{:S(2)}) collective-permute-start(bf16[640,512]{1,0:T(8,128)(2,1)} %slice.16), channel_id=1, source_target_pairs={{0,96},{4,100},{8,104},{12,108},{16,112},{20,116},{24,120},{28,124... | collective-permute-start | bytes 1966088 | tf_op jit(solution)/shard_map/ppermute | solution.py:30
  112.5 17.6 %collective-permute-start.9 = (bf16[640,512]{1,0:T(8,128)(2,1)}, bf16[640,512]{1,0:T(8,128)(2,1)}, u32[]{:S(2)}, u32[]{:S(2)}) collective-permute-start(bf16[640,512]{1,0:T(8,128)(2,1)} %slice.17), channel_id=1, source_target_pairs={{0,32},{4,36},{8,40},{12,44},{16,48},{20,52},{24,56},{28,60},{32,6... | collective-permute-start | bytes 1966088 | tf_op jit(solution)/shard_map/ppermute | solution.py:30
  114.5 31.2 %collective-permute-start.13 = (bf16[160,2560]{1,0:T(8,128)(2,1)}, bf16[160,2560]{1,0:T(8,128)(2,1)S(1)}, u32[]{:S(2)}, u32[]{:S(2)}) collective-permute-start(bf16[160,2560]{1,0:T(8,128)(2,1)} %collective-permute-done.12.refs_2_), channel_id=1, source_target_pairs={{0,4},{4,0},{8,12},{12,8},{16,20},{20,16},{24,28},{28,24},{32,36},... | collective-permute-start | bytes 2457608 | tf_op jit(solution)/shard_map/ppermute | solution.py:30
  114.9 33.3 %collective-permute-start.17 = (bf16[160,2560]{1,0:T(8,128)(2,1)}, bf16[160,2560]{1,0:T(8,128)(2,1)}, u32[]{:S(2)}, u32[]{:S(2)}) collective-permute-start(bf16[160,2560]{1,0:T(8,128)(2,1)} %collective-permute-done.16.refs_6_), channel_id=1, source_target_pairs={{0,4},{4,0},{8,12},{12,8},{16,20},{20,16},{24,28},{28,24},{32,36},... | collective-permute-start | bytes 2457608 | tf_op jit(solution)/shard_map/ppermute | solution.py:30
  127.6 28.2 %collective-permute-start.21 = (bf16[160,2560]{1,0:T(8,128)(2,1)S(1)}, bf16[160,2560]{1,0:T(8,128)(2,1)}, u32[]{:S(2)}, u32[]{:S(2)}) collective-permute-start(bf16[160,2560]{1,0:T(8,128)(2,1)S(1)} %collective-permute-done.20.refs_2_), channel_id=1, source_target_pairs={{0,4},{4,0},{8,12},{12,8},{16,20},{20,16},{24,28},{28,24},{32,36},... | collective-permute-start | bytes 2457608 | tf_op jit(solution)/shard_map/ppermute | solution.py:30
  130.0 25.7 %collective-permute-start.23 = (bf16[160,2560]{1,0:T(8,128)(2,1)}, bf16[160,2560]{1,0:T(8,128)(2,1)}, u32[]{:S(2)}, u32[]{:S(2)}) collective-permute-start(bf16[160,2560]{1,0:T(8,128)(2,1)} %collective-permute-done.22.refs_6_), channel_id=1, source_target_pairs={{0,4},{4,0},{8,12},{12,8},{16,20},{20,16},{24,28},{28,24},{32,36},... | collective-permute-start | bytes 2457608 | tf_op jit(solution)/shard_map/ppermute | solution.py:30
  145.6 1.0 copy-start.1
  145.6 67.6 %collective-permute-start.10 = (bf16[160,5120]{1,0:T(8,128)(2,1)}, bf16[160,5120]{1,0:T(8,128)(2,1)}, u32[]{:S(2)}, u32[]{:S(2)}) collective-permute-start(bf16[160,5120]{1,0:T(8,128)(2,1)} %input_step.2), channel_id=1, source_target_pairs={{0,4},{4,0},{8,12},{12,8},{16,20},{20,16},{24,28},{28,24},{32,36},... | collective-permute-start | bytes 4915208 | tf_op jit(solution)/shard_map/ppermute | solution.py:30
  148.2 1.1 copy-start.2
  155.7 6.9 %copy-start.3 = (bf16[2560,128]{1,0:T(8,128)(2,1)}, bf16[2560,128]{1,0:T(8,128)(2,1)S(1)}, u32[]{:S(2)}) copy-start(bf16[2560,128]{1,0:T(8,128)(2,1)S(1)} %get-tuple-element.11) | copy-start | bytes 1966084
  155.7 6.9 %copy-start.7 = (bf16[2560,128]{1,0:T(8,128)(2,1)}, bf16[2560,128]{1,0:T(8,128)(2,1)S(1)}, u32[]{:S(2)}) copy-start(bf16[2560,128]{1,0:T(8,128)(2,1)S(1)} %get-tuple-element.13) | copy-start | bytes 1966084
  155.8 50.1 %copy-start.17 = (s32[160]{0:T(256)S(1)}, s32[160]{0:T(256)}, u32[]{:S(2)}) copy-start(s32[160]{0:T(256)} %param.7) | copy-start | bytes 1924
  162.6 0.8 copy-start.5
  163.4 0.8 copy-start.8
  164.3 3.9 %collective-permute-start.26 = (s32[160,128]{1,0:T(8,128)S(1)}, s32[160,128]{1,0:T(8,128)S(1)}, u32[]{:S(2)}, u32[]{:S(2)}) collective-permute-start(s32[160,128]{1,0:T(8,128)S(1)} %constant_dynamic-update-slice_fusion.5), channel_id=1, source_target_pairs={{8,136},{12,140},{16,144},{20,148},{40,168},{44,172},{48,176},{52,... | collective-permute-start | bytes 245768 | tf_op jit(solution)/shard_map/ppermute | solution.py:30
  165.0 23.3 %collective-permute-start.28 = (s32[160,128]{1,0:T(8,128)S(1)}, s32[160,128]{1,0:T(8,128)S(1)}, u32[]{:S(2)}, u32[]{:S(2)}) collective-permute-start(s32[160,128]{1,0:T(8,128)S(1)} %constant_dynamic-update-slice_fusion.7), channel_id=1, source_target_pairs={{8,128},{12,132},{16,152},{20,156},{40,160},{44,164},{48,184},{52,... | collective-permute-start | bytes 245768 | tf_op jit(solution)/shard_map/ppermute | solution.py:30
  166.3 25.2 %collective-permute-start.27 = (s32[160,128]{1,0:T(8,128)S(1)}, s32[160,128]{1,0:T(8,128)S(1)}, u32[]{:S(2)}, u32[]{:S(2)}) collective-permute-start(s32[160,128]{1,0:T(8,128)S(1)} %constant_dynamic-update-slice_fusion.7), channel_id=1, source_target_pairs={{8,0},{12,4},{16,24},{20,28},{40,32},{44,36},{48,56},{52,60},{72,6... | collective-permute-start | bytes 245768 | tf_op jit(solution)/shard_map/ppermute | solution.py:30
  167.6 60.4 %collective-permute-start.33 = (bf16[5120,128]{1,0:T(8,128)(2,1)S(1)}, bf16[5120,128]{1,0:T(8,128)(2,1)S(1)}, u32[]{:S(2)}, u32[]{:S(2)}) collective-permute-start(bf16[5120,128]{1,0:T(8,128)(2,1)S(1)} %copy-done), channel_id=1, source_target_pairs={{0,4},{4,0},{8,12},{12,8},{16,20},{20,16},{24,28},{28,24},{32,36},... | collective-permute-start | bytes 3932168 | tf_op jit(solution)/shard_map/ppermute | solution.py:30
  191.5 6.3 %collective-permute-start.31 = (s32[2,160,128]{2,1,0:T(8,128)S(1)}, s32[2,160,128]{2,1,0:T(8,128)S(1)}, u32[]{:S(2)}, u32[]{:S(2)}) collective-permute-start(s32[2,160,128]{2,1,0:T(8,128)S(1)} %add_select_fusion), channel_id=1, source_target_pairs={{0,64},{4,68},{8,72},{12,76},{16,80},{20,84},{24,88},{28,92},{32,9... | collective-permute-start | bytes 491528 | tf_op jit(solution)/shard_map/ppermute | solution.py:30
  194.1 27.5 %collective-permute-start.25 = (bf16[2560,128]{1,0:T(8,128)(2,1)}, bf16[2560,128]{1,0:T(8,128)(2,1)}, u32[]{:S(2)}, u32[]{:S(2)}) collective-permute-start(bf16[2560,128]{1,0:T(8,128)(2,1)} %copy-done.8), channel_id=1, source_target_pairs={{8,0},{12,4},{16,24},{20,28},{40,32},{44,36},{48,56},{52,60},{72,6... | collective-permute-start | bytes 1966088 | tf_op jit(solution)/shard_map/ppermute | solution.py:30
  195.4 29.9 %collective-permute-start.24 = (bf16[2560,128]{1,0:T(8,128)(2,1)}, bf16[2560,128]{1,0:T(8,128)(2,1)}, u32[]{:S(2)}, u32[]{:S(2)}) collective-permute-start(bf16[2560,128]{1,0:T(8,128)(2,1)} %copy-done.7), channel_id=1, source_target_pairs={{8,0},{12,4},{16,24},{20,28},{40,32},{44,36},{48,56},{52,60},{72,6... | collective-permute-start | bytes 1966088 | tf_op jit(solution)/shard_map/ppermute | solution.py:30
  197.7 6.2 %collective-permute-start.30 = (s32[2,160,128]{2,1,0:T(8,128)S(1)}, s32[2,160,128]{2,1,0:T(8,128)S(1)}, u32[]{:S(2)}, u32[]{:S(2)}) collective-permute-start(s32[2,160,128]{2,1,0:T(8,128)S(1)} %add_select_fusion), channel_id=1, source_target_pairs={{0,32},{4,36},{8,40},{12,44},{16,48},{20,52},{24,56},{28,60},{32,6... | collective-permute-start | bytes 491528 | tf_op jit(solution)/shard_map/ppermute | solution.py:30
  203.9 4.6 %collective-permute-start.29 = (s32[2,160,128]{2,1,0:T(8,128)S(1)}, s32[2,160,128]{2,1,0:T(8,128)}, u32[]{:S(2)}, u32[]{:S(2)}) collective-permute-start(s32[2,160,128]{2,1,0:T(8,128)S(1)} %add_select_fusion), channel_id=1, source_target_pairs={{0,96},{4,100},{8,104},{12,108},{16,112},{20,116},{24,120},{28,124... | collective-permute-start | bytes 491528 | tf_op jit(solution)/shard_map/ppermute | solution.py:30
  209.5 18.5 %collective-permute-start.32 = (s32[8,160,128]{2,1,0:T(8,128)S(1)}, s32[8,160,128]{2,1,0:T(8,128)S(1)}, u32[]{:S(2)}, u32[]{:S(2)}) collective-permute-start(s32[8,160,128]{2,1,0:T(8,128)S(1)} %pad_add_fusion.words_own), channel_id=1, source_target_pairs={{0,4},{4,0},{8,12},{12,8},{16,20},{20,16},{24,28},{28,24},{32,36},... | collective-permute-start | bytes 1966088 | tf_op jit(solution)/shard_map/ppermute | solution.py:30
  213.2 12.0 %copy-start.4 = (bf16[2560,128]{1,0:T(8,128)(2,1)S(1)}, bf16[2560,128]{1,0:T(8,128)(2,1)}, u32[]{:S(2)}) copy-start(bf16[2560,128]{1,0:T(8,128)(2,1)} %copy-done.3) | copy-start | bytes 1966084
  213.3 12.0 %copy-start.6 = (bf16[2560,128]{1,0:T(8,128)(2,1)S(1)}, bf16[2560,128]{1,0:T(8,128)(2,1)}, u32[]{:S(2)}) copy-start(bf16[2560,128]{1,0:T(8,128)(2,1)} %copy-done.5) | copy-start | bytes 1966084

commit v2 on v1

v2 whole, which is shorter than its diff:
```python
import jax
import jax.numpy as jnp
from jax import lax
from jax.experimental import pallas as pl
from jax.experimental.pallas import tpu as pltpu
from jax.sharding import PartitionSpec as P

beta_slow = 0.99
beta_vote = 0.9
step_rate = 0.02

AXES = ("dp", "tensor")
HI, YS, LINE, CORES = 2, 4, 4, 2
WIDTH = 1280
CUT = 2560
VMEM = 48 * 1024 * 1024


def permute(array, place):
    pairs = []
    for hi in range(HI):
        for y in range(YS):
            for c in range(LINE):
                for k in range(CORES):
                    to = place(hi, y, c, k)
                    if to is not None:
                        h2, y2, c2, k2 = to
                        source = ((hi * YS + y) * LINE + c) * CORES + k
                        target = ((h2 % HI * YS + y2 % YS) * LINE + c2) * CORES + k2
                        pairs.append((source, target))
    return lax.ppermute(array, AXES, pairs)


def core_swap(array):
    return permute(array, lambda h, y, c, k: (h, y, c, 1 - k))


def along_y(array, step):
    return permute(array, lambda h, y, c, k: (h, y - step, c, k))


def in_pair(array):
    return permute(array, lambda h, y, c, k: (h, y, c ^ 1, k))


def out_of_pair(array):
    def place(h, y, c, k):
        z = (h * LINE + c + (1 if c % 2 else -1)) % (HI * LINE)
        return z // LINE, y, z % LINE, k

    return permute(array, place)


def along_z(array, step):
    def place(h, y, c, k):
        z = (h * LINE + c - step) % (HI * LINE)
        return z // LINE, y, z % LINE, k

    return permute(array, place)


def inward(array):
    return permute(array, lambda h, y, c, k: (h, y, c ^ 1, k) if c in (0, 3) else None)


def outward(array, flip=0):
    return permute(array, lambda h, y, c, k: (h ^ flip, y, c ^ 1, k) if c in (1, 2) else None)


def across(array):
    return permute(array, lambda h, y, c, k: (h, y, 3 - c, k) if c in (1, 2) else None)


def inner_flip(array):
    return permute(array, lambda h, y, c, k: (h ^ 1, y, c, k) if c in (1, 2) else None)


def params():
    return pltpu.CompilerParams(vmem_limit_bytes=VMEM)


def cot_rows(place, first, count, cot_own, cot_side):
    share = cot_own.shape[0] // (LINE * CORES)
    blocks = [pl.ds(pl.multiple_of(place[first + i] * share, share), share) for i in range(count)]
    return jnp.concatenate(
        [jnp.concatenate([ref[block, :] for block in blocks], 0) for ref in (cot_own, cot_side)], 1
    )


def multiply(tokens, cot):
    rows = jnp.concatenate([ref[...] for ref in tokens], 0)
    return lax.dot_general(rows, cot, (((0,), (0,)), ((), ())), preferred_element_type=jnp.float32)


def gather_kernel(place, *refs):
    tokens, cot_own, cot_side, out = refs[:-3], refs[-3], refs[-2], refs[-1]
    out[...] = multiply(tokens, cot_rows(place, 0, len(tokens), cot_own, cot_side))


def gather_step(place, tokens, cot_own, cot_side, start, size):
    share, rows = tokens[0][0].shape[0], cot_own.shape[0]
    return pl.pallas_call(
        gather_kernel,
        grid_spec=pltpu.PrefetchScalarGridSpec(
            num_scalar_prefetch=1,
            grid=(size // WIDTH,),
            in_specs=[
                pl.BlockSpec((share, WIDTH), lambda i, place, skip=first // WIDTH: (0, i + skip))
                for _, first in tokens
            ]
            + [
                pl.BlockSpec((rows, 128), lambda i, place: (0, 0)),
                pl.BlockSpec((rows, 128), lambda i, place: (cot_side[1], 0)),
            ],
            out_specs=pl.BlockSpec((WIDTH, 256), lambda i, place: (i, 0)),
        ),
        out_shape=jax.ShapeDtypeStruct((size, 256), jnp.float32),
        compiler_params=params(),
        cost_estimate=pl.CostEstimate(
            flops=2 * size * 960 * 256, bytes_accessed=size * 2944, transcendentals=0
        ),
        name="gather_step",
    )(place, *[array for array, _ in tokens], cot_own, cot_side[0])


def momentum_kernel(place, *refs):
    first, second, cot_own, cot_side, early, prior_own, prior_side = refs[:7]
    new_own, new_side, words_own, words_side = refs[-4:]
    grad = early[...] + multiply((first, second), cot_rows(place, 6, 2, cot_own, cot_side))
    for i, (prior, new, words) in enumerate(
        ((prior_own, new_own, words_own), (prior_side, new_side, words_side))
    ):
        part = grad[:, i * 128 : (i + 1) * 128]
        before = prior[...].astype(jnp.float32)
        new[...] = (beta_slow * before + (1.0 - beta_slow) * part).astype(jnp.bfloat16)
        positive = (beta_vote * before + (1.0 - beta_vote) * part > 0).astype(jnp.int32)
        step = WIDTH // 32
        packed = positive[:step]
        for bit in range(1, 32):
            packed = packed | (positive[bit * step : (bit + 1) * step] << bit)
        words[...] = packed


def momentum_step(place, first, second, cot_own, cot_side, early, prior_own, prior_side, start, buffers):
    share, size = first.shape
    rows = cot_own.shape[0]
    features = prior_own.shape[0]
    skip = start // WIDTH
    here = lambda i, place: (i, 0)
    there = lambda i, place: (i + skip, 0)
    token_spec = pl.BlockSpec((share, WIDTH), lambda i, place: (0, i))
    word_spec = pl.BlockSpec((WIDTH // 32, 128), there)
    word_shape = jax.ShapeDtypeStruct((features // 32, 128), jnp.int32)
    return pl.pallas_call(
        momentum_kernel,
        grid_spec=pltpu.PrefetchScalarGridSpec(
            num_scalar_prefetch=1,
            grid=(size // WIDTH,),
            in_specs=[
                token_spec,
                token_spec,
                pl.BlockSpec((rows, 128), lambda i, place: (0, 0)),
                pl.BlockSpec((rows, 128), lambda i, place: (cot_side[1], 0)),
                pl.BlockSpec((WIDTH, 256), here),
                pl.BlockSpec((WIDTH, 128), there),
                pl.BlockSpec((WIDTH, 128), here),
            ]
            + [pl.BlockSpec(memory_space=pl.ANY)] * len(buffers),
            out_specs=[
                pl.BlockSpec((WIDTH, 128), there),
                pl.BlockSpec((WIDTH, 128), here),
                word_spec,
                word_spec,
            ],
        ),
        out_shape=[
            jax.ShapeDtypeStruct((features, 128), jnp.bfloat16),
            jax.ShapeDtypeStruct((size, 128), jnp.bfloat16),
            word_shape,
            word_shape,
        ],
        input_output_aliases={8: 0, 9: 2, 10: 3} if buffers else {},
        compiler_params=params(),
        cost_estimate=pl.CostEstimate(
            flops=2 * size * 320 * 256, bytes_accessed=size * 2688, transcendentals=0
        ),
        name="momentum_step",
    )(place, first, second, cot_own, cot_side[0], early, prior_own, prior_side, *buffers)


def majority(words):
    def half(a, b):
        return a ^ b, a & b

    def full(a, b, c):
        x = a ^ b
        return x ^ c, (a & b) | (x & c)

    s0, c0 = full(words[0], words[1], words[2])
    s1, c1 = full(words[3], words[4], words[5])
    s2, c2 = half(words[6], words[7])
    ones, c3 = full(s0, s1, s2)
    t0, d0 = full(c0, c1, c2)
    twos, d1 = half(t0, c3)
    fours, eights = half(d0, d1)
    more = eights | (fours & (ones | twos))
    fewer = ~(eights | fours)
    return more, fewer


def vote_kernel(core, words_own, words_other, w_own, w_other, out):
    is_low = core[0] == 0
    step = WIDTH // 32
    for block in range(out.shape[0] // WIDTH):
        rows = slice(block * WIDTH, (block + 1) * WIDTH)
        updated = []
        for words, weights in ((words_own, w_own), (words_other, w_other)):
            more, fewer = majority([words[i, block * step : (block + 1) * step] for i in range(8)])
            direction = jnp.concatenate(
                [((more >> bit) & 1) - ((fewer >> bit) & 1) for bit in range(32)], 0
            ).astype(jnp.float32)
            updated.append(
                (weights[rows, :].astype(jnp.float32) - step_rate * direction).astype(jnp.bfloat16)
            )
        out[rows, :128] = jnp.where(is_low, updated[0], updated[1])
        out[rows, 128:] = jnp.where(is_low, updated[1], updated[0])


def vote_step(core, words_own, words_other, w_own, w_other):
    features = w_own.shape[0]
    size = 2 * WIDTH
    word_spec = pl.BlockSpec((8, size // 32, 128), lambda i, core: (0, i, 0))
    weight_spec = pl.BlockSpec((size, 128), lambda i, core: (i, 0))
    return pl.pallas_call(
        vote_kernel,
        grid_spec=pltpu.PrefetchScalarGridSpec(
            num_scalar_prefetch=1,
            grid=(features // size,),
            in_specs=[word_spec, word_spec, weight_spec, weight_spec],
            out_specs=pl.BlockSpec((size, 256), lambda i, core: (i, 0)),
        ),
        out_shape=jax.ShapeDtypeStruct((features, 256), jnp.bfloat16),
        compiler_params=params(),
        cost_estimate=pl.CostEstimate(flops=features * 256 * 8, bytes_accessed=features * 1280, transcendentals=0),
        name="vote_step",
    )(core, words_own, words_other, w_own, w_other)


def input_kernel(cot, w_own, w_rest, ours, theirs):
    weights = jnp.concatenate([w_own[...], w_rest[...]], 1)
    total = lax.dot_general(
        cot[...], weights, (((1,), (1,)), ((), ())), preferred_element_type=jnp.float32
    ).astype(jnp.bfloat16)
    rows = ours.shape[0]
    ours[...] = total[:rows]
    theirs[...] = total[rows:]


def input_step(cot, w_own, w_rest):
    rows, depth = cot.shape
    features = w_own.shape[0]
    width = 2 * WIDTH
    out_spec = pl.BlockSpec((rows // 2, width), lambda i: (0, i))
    return pl.pallas_call(
        input_kernel,
        grid=(features // width,),
        in_specs=[pl.BlockSpec((rows, depth), lambda i: (0, 0))]
        + [pl.BlockSpec((width, w.shape[1]), lambda i: (i, 0)) for w in (w_own, w_rest)],
        out_specs=[out_spec] * 2,
        out_shape=[jax.ShapeDtypeStruct((rows // 2, features), jnp.bfloat16)] * 2,
        compiler_params=params(),
        cost_estimate=pl.CostEstimate(
            flops=2 * rows * depth * features, bytes_accessed=2 * (depth + rows) * features, transcendentals=0
        ),
        name="input_step",
    )(cot, w_own, w_rest)


def after(arrays, *others):
    return lax.optimization_barrier((arrays, *others))[0]


def per_device(tokens_in, key_cot, row_mask, w_key, momentum):
    position = lax.axis_index("tensor")
    chip, core = position // CORES, position % CORES
    y = lax.axis_index("dp") % YS
    inner = (chip == 1) | (chip == 2)
    features = w_key.shape[0]
    share = tokens_in.shape[0]
    quarter = features // YS
    cut = CUT
    prior = momentum[0]
    place = jnp.stack(
        [
            of_chip * CORES + of_core
            for of_chip in (chip, chip ^ 1, chip ^ 3, chip ^ 2)
            for of_core in (core, 1 - core)
        ]
    ).astype(jnp.int32)

    w_part = lax.dynamic_slice(w_key, (y * quarter, 0), (quarter, 128))
    w_rest = [
        in_pair(w_part),
        out_of_pair(w_part),
        along_z(w_part[: quarter // 2], 2),
        along_z(w_part[quarter // 2 :], -2),
    ]
    tokens = jnp.where(row_mask[:, None] != 0, tokens_in, jnp.zeros_like(tokens_in))
    tokens, w_rest = lax.optimization_barrier((tokens, w_rest))
    w_rest = lax.all_gather(
        jnp.concatenate([w_rest[0], w_rest[1], jnp.concatenate(w_rest[2:], 0)], 1),
        "dp",
        axis=0,
        tiled=True,
        axis_index_groups=[[h * YS + y for y in range(YS)] for h in range(HI)],
    )

    near, side, own_swapped = across(tokens), inward(tokens), core_swap(tokens)
    cot_pieces = []
    for step in (0, 1, 3, 2):
        rows = lax.dynamic_slice(key_cot, ((chip ^ step) * CORES * share, 0), (CORES * share, 128))
        if step:
            rows = permute(rows, lambda h, y, c, k, step=step: (h, y, c ^ step, k))
        cot_pieces.append(rows)
    lend = jnp.concatenate([prior[:cut], key_cot], 0)
    near, side, own_swapped, cot_pieces, lend = lax.optimization_barrier(
        (near, side, own_swapped, cot_pieces, lend)
    )

    far = across(side[:, :cut])
    lent = inward(lend)
    near_swapped, side_swapped, w_other = core_swap(near), core_swap(side), core_swap(w_key)
    far, lent, near_swapped, side_swapped, w_other = lax.optimization_barrier(
        (far, lent, near_swapped, side_swapped, w_other)
    )

    far_late = across(side[:, cut:])
    lent_late = inward(prior[cut:])
    cot_side = (lent, cut // key_cot.shape[0])
    arrays = (tokens, own_swapped, side, side_swapped, near, near_swapped)

    def early(start):
        return gather_step(place, [(array, start) for array in arrays], key_cot, cot_side, start, cut)

    new_own, new_side, words, side_words = momentum_step(
        place, far, core_swap(far), key_cot, cot_side, early(0), prior, lent, 0, []
    )
    returned = [outward(new_side)]
    summed, far_late, lent_late, new_own, words, side_words, cot_pieces = lax.optimization_barrier(
        (early(cut), far_late, lent_late, new_own, words, side_words, cot_pieces)
    )

    new_own, new_side, words, side_words = momentum_step(
        place, far_late, core_swap(far_late), key_cot, cot_side, summed, prior, lent_late, cut,
        [new_own, words, side_words],
    )
    words, cot_pieces = lax.optimization_barrier((words, cot_pieces))
    words_flip = inner_flip(words)
    side_here, side_flip = outward(side_words), outward(side_words, 1)
    cot_mine = jnp.concatenate(cot_pieces, 1)
    theirs = lax.dynamic_slice(cot_mine, ((1 - core) * share, 0), (share, 512))
    ours = lax.dynamic_slice(cot_mine, (core * share, 0), (share, 512))
    ours, theirs = input_step(jnp.concatenate([ours, theirs], 0), w_key, w_rest)
    words_flip, side_here, side_flip, returned[0], new_side, ours, theirs = lax.optimization_barrier(
        (words_flip, side_here, side_flip, returned[0], new_side, ours, theirs)
    )

    pair = jnp.where(inner, jnp.stack([words, words_flip]), jnp.stack([side_here, side_flip]))
    votes = jnp.concatenate([pair, along_y(pair, 1), along_y(pair, -1), along_y(pair, 2)], 0)
    returned.append(outward(new_side))
    total = ours.astype(jnp.float32) + core_swap(theirs).astype(jnp.float32)
    input_grad = (total * row_mask.astype(jnp.float32)[:, None]).astype(jnp.bfloat16)
    new_momentum = jnp.where(inner, new_own, jnp.concatenate(returned, 0))[None]
    votes_other, new_momentum, input_grad = after((core_swap(votes), new_momentum, input_grad))
    rollout_weight = vote_step(core[None], votes, votes_other, w_key, w_other)[None]
    return (input_grad, new_momentum, rollout_weight)


def solution(mesh):
    return jax.shard_map(
        per_device,
        mesh=mesh,
        in_specs=(
            P(("section", "dp", "tensor"), None),
            P(("section", "dp"), "tensor"),
            P(("section", "dp", "tensor")),
            P("section", "tensor"),
            P("dp", "section", "tensor"),
        ),
        out_specs=(
            P(("section", "dp", "tensor"), None),
            P("dp", "section", "tensor"),
            P("tensor", "section", None),
        ),
        check_vma=False,
    )
```

time: 235 us -> 192 us (0.82)
  waiting for transfers between devices: 102 us -> 73.4 us
  between operations: 1.09 us -> 14.3 us
  local copies, waits for them, and re-layouts: 21.7 us -> 10.7 us
  Pallas kernels: 34.3 us -> 25.7 us
  starting transfers between devices: 62.9 us -> 57 us
    ppermute x34 -> x29, waiting for transfers between devices: 102 us -> 73.3 us  [permute(): return lax.ppermute(array, AXES, pairs)]
    pallas_call x4 -> x5, Pallas kernels: 29.5 us -> 22.5 us  [the longest x2 10.1 us: gather_step(): pl.pallas_call(gather_kernel, grid_spec=pltpu.PrefetchScalarGridSpec(num_...]
    unnamed x42 -> x29, local copies, waits for them, and re-layouts: 11 us -> 4.49 us
    ppermute x34 -> x29, starting transfers between devices: 62.9 us -> 57 us  [permute(): return lax.ppermute(array, AXES, pairs)]
    concatenate x4 -> x1, local copies, waits for them, and re-layouts: 3.52 us -> 0.02 us  [per_device(): cot_mine = jnp.concatenate(cot_pieces, 1)]
    convert_element_type x0 -> x1, other arithmetic: none -> 3.34 us  [per_device(): (total * row_mask.astype(jnp.float32)[:, None]).astype(jnp.bfloat16)]
    concatenate x4 -> x3, other arithmetic: 5.15 us -> 2.24 us  [the longest x1 2.15 us: per_device(): jnp.concatenate([w_rest[0], w_rest[1], jnp.concatenate(w_rest[2:], 0)], 1)]
    select_n x2 -> x1, other arithmetic: 2.7 us -> 0.02 us  [per_device(): jnp.where(inner, jnp.stack([words, words_flip]), jnp.stack([side_here, si...]
  transfers between devices with their start and end apart: 34 -> 30, of which waited for: 13 -> 11; matrix products, arithmetic and copies ran while one was open for 12% -> 7% of each run, Pallas kernels for 13% -> 12%
where the time goes in v2:
time: 192 us
  waiting for transfers between devices  73.4 us (38%)
  starting transfers between devices  57 us (30%)
  Pallas kernels  25.7 us (13%)
  between operations  14.3 us (7%)
  local copies, waits for them, and re-layouts  10.7 us (6%)
  other arithmetic  10.5 us (5%)
    ppermute x29, waiting for transfers between devices, permute(): return lax.ppermute(array, AXES, pairs)  73.3 us
    ppermute x29, starting transfers between devices, permute(): return lax.ppermute(array, AXES, pairs)  57 us
    pallas_call x2, Pallas kernels, gather_step(): pl.pallas_call(gather_kernel, grid_spec=pltpu.PrefetchScalarGridSpec(num_...  10.1 us
    pallas_call x2, Pallas kernels, momentum_step(): pl.pallas_call(momentum_kernel, grid_spec=pltpu.PrefetchScalarGridSpec(nu...  7.7 us
    pallas_call x1, Pallas kernels, input_step(): pl.pallas_call(input_kernel, grid=(features // width,), in_specs=[pl.Bloc...  4.69 us
    unnamed x29, local copies, waits for them, and re-layouts  4.49 us
  transfers between devices with their start and end apart: 30, of which 11 were waited for; matrix products, arithmetic and copies ran while one was open for 7% of the time, Pallas kernels for 12%

profile of v2, /device:TPU:1, one launch (start us, length us, event | category | flops | bytes accessed | tf_op | source)
XLA Modules:
  0.0 191.7 jit_solution(6393850987597477362)
XLA Ops:
  7.2 0.0 all-gather.2.cloned.1.call-start
  7.2 1.7 constant_dynamic-slice_fusion.8
  9.0 2.5 %collective-permute-start = (bf16[1280,128]{1,0:T(8,128)(2,1)}, bf16[1280,128]{1,0:T(8,128)(2,1)}, u32[]{:S(2)}, u32[]{:S(2)}) collective-permute-start(bf16[1280,128]{1,0:T(8,128)(2,1)} %constant_dynamic-slice_fusion.8), channel_id=1, source_target_pairs={{0,8},{4,12},{8,0},{12,4},{16,24},{20,28},{24,16},{28,20},{32,40},... | collective-permute-start | bytes 983048 | tf_op jit(solution)/shard_map/ppermute | solution.py:31
  11.4 4.7 %collective-permute-start.1 = (bf16[1280,128]{1,0:T(8,128)(2,1)}, bf16[1280,128]{1,0:T(8,128)(2,1)}, u32[]{:S(2)}, u32[]{:S(2)}) collective-permute-start(bf16[1280,128]{1,0:T(8,128)(2,1)} %constant_dynamic-slice_fusion.8), channel_id=1, source_target_pairs={{0,152},{4,156},{8,16},{12,20},{16,8},{20,12},{24,128},{28,132},{3... | collective-permute-start | bytes 983048 | tf_op jit(solution)/shard_map/ppermute | solution.py:31
  16.1 1.0 constant_dynamic-slice_fusion
  17.1 1.2 collective-permute-start.2
  18.4 1.2 collective-permute-start.3
  19.5 0.7 broadcast_compare_fusion
  20.2 1.6 broadcast_select_fusion.refs_0_
  21.9 0.0 copy-start.11
  21.9 7.5 %collective-permute-done.2 = bf16[640,128]{1,0:T(8,128)(2,1)S(1)} collective-permute-done((bf16[640,128]{1,0:T(8,128)(2,1)S(1)}, bf16[640,128]{1,0:T(8,128)(2,1)S(1)}, u32[]{:S(2)}, u32[]{:S(2)}) %collective-permute-start.2) | collective-permute-done | bytes 163872 | tf_op jit(solution)/shard_map/ppermute | solution.py:31
  29.4 2.1 %maximum_maximum_fusion = bf16[1280,384]{1,0:T(8,128)(2,1)} fusion(bf16[640,128]{1,0:T(8,128)(2,1)S(1)} %collective-permute-done.3, bf16[640,128]{1,0:T(8,128)(2,1)S(1)} %collective-permute-done.2, bf16[1280,128]{1,0:T(8,128)(2,1)} %collective-permute-done.1, bf16[1280,128]{1,0:T(8,128)(2,1)} %collective-permute-done), kind=kLoop, calls=%fused_computation.5 | loop fusion | flops 3932160 | bytes 1966080 | tf_op jit(solution)/shard_map/concatenate | solution.py:311
  31.5 0.0 all-gather.2.cloned.1.call-update
  31.6 1.8 collective-permute-start.4
  33.4 6.3 %collective-permute-start.5 = (bf16[160,5120]{1,0:T(8,128)(2,1)S(1)}, bf16[160,5120]{1,0:T(8,128)(2,1)}, u32[]{:S(2)}, u32[]{:S(2)}) collective-permute-start(bf16[160,5120]{1,0:T(8,128)(2,1)S(1)} %broadcast_select_fusion.refs_0_), channel_id=1, source_target_pairs={{0,8},{4,12},{24,16},{28,20},{32,40},{36,44},{56,48},{60,52},{64,7... | collective-permute-start | bytes 4915208 | tf_op jit(solution)/shard_map/ppermute | solution.py:31
  39.7 2.1 %collective-permute-start.6 = (bf16[160,5120]{1,0:T(8,128)(2,1)S(1)}, bf16[160,5120]{1,0:T(8,128)(2,1)}, u32[]{:S(2)}, u32[]{:S(2)}) collective-permute-start(bf16[160,5120]{1,0:T(8,128)(2,1)S(1)} %broadcast_select_fusion.refs_0_), channel_id=1, source_target_pairs={{0,4},{4,0},{8,12},{12,8},{16,20},{20,16},{24,28},{28,24},{32,36},... | collective-permute-start | bytes 4915208 | tf_op jit(solution)/shard_map/ppermute | solution.py:31
  41.8 0.1 collective-permute-start.7
  41.9 1.7 collective-permute-start.8
  43.6 0.9 slice_bitcast_fusion
  44.6 28.8 %collective-permute-done.7 = bf16[320,128]{1,0:T(8,128)(2,1)S(1)} collective-permute-done((bf16[320,128]{1,0:T(8,128)(2,1)S(1)}, bf16[320,128]{1,0:T(8,128)(2,1)S(1)}, u32[]{:S(2)}, u32[]{:S(2)}) %collective-permute-start.7) | collective-permute-done | bytes 81952 | tf_op jit(solution)/shard_map/ppermute | solution.py:31
  73.4 2.8 %collective-permute-start.9 = (bf16[320,128]{1,0:T(8,128)(2,1)S(1)}, bf16[320,128]{1,0:T(8,128)(2,1)S(1)}, u32[]{:S(2)}, u32[]{:S(2)}) collective-permute-start(bf16[320,128]{1,0:T(8,128)(2,1)S(1)} %get-tuple-element.117), channel_id=1, source_target_pairs={{0,16},{4,20},{8,24},{12,28},{16,0},{20,4},{24,8},{28,12},{32,48},... | collective-permute-start | bytes 245768 | tf_op jit(solution)/shard_map/ppermute | solution.py:31
  76.2 0.1 pad_maximum_fusion
  76.2 1.2 collective-permute-done.8
  77.4 1.1 collective-permute-done.9
  78.5 4.0 %collective-permute-start.12 = (bf16[160,5120]{1,0:T(8,128)(2,1)}, bf16[160,5120]{1,0:T(8,128)(2,1)}, u32[]{:S(2)}, u32[]{:S(2)}) collective-permute-start(bf16[160,5120]{1,0:T(8,128)(2,1)} %collective-permute-done.4.refs_4_), channel_id=1, source_target_pairs={{0,4},{4,0},{8,12},{12,8},{16,20},{20,16},{24,28},{28,24},{32,36},... | collective-permute-start | bytes 4915208 | tf_op jit(solution)/shard_map/ppermute | solution.py:31
  82.5 0.1 collective-permute-start.13
  82.6 0.4 collective-permute-start.14
  83.0 4.2 %collective-permute-start.11 = (bf16[3840,128]{1,0:T(8,128)(2,1)S(1)}, bf16[3840,128]{1,0:T(8,128)(2,1)S(1)}, u32[]{:S(2)}, u32[]{:S(2)}) collective-permute-start(bf16[3840,128]{1,0:T(8,128)(2,1)S(1)} %pad_maximum_fusion), channel_id=1, source_target_pairs={{0,8},{4,12},{24,16},{28,20},{32,40},{36,44},{56,48},{60,52},{64,7... | collective-permute-start | bytes 2949128 | tf_op jit(solution)/shard_map/ppermute | solution.py:31
  87.2 2.4 %fusion.1 = (bf16[160,2560]{1,0:T(8,128)(2,1)}, bf16[160,2560]{1,0:T(8,128)(2,1)S(1)}) fusion(bf16[160,5120]{1,0:T(8,128)(2,1)} %collective-permute-done.5.refs_2_), kind=kLoop, calls=%fused_computation.25 | loop fusion | bytes 3276800 | tf_op jit(solution)/shard_map/slice | solution.py:337
  89.6 1.6 collective-permute-start.10
  91.1 1.1 copy-done.6
  92.2 16.0 %collective-permute-done.11.refs_7_.refs_3_.refs_6_ = bf16[3840,128]{1,0:T(8,128)(2,1)S(1)} collective-permute-done((bf16[3840,128]{1,0:T(8,128)(2,1)S(1)}, bf16[3840,128]{1,0:T(8,128)(2,1)S(1)}, u32[]{:S(2)}, u32[]{:S(2)}) %collective-permute-start.11) | collective-permute-done | bytes 983072 | tf_op jit(solution)/shard_map/ppermute | solution.py:31
  108.2 0.9 collective-permute-start.17
  109.1 1.5 collective-permute-start.15
  110.6 6.4 %collective-permute-start.16 = (bf16[2560,128]{1,0:T(8,128)(2,1)}, bf16[2560,128]{1,0:T(8,128)(2,1)}, u32[]{:S(2)}, u32[]{:S(2)}) collective-permute-start(bf16[2560,128]{1,0:T(8,128)(2,1)} %get-tuple-element.111), channel_id=1, source_target_pairs={{0,8},{4,12},{24,16},{28,20},{32,40},{36,44},{56,48},{60,52},{64,7... | collective-permute-start | bytes 1966088 | tf_op jit(solution)/shard_map/ppermute | solution.py:31
  117.0 0.1 stack.53.place
  117.1 5.1 %gather_step.3.refs_4_ = f32[2560,256]{1,0:T(8,128)} custom-call(s32[8]{0:T(128)S(1)} %stack.53.place, bf16[160,5120]{1,0:T(8,128)(2,1)S(1)} %broadcast_select_fusion.refs_0_, bf16[160,5120]{1,0:T(8,128)(2,1)} %collective-permute-done.6.refs_1_, bf16[160,5120]{1,0:T(8,128)(2,1)} %collective-permute-done.5.refs_2_, ...), custom_call_target="tpu_custom_call" | custom-call | flops 1258291200 | bytes 7536640 | tf_op jit(solution)/shard_map/gather_step/pallas_call | solution.py:102
  122.2 5.0 %gather_step.2.refs_4_ = f32[2560,256]{1,0:T(8,128)} custom-call(s32[8]{0:T(128)S(1)} %stack.53.place, bf16[160,5120]{1,0:T(8,128)(2,1)S(1)} %broadcast_select_fusion.refs_0_, bf16[160,5120]{1,0:T(8,128)(2,1)} %collective-permute-done.6.refs_1_, bf16[160,5120]{1,0:T(8,128)(2,1)} %collective-permute-done.5.refs_2_, ...), custom_call_target="tpu_custom_call" | custom-call | flops 1258291200 | bytes 7536640 | tf_op jit(solution)/shard_map/gather_step/pallas_call | solution.py:102
  127.2 3.8 %momentum_step.2 = (bf16[5120,128]{1,0:T(8,128)(2,1)S(1)}, bf16[2560,128]{1,0:T(8,128)(2,1)S(1)}, s32[160,128]{1,0:T(8,128)S(1)}, s32[160,128]{1,0:T(8,128)S(1)}) custom-call(s32[8]{0:T(128)S(1)} %stack.53.place, bf16[160,2560]{1,0:T(8,128)(2,1)} %collective-permute-done.10.refs_0_, bf16[160,2560]{1,0:T(8,128)(2,1)} %collective-permute-done.17.refs_1_, ...), custom_call_target="tpu_custom_call" | custom-call | flops 419430400 | bytes 6881280 | tf_op jit(solution)/shard_map/momentum_step/pallas_call | solution.py:154
  131.0 0.8 copy-done.10
  131.8 0.6 collective-permute-start.18
  132.4 1.5 collective-permute-start.22
  133.9 0.8 collective-permute-done.18.refs_1_
  134.7 3.9 %momentum_step.3 = (bf16[5120,128]{1,0:T(8,128)(2,1)S(1)}, bf16[2560,128]{1,0:T(8,128)(2,1)S(1)}, s32[160,128]{1,0:T(8,128)S(1)}, s32[160,128]{1,0:T(8,128)S(1)}) custom-call(s32[8]{0:T(128)S(1)} %stack.53.place, bf16[160,2560]{1,0:T(8,128)(2,1)} %collective-permute-done.15.refs_0_, ...), custom_call_target="tpu_custom_call", output_to_operand_aliasing={{0}: (8, {}), {2}: (9, {}), {3}: (10, {})} | custom-call | flops 419430400 | bytes 6881280 | tf_op jit(solution)/shard_map/momentum_step/pallas_call | solution.py:154
  138.7 1.3 collective-permute-start.20
  140.0 1.3 collective-permute-start.21
  141.3 0.7 collective-permute-start.19
  142.1 0.0 all-gather.2.cloned.1.call-done.w_rest
  142.2 1.3 copy-done.2
  143.5 4.7 %input_step.1 = (bf16[160,5120]{1,0:T(8,128)(2,1)S(1)}, bf16[160,5120]{1,0:T(8,128)(2,1)}) custom-call(bf16[320,512]{1,0:T(8,128)(2,1)S(1)} %pad_maximum_fusion.1.cot, bf16[5120,128]{1,0:T(8,128)(2,1)S(1)} %copy-done.2, bf16[5120,384]{1,0:T(8,128)(2,1)} %all-gather.2.cloned.1.call-done.w_rest), custom_call_target="tpu_custom_call" | custom-call | flops 1677721600 | bytes 8519680 | tf_op jit(solution)/shard_map/input_step/pallas_call | solution.py:264
  148.2 1.2 copy-done.4
  149.3 3.4 %collective-permute-done.22 = bf16[2560,128]{1,0:T(8,128)(2,1)} collective-permute-done((bf16[2560,128]{1,0:T(8,128)(2,1)}, bf16[2560,128]{1,0:T(8,128)(2,1)}, u32[]{:S(2)}, u32[]{:S(2)}) %collective-permute-start.22) | collective-permute-done | bytes 655392 | tf_op jit(solution)/shard_map/ppermute | solution.py:31
  152.7 1.6 collective-permute-done.20
  154.4 1.3 collective-permute-start.27
  155.6 1.3 collective-permute-start.28
  157.0 2.8 %collective-permute-start.23 = (s32[2,160,128]{2,1,0:T(8,128)S(1)}, s32[2,160,128]{2,1,0:T(8,128)S(1)}, u32[]{:S(2)}, u32[]{:S(2)}) collective-permute-start(s32[2,160,128]{2,1,0:T(8,128)S(1)} %add_select_fusion), channel_id=1, source_target_pairs={{0,96},{4,100},{8,104},{12,108},{16,112},{20,116},{24,120},{28,124... | collective-permute-start | bytes 491528 | tf_op jit(solution)/shard_map/ppermute | solution.py:31
  159.8 1.6 collective-permute-start.25
  161.5 1.9 %collective-permute-done.23 = s32[2,160,128]{2,1,0:T(8,128)S(1)} collective-permute-done((s32[2,160,128]{2,1,0:T(8,128)S(1)}, s32[2,160,128]{2,1,0:T(8,128)S(1)}, u32[]{:S(2)}, u32[]{:S(2)}) %collective-permute-start.23) | collective-permute-done | bytes 163872 | tf_op jit(solution)/shard_map/ppermute | solution.py:31
  163.4 6.6 %collective-permute-done.24 = s32[2,160,128]{2,1,0:T(8,128)S(1)} collective-permute-done((s32[2,160,128]{2,1,0:T(8,128)S(1)}, s32[2,160,128]{2,1,0:T(8,128)S(1)}, u32[]{:S(2)}, u32[]{:S(2)}) %collective-permute-start.24) | collective-permute-done | bytes 163872 | tf_op jit(solution)/shard_map/ppermute | solution.py:31
  170.1 1.2 collective-permute-start.26
  171.3 4.3 %collective-permute-done.27 = bf16[2560,128]{1,0:T(8,128)(2,1)S(1)} collective-permute-done((bf16[2560,128]{1,0:T(8,128)(2,1)S(1)}, bf16[2560,128]{1,0:T(8,128)(2,1)S(1)}, u32[]{:S(2)}, u32[]{:S(2)}) %collective-permute-start.27) | collective-permute-done | bytes 655392 | tf_op jit(solution)/shard_map/ppermute | solution.py:31
  175.6 2.6 %fusion = bf16[1,5120,128]{2,1,0:T(8,128)(2,1)} fusion(bf16[5120,128]{1,0:T(8,128)(2,1)S(1)} %get-tuple-element.100, bf16[2560,128]{1,0:T(8,128)(2,1)S(1)} %collective-permute-done.27, bf16[2560,128]{1,0:T(8,128)(2,1)} %collective-permute-done.22, pred[]{:T(512)S(6)} %or.3), kind=kLoop, calls=%fused_computation.3 | loop fusion | flops 3276800 | bytes 3932161 | tf_op jit(solution)/shard_map/broadcast_in_dim | solution.py:373
  178.2 3.3 %multiply_convert_fusion = bf16[160,5120]{1,0:T(8,128)(2,1)} fusion(bf16[160,5120]{1,0:T(8,128)(2,1)} %collective-permute-done.28, bf16[160,5120]{1,0:T(8,128)(2,1)S(1)} %copy-done.5, f32[160]{0:T(256)S(1)} %convert_element_type.14), kind=kLoop, calls=%fused_computation | loop fusion | flops 4096000 | bytes 4915840 | tf_op jit(solution)/shard_map/convert_element_type | solution.py:372
  181.6 3.2 %vote_step.1 = bf16[5120,256]{1,0:T(8,128)(2,1)} custom-call(s32[1]{0:T(128)} %bitcast.16.core, s32[8,160,128]{2,1,0:T(8,128)S(1)} %pad_add_fusion.words_own, s32[8,160,128]{2,1,0:T(8,128)S(1)} %collective-permute-done.26.words_other, bf16[5120,128]{1,0:T(8,128)(2,1)S(1)} %copy-done.3, bf16[5120,128]{1,0:T(8,128)(2,1)S(1)} %copy-done.7), custom_call_target="tpu_custom_call" | custom-call | flops 10485760 | bytes 6553600 | tf_op jit(solution)/shard_map/vote_step/pallas_call | solution.py:234
  (50 shorter events, 0.3 us)
Async XLA Ops:
  7.2 135.0 %all-gather.2.cloned.1.call-start = ((), (), s32[]{:S(2)}) async-start(), calls=%async_computation | async-start | bytes 4915200 | tf_op jit(solution)/shard_map/all_gather | solution.py:310
  9.0 20.4 %collective-permute-start = (bf16[1280,128]{1,0:T(8,128)(2,1)}, bf16[1280,128]{1,0:T(8,128)(2,1)}, u32[]{:S(2)}, u32[]{:S(2)}) collective-permute-start(bf16[1280,128]{1,0:T(8,128)(2,1)} %constant_dynamic-slice_fusion.8), channel_id=1, source_target_pairs={{0,8},{4,12},{8,0},{12,4},{16,24},{20,28},{24,16},{28,20},{32,40},... | collective-permute-start | bytes 983048 | tf_op jit(solution)/shard_map/ppermute | solution.py:31
  11.4 18.0 %collective-permute-start.1 = (bf16[1280,128]{1,0:T(8,128)(2,1)}, bf16[1280,128]{1,0:T(8,128)(2,1)}, u32[]{:S(2)}, u32[]{:S(2)}) collective-permute-start(bf16[1280,128]{1,0:T(8,128)(2,1)} %constant_dynamic-slice_fusion.8), channel_id=1, source_target_pairs={{0,152},{4,156},{8,16},{12,20},{16,8},{20,12},{24,128},{28,132},{3... | collective-permute-start | bytes 983048 | tf_op jit(solution)/shard_map/ppermute | solution.py:31
  17.1 12.3 %collective-permute-start.2 = (bf16[640,128]{1,0:T(8,128)(2,1)S(1)}, bf16[640,128]{1,0:T(8,128)(2,1)S(1)}, u32[]{:S(2)}, u32[]{:S(2)}) collective-permute-start(bf16[640,128]{1,0:T(8,128)(2,1)S(1)} %get-tuple-element.114), channel_id=1, source_target_pairs={{0,144},{4,148},{8,152},{12,156},{16,0},{20,4},{24,8},{28,12},{32,... | collective-permute-start | bytes 491528 | tf_op jit(solution)/shard_map/ppermute | solution.py:31
  18.4 11.0 %collective-permute-start.3 = (bf16[640,128]{1,0:T(8,128)(2,1)S(1)}, bf16[640,128]{1,0:T(8,128)(2,1)S(1)}, u32[]{:S(2)}, u32[]{:S(2)}) collective-permute-start(bf16[640,128]{1,0:T(8,128)(2,1)S(1)} %get-tuple-element.113), channel_id=1, source_target_pairs={{0,16},{4,20},{8,24},{12,28},{16,128},{20,132},{24,136},{28,140},{... | collective-permute-start | bytes 491528 | tf_op jit(solution)/shard_map/ppermute | solution.py:31
  21.8 19.9 %copy-start = (bf16[1280,128]{1,0:T(8,128)(2,1)S(1)}, bf16[1280,128]{1,0:T(8,128)(2,1)}, u32[]{:S(2)}) copy-start(bf16[1280,128]{1,0:T(8,128)(2,1)} %refs_2_.3) | copy-start | bytes 983044
  21.9 21.8 %copy-start.11 = (bf16[1,5120,128]{2,1,0:T(8,128)(2,1)S(1)}, bf16[1,5120,128]{2,1,0:T(8,128)(2,1)}, u32[]{:S(2)}) copy-start(bf16[1,5120,128]{2,1,0:T(8,128)(2,1)} %param.9) | copy-start | bytes 3932164
  31.6 46.9 %collective-permute-start.4 = (bf16[160,5120]{1,0:T(8,128)(2,1)S(1)}, bf16[160,5120]{1,0:T(8,128)(2,1)}, u32[]{:S(2)}, u32[]{:S(2)}) collective-permute-start(bf16[160,5120]{1,0:T(8,128)(2,1)S(1)} %broadcast_select_fusion.refs_0_), channel_id=1, source_target_pairs={{8,16},{12,20},{16,8},{20,12},{40,48},{44,52},{48,40},{52,44},{72,... | collective-permute-start | bytes 4915208 | tf_op jit(solution)/shard_map/ppermute | solution.py:31
  33.4 45.1 %collective-permute-start.5 = (bf16[160,5120]{1,0:T(8,128)(2,1)S(1)}, bf16[160,5120]{1,0:T(8,128)(2,1)}, u32[]{:S(2)}, u32[]{:S(2)}) collective-permute-start(bf16[160,5120]{1,0:T(8,128)(2,1)S(1)} %broadcast_select_fusion.refs_0_), channel_id=1, source_target_pairs={{0,8},{4,12},{24,16},{28,20},{32,40},{36,44},{56,48},{60,52},{64,7... | collective-permute-start | bytes 4915208 | tf_op jit(solution)/shard_map/ppermute | solution.py:31
  39.7 38.8 %collective-permute-start.6 = (bf16[160,5120]{1,0:T(8,128)(2,1)S(1)}, bf16[160,5120]{1,0:T(8,128)(2,1)}, u32[]{:S(2)}, u32[]{:S(2)}) collective-permute-start(bf16[160,5120]{1,0:T(8,128)(2,1)S(1)} %broadcast_select_fusion.refs_0_), channel_id=1, source_target_pairs={{0,4},{4,0},{8,12},{12,8},{16,20},{20,16},{24,28},{28,24},{32,36},... | collective-permute-start | bytes 4915208 | tf_op jit(solution)/shard_map/ppermute | solution.py:31
  41.8 31.6 %collective-permute-start.7 = (bf16[320,128]{1,0:T(8,128)(2,1)S(1)}, bf16[320,128]{1,0:T(8,128)(2,1)S(1)}, u32[]{:S(2)}, u32[]{:S(2)}) collective-permute-start(bf16[320,128]{1,0:T(8,128)(2,1)S(1)} %get-tuple-element.119), channel_id=1, source_target_pairs={{0,8},{4,12},{8,0},{12,4},{16,24},{20,28},{24,16},{28,20},{32,40},... | collective-permute-start | bytes 245768 | tf_op jit(solution)/shard_map/ppermute | solution.py:31
  41.9 35.5 %collective-permute-start.8 = (bf16[320,128]{1,0:T(8,128)(2,1)S(1)}, bf16[320,128]{1,0:T(8,128)(2,1)S(1)}, u32[]{:S(2)}, u32[]{:S(2)}) collective-permute-start(bf16[320,128]{1,0:T(8,128)(2,1)S(1)} %get-tuple-element.118), channel_id=1, source_target_pairs={{0,24},{4,28},{8,16},{12,20},{16,8},{20,12},{24,0},{28,4},{32,56},... | collective-permute-start | bytes 245768 | tf_op jit(solution)/shard_map/ppermute | solution.py:31
  44.6 38.0 %copy-start.1 = (bf16[5120,128]{1,0:T(8,128)(2,1)S(1)}, bf16[5120,128]{1,0:T(8,128)(2,1)}, u32[]{:S(2)}) copy-start(bf16[5120,128]{1,0:T(8,128)(2,1)} %w_own.3) | copy-start | bytes 3932164
  73.4 5.1 %collective-permute-start.9 = (bf16[320,128]{1,0:T(8,128)(2,1)S(1)}, bf16[320,128]{1,0:T(8,128)(2,1)S(1)}, u32[]{:S(2)}, u32[]{:S(2)}) collective-permute-start(bf16[320,128]{1,0:T(8,128)(2,1)S(1)} %get-tuple-element.117), channel_id=1, source_target_pairs={{0,16},{4,20},{8,24},{12,28},{16,0},{20,4},{24,8},{28,12},{32,48},... | collective-permute-start | bytes 245768 | tf_op jit(solution)/shard_map/ppermute | solution.py:31
  78.5 29.7 %collective-permute-start.12 = (bf16[160,5120]{1,0:T(8,128)(2,1)}, bf16[160,5120]{1,0:T(8,128)(2,1)}, u32[]{:S(2)}, u32[]{:S(2)}) collective-permute-start(bf16[160,5120]{1,0:T(8,128)(2,1)} %collective-permute-done.4.refs_4_), channel_id=1, source_target_pairs={{0,4},{4,0},{8,12},{12,8},{16,20},{20,16},{24,28},{28,24},{32,36},... | collective-permute-start | bytes 4915208 | tf_op jit(solution)/shard_map/ppermute | solution.py:31
  82.5 25.7 %collective-permute-start.13 = (bf16[160,5120]{1,0:T(8,128)(2,1)}, bf16[160,5120]{1,0:T(8,128)(2,1)}, u32[]{:S(2)}, u32[]{:S(2)}) collective-permute-start(bf16[160,5120]{1,0:T(8,128)(2,1)} %collective-permute-done.5.refs_2_), channel_id=1, source_target_pairs={{0,4},{4,0},{8,12},{12,8},{16,20},{20,16},{24,28},{28,24},{32,36},... | collective-permute-start | bytes 4915208 | tf_op jit(solution)/shard_map/ppermute | solution.py:31
  82.6 8.6 %collective-permute-start.14 = (bf16[5120,128]{1,0:T(8,128)(2,1)S(1)}, bf16[5120,128]{1,0:T(8,128)(2,1)S(1)}, u32[]{:S(2)}, u32[]{:S(2)}) collective-permute-start(bf16[5120,128]{1,0:T(8,128)(2,1)S(1)} %copy-done.1), channel_id=1, source_target_pairs={{0,4},{4,0},{8,12},{12,8},{16,20},{20,16},{24,28},{28,24},{32,36},... | collective-permute-start | bytes 3932168 | tf_op jit(solution)/shard_map/ppermute | solution.py:31
  83.0 25.2 %collective-permute-start.11 = (bf16[3840,128]{1,0:T(8,128)(2,1)S(1)}, bf16[3840,128]{1,0:T(8,128)(2,1)S(1)}, u32[]{:S(2)}, u32[]{:S(2)}) collective-permute-start(bf16[3840,128]{1,0:T(8,128)(2,1)S(1)} %pad_maximum_fusion), channel_id=1, source_target_pairs={{0,8},{4,12},{24,16},{28,20},{32,40},{36,44},{56,48},{60,52},{64,7... | collective-permute-start | bytes 2949128 | tf_op jit(solution)/shard_map/ppermute | solution.py:31
  89.6 2.7 %collective-permute-start.10 = (bf16[160,2560]{1,0:T(8,128)(2,1)S(1)}, bf16[160,2560]{1,0:T(8,128)(2,1)}, u32[]{:S(2)}, u32[]{:S(2)}) collective-permute-start(bf16[160,2560]{1,0:T(8,128)(2,1)S(1)} %get-tuple-element.110), channel_id=1, source_target_pairs={{8,16},{12,20},{16,8},{20,12},{40,48},{44,52},{48,40},{52,44},{72,... | collective-permute-start | bytes 2457608 | tf_op jit(solution)/shard_map/ppermute | solution.py:31
  91.1 1.1 copy-start.6
  108.2 19.0 %collective-permute-start.17 = (bf16[160,2560]{1,0:T(8,128)(2,1)}, bf16[160,2560]{1,0:T(8,128)(2,1)}, u32[]{:S(2)}, u32[]{:S(2)}) collective-permute-start(bf16[160,2560]{1,0:T(8,128)(2,1)} %collective-permute-done.10.refs_0_), channel_id=1, source_target_pairs={{0,4},{4,0},{8,12},{12,8},{16,20},{20,16},{24,28},{28,24},{32,36},... | collective-permute-start | bytes 2457608 | tf_op jit(solution)/shard_map/ppermute | solution.py:31
  109.1 22.8 %collective-permute-start.15 = (bf16[160,2560]{1,0:T(8,128)(2,1)}, bf16[160,2560]{1,0:T(8,128)(2,1)}, u32[]{:S(2)}, u32[]{:S(2)}) collective-permute-start(bf16[160,2560]{1,0:T(8,128)(2,1)} %get-tuple-element.109), channel_id=1, source_target_pairs={{8,16},{12,20},{16,8},{20,12},{40,48},{44,52},{48,40},{52,44},{72,... | collective-permute-start | bytes 2457608 | tf_op jit(solution)/shard_map/ppermute | solution.py:31
  110.6 21.2 %collective-permute-start.16 = (bf16[2560,128]{1,0:T(8,128)(2,1)}, bf16[2560,128]{1,0:T(8,128)(2,1)}, u32[]{:S(2)}, u32[]{:S(2)}) collective-permute-start(bf16[2560,128]{1,0:T(8,128)(2,1)} %get-tuple-element.111), channel_id=1, source_target_pairs={{0,8},{4,12},{24,16},{28,20},{32,40},{36,44},{56,48},{60,52},{64,7... | collective-permute-start | bytes 1966088 | tf_op jit(solution)/shard_map/ppermute | solution.py:31
  131.0 0.9 copy-start.10
  131.8 2.9 %collective-permute-start.18 = (bf16[160,2560]{1,0:T(8,128)(2,1)}, bf16[160,2560]{1,0:T(8,128)(2,1)}, u32[]{:S(2)}, u32[]{:S(2)}) collective-permute-start(bf16[160,2560]{1,0:T(8,128)(2,1)} %collective-permute-done.15.refs_0_), channel_id=1, source_target_pairs={{0,4},{4,0},{8,12},{12,8},{16,20},{20,16},{24,28},{28,24},{32,36},... | collective-permute-start | bytes 2457608 | tf_op jit(solution)/shard_map/ppermute | solution.py:31
  132.4 20.3 %collective-permute-start.22 = (bf16[2560,128]{1,0:T(8,128)(2,1)}, bf16[2560,128]{1,0:T(8,128)(2,1)}, u32[]{:S(2)}, u32[]{:S(2)}) collective-permute-start(bf16[2560,128]{1,0:T(8,128)(2,1)} %copy-done.10), channel_id=1, source_target_pairs={{8,0},{12,4},{16,24},{20,28},{40,32},{44,36},{48,56},{52,60},{72,6... | collective-permute-start | bytes 1966088 | tf_op jit(solution)/shard_map/ppermute | solution.py:31
  138.7 3.4 %copy-start.8 = (bf16[2560,128]{1,0:T(8,128)(2,1)}, bf16[2560,128]{1,0:T(8,128)(2,1)S(1)}, u32[]{:S(2)}) copy-start(bf16[2560,128]{1,0:T(8,128)(2,1)S(1)} %get-tuple-element.102) | copy-start | bytes 1966084
  138.7 15.7 %collective-permute-start.20 = (s32[160,128]{1,0:T(8,128)S(1)}, s32[160,128]{1,0:T(8,128)S(1)}, u32[]{:S(2)}, u32[]{:S(2)}) collective-permute-start(s32[160,128]{1,0:T(8,128)S(1)} %get-tuple-element.84), channel_id=1, source_target_pairs={{8,0},{12,4},{16,24},{20,28},{40,32},{44,36},{48,56},{52,60},{72,6... | collective-permute-start | bytes 245768 | tf_op jit(solution)/shard_map/ppermute | solution.py:31
  140.0 14.4 %collective-permute-start.21 = (s32[160,128]{1,0:T(8,128)S(1)}, s32[160,128]{1,0:T(8,128)S(1)}, u32[]{:S(2)}, u32[]{:S(2)}) collective-permute-start(s32[160,128]{1,0:T(8,128)S(1)} %get-tuple-element.84), channel_id=1, source_target_pairs={{8,128},{12,132},{16,152},{20,156},{40,160},{44,164},{48,184},{52,... | collective-permute-start | bytes 245768 | tf_op jit(solution)/shard_map/ppermute | solution.py:31
  141.3 11.4 %collective-permute-start.19 = (s32[160,128]{1,0:T(8,128)S(1)}, s32[160,128]{1,0:T(8,128)S(1)}, u32[]{:S(2)}, u32[]{:S(2)}) collective-permute-start(s32[160,128]{1,0:T(8,128)S(1)} %get-tuple-element.83), channel_id=1, source_target_pairs={{8,136},{12,140},{16,144},{20,148},{40,168},{44,172},{48,176},{52,... | collective-permute-start | bytes 245768 | tf_op jit(solution)/shard_map/ppermute | solution.py:31
  142.2 1.3 copy-start.2
  143.5 10.9 %copy-start.9 = (bf16[2560,128]{1,0:T(8,128)(2,1)S(1)}, bf16[2560,128]{1,0:T(8,128)(2,1)}, u32[]{:S(2)}) copy-start(bf16[2560,128]{1,0:T(8,128)(2,1)} %copy-done.8) | copy-start | bytes 1966084
  143.5 18.0 %copy-start.12 = (s32[160]{0:T(256)S(1)}, s32[160]{0:T(256)}, u32[]{:S(2)}) copy-start(s32[160]{0:T(256)} %param.7) | copy-start | bytes 1924
  148.2 1.2 copy-start.4
  154.4 21.3 %collective-permute-start.27 = (bf16[2560,128]{1,0:T(8,128)(2,1)S(1)}, bf16[2560,128]{1,0:T(8,128)(2,1)S(1)}, u32[]{:S(2)}, u32[]{:S(2)}) collective-permute-start(bf16[2560,128]{1,0:T(8,128)(2,1)S(1)} %copy-done.9), channel_id=1, source_target_pairs={{8,0},{12,4},{16,24},{20,28},{40,32},{44,36},{48,56},{52,60},{72,6... | collective-permute-start | bytes 1966088 | tf_op jit(solution)/shard_map/ppermute | solution.py:31
  155.6 22.6 %collective-permute-start.28 = (bf16[160,5120]{1,0:T(8,128)(2,1)}, bf16[160,5120]{1,0:T(8,128)(2,1)}, u32[]{:S(2)}, u32[]{:S(2)}) collective-permute-start(bf16[160,5120]{1,0:T(8,128)(2,1)} %get-tuple-element.104), channel_id=1, source_target_pairs={{0,4},{4,0},{8,12},{12,8},{16,20},{20,16},{24,28},{28,24},{32,36},... | collective-permute-start | bytes 4915208 | tf_op jit(solution)/shard_map/ppermute | solution.py:31
  157.0 6.4 %collective-permute-start.23 = (s32[2,160,128]{2,1,0:T(8,128)S(1)}, s32[2,160,128]{2,1,0:T(8,128)S(1)}, u32[]{:S(2)}, u32[]{:S(2)}) collective-permute-start(s32[2,160,128]{2,1,0:T(8,128)S(1)} %add_select_fusion), channel_id=1, source_target_pairs={{0,96},{4,100},{8,104},{12,108},{16,112},{20,116},{24,120},{28,124... | collective-permute-start | bytes 491528 | tf_op jit(solution)/shard_map/ppermute | solution.py:31
  159.8 10.2 %collective-permute-start.24 = (s32[2,160,128]{2,1,0:T(8,128)S(1)}, s32[2,160,128]{2,1,0:T(8,128)S(1)}, u32[]{:S(2)}, u32[]{:S(2)}) collective-permute-start(s32[2,160,128]{2,1,0:T(8,128)S(1)} %add_select_fusion), channel_id=1, source_target_pairs={{0,32},{4,36},{8,40},{12,44},{16,48},{20,52},{24,56},{28,60},{32,6... | collective-permute-start | bytes 491528 | tf_op jit(solution)/shard_map/ppermute | solution.py:31
  159.8 10.2 %collective-permute-start.25 = (s32[2,160,128]{2,1,0:T(8,128)S(1)}, s32[2,160,128]{2,1,0:T(8,128)S(1)}, u32[]{:S(2)}, u32[]{:S(2)}) collective-permute-start(s32[2,160,128]{2,1,0:T(8,128)S(1)} %add_select_fusion), channel_id=1, source_target_pairs={{0,64},{4,68},{8,72},{12,76},{16,80},{20,84},{24,88},{28,92},{32,9... | collective-permute-start | bytes 491528 | tf_op jit(solution)/shard_map/ppermute | solution.py:31
  170.1 11.5 %collective-permute-start.26 = (s32[8,160,128]{2,1,0:T(8,128)S(1)}, s32[8,160,128]{2,1,0:T(8,128)S(1)}, u32[]{:S(2)}, u32[]{:S(2)}) collective-permute-start(s32[8,160,128]{2,1,0:T(8,128)S(1)} %pad_add_fusion.words_own), channel_id=1, source_target_pairs={{0,4},{4,0},{8,12},{12,8},{16,20},{20,16},{24,28},{28,24},{32,36},... | collective-permute-start | bytes 1966088 | tf_op jit(solution)/shard_map/ppermute | solution.py:31
  175.6 2.6 %copy-start.5 = (bf16[160,5120]{1,0:T(8,128)(2,1)S(1)}, bf16[160,5120]{1,0:T(8,128)(2,1)}, u32[]{:S(2)}) copy-start(bf16[160,5120]{1,0:T(8,128)(2,1)} %copy-done.4) | copy-start | bytes 4915204
  178.2 3.4 %copy-start.3 = (bf16[5120,128]{1,0:T(8,128)(2,1)S(1)}, bf16[5120,128]{1,0:T(8,128)(2,1)}, u32[]{:S(2)}) copy-start(bf16[5120,128]{1,0:T(8,128)(2,1)} %w_own.3) | copy-start | bytes 3932164
  178.2 3.4 %copy-start.7 = (bf16[5120,128]{1,0:T(8,128)(2,1)S(1)}, bf16[5120,128]{1,0:T(8,128)(2,1)}, u32[]{:S(2)}) copy-start(bf16[5120,128]{1,0:T(8,128)(2,1)} %copy-done.6) | copy-start | bytes 3932164
Sparse Core Ops, SparseCore 0:
  31.7 50.6 all-gather.1

commit v3 on v2

--- a/solution.py
+++ b/solution.py
@@ -11,8 +11,9 @@
 
 AXES = ("dp", "tensor")
 HI, YS, LINE, CORES = 2, 4, 4, 2
-WIDTH = 1280
-CUT = 2560
+WIDTH = 1024
+CUT = 2048
+COST = pl.CostEstimate(flops=2_000_000_000, bytes_accessed=10_000_000, transcendentals=0)
 VMEM = 48 * 1024 * 1024
 
 
@@ -51,9 +52,9 @@
     return permute(array, place)
 
 
-def along_z(array, step):
+def opposite_heads(array):
     def place(h, y, c, k):
-        z = (h * LINE + c - step) % (HI * LINE)
+        z = (h * LINE + c + (2 if c >= 2 else -2)) % (HI * LINE)
         return z // LINE, y, z % LINE, k
 
     return permute(array, place)
@@ -63,16 +64,16 @@
     return permute(array, lambda h, y, c, k: (h, y, c ^ 1, k) if c in (0, 3) else None)
 
 
-def outward(array, flip=0):
-    return permute(array, lambda h, y, c, k: (h ^ flip, y, c ^ 1, k) if c in (1, 2) else None)
+def outward(array):
+    return permute(array, lambda h, y, c, k: (h, y, c ^ 1, k) if c in (1, 2) else None)
 
 
 def across(array):
     return permute(array, lambda h, y, c, k: (h, y, 3 - c, k) if c in (1, 2) else None)
 
 
-def inner_flip(array):
-    return permute(array, lambda h, y, c, k: (h ^ 1, y, c, k) if c in (1, 2) else None)
+def z_flip(array):
+    return permute(array, lambda h, y, c, k: (h ^ 1, y, c, k))
 
 
 def params():
@@ -93,8 +94,13 @@
 
 
 def gather_kernel(place, *refs):
-    tokens, cot_own, cot_side, out = refs[:-3], refs[-3], refs[-2], refs[-1]
-    out[...] = multiply(tokens, cot_rows(place, 0, len(tokens), cot_own, cot_side))
+    tokens, cot_own, cot_side, out, cot = refs[:-4], refs[-4], refs[-3], refs[-2], refs[-1]
+
+    @pl.when(pl.program_id(0) == 0)
+    def _():
+        cot[...] = cot_rows(place, 0, len(tokens), cot_own, cot_side)
+
+    out[...] = multiply(tokens, cot[...])
 
 
 def gather_step(place, tokens, cot_own, cot_side, start, size):
@@ -113,12 +119,11 @@
                 pl.BlockSpec((rows, 128), lambda i, place: (cot_side[1], 0)),
             ],
             out_specs=pl.BlockSpec((WIDTH, 256), lambda i, place: (i, 0)),
+            scratch_shapes=[pltpu.VMEM((len(tokens) * share, 256), jnp.bfloat16)],
         ),
         out_shape=jax.ShapeDtypeStruct((size, 256), jnp.float32),
         compiler_params=params(),
-        cost_estimate=pl.CostEstimate(
-            flops=2 * size * 960 * 256, bytes_accessed=size * 2944, transcendentals=0
-        ),
+        cost_estimate=COST,
         name="gather_step",
     )(place, *[array for array, _ in tokens], cot_own, cot_side[0])
 
@@ -181,9 +186,7 @@
         ],
         input_output_aliases={8: 0, 9: 2, 10: 3} if buffers else {},
         compiler_params=params(),
-        cost_estimate=pl.CostEstimate(
-            flops=2 * size * 320 * 256, bytes_accessed=size * 2688, transcendentals=0
-        ),
+        cost_estimate=COST,
         name="momentum_step",
     )(place, first, second, cot_own, cot_side[0], early, prior_own, prior_side, *buffers)
 
@@ -208,14 +211,40 @@
     return more, fewer
 
 
-def vote_kernel(core, words_own, words_other, w_own, w_other, out):
+def choose_kernel(inner, own, returned, out):
+    out[...] = jnp.where(inner[0] == 1, own[...], returned[...])
+
+
+def choose_step(inner, own, returned, start):
+    skip = start // WIDTH
+    there = pl.BlockSpec((WIDTH, 128), lambda i, inner: (i + skip, 0))
+    return pl.pallas_call(
+        choose_kernel,
+        grid_spec=pltpu.PrefetchScalarGridSpec(
+            num_scalar_prefetch=1,
+            grid=(returned.shape[0] // WIDTH,),
+            in_specs=[there, pl.BlockSpec((WIDTH, 128), lambda i, inner: (i, 0))],
+            out_specs=there,
+        ),
+        out_shape=jax.ShapeDtypeStruct(own.shape, own.dtype),
+        input_output_aliases={1: 0},
+        compiler_params=params(),
+        cost_estimate=COST,
+        name="choose_step",
+    )(inner, own, returned)
+
+
+def vote_kernel(core, *refs):
+    words_own, words_other, (w_own, w_other, out) = refs[:4], refs[4:8], refs[8:]
     is_low = core[0] == 0
     step = WIDTH // 32
     for block in range(out.shape[0] // WIDTH):
         rows = slice(block * WIDTH, (block + 1) * WIDTH)
         updated = []
         for words, weights in ((words_own, w_own), (words_other, w_other)):
-            more, fewer = majority([words[i, block * step : (block + 1) * step] for i in range(8)])
+            more, fewer = majority(
+                [ref[i, block * step : (block + 1) * step] for ref in words for i in range(2)]
+            )
             direction = jnp.concatenate(
                 [((more >> bit) & 1) - ((fewer >> bit) & 1) for bit in range(32)], 0
             ).astype(jnp.float32)
@@ -228,52 +257,85 @@
 
 def vote_step(core, words_own, words_other, w_own, w_other):
     features = w_own.shape[0]
-    size = 2 * WIDTH
-    word_spec = pl.BlockSpec((8, size // 32, 128), lambda i, core: (0, i, 0))
+    size = WIDTH
+    word_spec = pl.BlockSpec((2, size // 32, 128), lambda i, core: (0, i, 0))
     weight_spec = pl.BlockSpec((size, 128), lambda i, core: (i, 0))
     return pl.pallas_call(
         vote_kernel,
         grid_spec=pltpu.PrefetchScalarGridSpec(
             num_scalar_prefetch=1,
             grid=(features // size,),
-            in_specs=[word_spec, word_spec, weight_spec, weight_spec],
+            in_specs=[word_spec] * 8 + [weight_spec] * 2,
             out_specs=pl.BlockSpec((size, 256), lambda i, core: (i, 0)),
         ),
         out_shape=jax.ShapeDtypeStruct((features, 256), jnp.bfloat16),
         compiler_params=params(),
-        cost_estimate=pl.CostEstimate(flops=features * 256 * 8, bytes_accessed=features * 1280, transcendentals=0),
+        cost_estimate=COST,
         name="vote_step",
-    )(core, words_own, words_other, w_own, w_other)
-
-
-def input_kernel(cot, w_own, w_rest, ours, theirs):
-    weights = jnp.concatenate([w_own[...], w_rest[...]], 1)
-    total = lax.dot_general(
-        cot[...], weights, (((1,), (1,)), ((), ())), preferred_element_type=jnp.float32
-    ).astype(jnp.bfloat16)
+    )(core, *words_own, *words_other, w_own, w_other)
+
+
+def input_kernel(place, cot, w_own, here, following, before, far_low, far_high, ours, theirs):
     rows = ours.shape[0]
-    ours[...] = total[:rows]
-    theirs[...] = total[rows:]
-
-
-def input_step(cot, w_own, w_rest):
+
+    def product(w_rest):
+        weights = jnp.concatenate([w_own[...], w_rest], 1)
+        total = lax.dot_general(
+            cot[...], weights, (((1,), (1,)), ((), ())), preferred_element_type=jnp.float32
+        ).astype(jnp.bfloat16)
+        ours[...] = total[:rows]
+        theirs[...] = total[rows:]
+
+    i = pl.program_id(0)
+    for at, ref in enumerate((here, following, before)):
+        pl.when(i == at)(lambda ref=ref: product(ref[...]))
+    pl.when(i == 3)(lambda: product(jnp.concatenate([far_low[...], far_high[...]], 0)))
+
+
+def input_step(place, cot, w_own, w_rest):
     rows, depth = cot.shape
     features = w_own.shape[0]
-    width = 2 * WIDTH
-    out_spec = pl.BlockSpec((rows // 2, width), lambda i: (0, i))
+    width = features // YS
+    out_spec = pl.BlockSpec((rows // 2, width), lambda i, place: (0, place[i]))
     return pl.pallas_call(
         input_kernel,
-        grid=(features // width,),
-        in_specs=[pl.BlockSpec((rows, depth), lambda i: (0, 0))]
-        + [pl.BlockSpec((width, w.shape[1]), lambda i: (i, 0)) for w in (w_own, w_rest)],
-        out_specs=[out_spec] * 2,
+        grid_spec=pltpu.PrefetchScalarGridSpec(
+            num_scalar_prefetch=1,
+            grid=(YS,),
+            in_specs=[
+                pl.BlockSpec((rows, depth), lambda i, place: (0, 0)),
+                pl.BlockSpec((width, 128), lambda i, place: (place[i], 0)),
+            ]
+            + [pl.BlockSpec(w.shape, lambda i, place: (0, 0)) for w in w_rest],
+            out_specs=[out_spec] * 2,
+        ),
         out_shape=[jax.ShapeDtypeStruct((rows // 2, features), jnp.bfloat16)] * 2,
         compiler_params=params(),
         cost_estimate=pl.CostEstimate(
             flops=2 * rows * depth * features, bytes_accessed=2 * (depth + rows) * features, transcendentals=0
         ),
         name="input_step",
-    )(cot, w_own, w_rest)
+    )(place, cot, w_own, *w_rest)
+
+
+def total_kernel(ours, theirs, mask, out):
+    total = ours[...].astype(jnp.float32) + theirs[...].astype(jnp.float32)
+    out[...] = (total * mask[...]).astype(jnp.bfloat16)
+
+
+def total_step(ours, theirs, mask):
+    rows, features = ours.shape
+    spec = pl.BlockSpec((rows, features // 2), lambda i: (0, i))
+    return pl.pallas_call(
+        total_kernel,
+        grid=(features // (features // 2),),
+        in_specs=[spec, spec, pl.BlockSpec((rows, 1), lambda i: (0, 0))],
+        out_specs=spec,
+        out_shape=jax.ShapeDtypeStruct(ours.shape, jnp.bfloat16),
+        compiler_params=params(),
+        cost_estimate=COST,
+        name="total_step",
+    )(ours, theirs, mask)
 
 
 def after(arrays, *others):
@@ -298,81 +360,75 @@
         ]
     ).astype(jnp.int32)
 
-    w_part = lax.dynamic_slice(w_key, (y * quarter, 0), (quarter, 128))
-    w_rest = [
-        in_pair(w_part),
-        out_of_pair(w_part),
-        along_z(w_part[: quarter // 2], 2),
-        along_z(w_part[quarter // 2 :], -2),
+    tokens = jnp.where(row_mask[:, None] != 0, tokens_in, jnp.zeros_like(tokens_in))
+    tokens, w_first = lax.optimization_barrier((tokens, w_key))
+    w_part = lax.dynamic_slice(w_first, (y * quarter, 0), (quarter, 128))
+    near, side = across(tokens), inward(tokens)
+    w_here = jnp.concatenate([in_pair(w_part), out_of_pair(w_part), opposite_heads(w_part)], 1)
+    w_next, w_before = along_y(w_here, 1), along_y(w_here, -1)
+    cot_pieces = [
+        lax.dynamic_slice(key_cot, ((chip ^ step) * CORES * share, 0), (CORES * share, 128))
+        for step in (0, 1, 3, 2)
     ]
-    tokens = jnp.where(row_mask[:, None] != 0, tokens_in, jnp.zeros_like(tokens_in))
-    tokens, w_rest = lax.optimization_barrier((tokens, w_rest))
-    w_rest = lax.all_gather(
-        jnp.concatenate([w_rest[0], w_rest[1], jnp.concatenate(w_rest[2:], 0)], 1),
-        "dp",
-        axis=0,
-        tiled=True,
-        axis_index_groups=[[h * YS + y for y in range(YS)] for h in range(HI)],
-    )
-
-    near, side, own_swapped = across(tokens), inward(tokens), core_swap(tokens)
-    cot_pieces = []
-    for step in (0, 1, 3, 2):
-        rows = lax.dynamic_slice(key_cot, ((chip ^ step) * CORES * share, 0), (CORES * share, 128))
-        if step:
-            rows = permute(rows, lambda h, y, c, k, step=step: (h, y, c ^ step, k))
-        cot_pieces.append(rows)
-    lend = jnp.concatenate([prior[:cut], key_cot], 0)
-    near, side, own_swapped, cot_pieces, lend = lax.optimization_barrier(
-        (near, side, own_swapped, cot_pieces, lend)
+    near, side, w_next, w_before, key_cot, cot_pieces, lend = lax.optimization_barrier(
+        (near, side, w_next, w_before, key_cot, cot_pieces, [prior[:cut], prior[cut:]])
     )
 
     far = across(side[:, :cut])
-    lent = inward(lend)
-    near_swapped, side_swapped, w_other = core_swap(near), core_swap(side), core_swap(w_key)
-    far, lent, near_swapped, side_swapped, w_other = lax.optimization_barrier(
-        (far, lent, near_swapped, side_swapped, w_other)
+    cot_side = inward(key_cot)
+    lent = inward(lend[0])
+    own_swapped, near_swapped, side_swapped = core_swap(tokens), core_swap(near), core_swap(side)
+    cot_pieces, own_swapped, near_swapped, side_swapped = lax.optimization_barrier(
+        (cot_pieces, own_swapped, near_swapped, side_swapped)
+    )
+    for i, step in ((1, 1), (2, 3), (3, 2)):
+        cot_pieces[i] = permute(cot_pieces[i], lambda h, y, c, k, step=step: (h, y, c ^ step, k))
+    w_far = [w_next[: quarter // 2], w_before[quarter // 2 :]]
+    arrays = (tokens, own_swapped, side, side_swapped, near, near_swapped)
+
+    def early(start, size):
+        return gather_step(place, [(array, start) for array in arrays], key_cot, (cot_side, 0), start, size)
+
+    summed = [early(0, cut), early(cut, features - cut)]
+    far, lent, summed, cot_pieces, w_far, side = lax.optimization_barrier(
+        (far, lent, summed, cot_pieces, w_far, side)
     )
 
     far_late = across(side[:, cut:])
-    lent_late = inward(prior[cut:])
-    cot_side = (lent, cut // key_cot.shape[0])
-    arrays = (tokens, own_swapped, side, side_swapped, near, near_swapped)
-
-    def early(start):
-        return gather_step(place, [(array, start) for array in arrays], key_cot, cot_side, start, cut)
-
+    lent_late = inward(lend[1])
     new_own, new_side, words, side_words = momentum_step(
-        place, far, core_swap(far), key_cot, cot_side, early(0), prior, lent, 0, []
-    )
-    returned = [outward(new_side)]
-    summed, far_late, lent_late, new_own, words, side_words, cot_pieces = lax.optimization_barrier(
-        (early(cut), far_late, lent_late, new_own, words, side_words, cot_pieces)
-    )
-
-    new_own, new_side, words, side_words = momentum_step(
-        place, far_late, core_swap(far_late), key_cot, cot_side, summed, prior, lent_late, cut,
-        [new_own, words, side_words],
-    )
-    words, cot_pieces = lax.optimization_barrier((words, cot_pieces))
-    words_flip = inner_flip(words)
-    side_here, side_flip = outward(side_words), outward(side_words, 1)
+        place, far, core_swap(far), key_cot, (cot_side, 0), summed[0], prior, lent, 0, []
+    )
+    returned = outward(new_side)
+    w_far = [along_y(w_far[0], 1), along_y(w_far[1], -1)]
+    w_other = core_swap(w_key)
     cot_mine = jnp.concatenate(cot_pieces, 1)
     theirs = lax.dynamic_slice(cot_mine, ((1 - core) * share, 0), (share, 512))
     ours = lax.dynamic_slice(cot_mine, (core * share, 0), (share, 512))
-    ours, theirs = input_step(jnp.concatenate([ours, theirs], 0), w_key, w_rest)
-    words_flip, side_here, side_flip, returned[0], new_side, ours, theirs = lax.optimization_barrier(
-        (words_flip, side_here, side_flip, returned[0], new_side, ours, theirs)
-    )
-
-    pair = jnp.where(inner, jnp.stack([words, words_flip]), jnp.stack([side_here, side_flip]))
-    votes = jnp.concatenate([pair, along_y(pair, 1), along_y(pair, -1), along_y(pair, 2)], 0)
-    returned.append(outward(new_side))
-    total = ours.astype(jnp.float32) + core_swap(theirs).astype(jnp.float32)
-    input_grad = (total * row_mask.astype(jnp.float32)[:, None]).astype(jnp.bfloat16)
-    new_momentum = jnp.where(inner, new_own, jnp.concatenate(returned, 0))[None]
-    votes_other, new_momentum, input_grad = after((core_swap(votes), new_momentum, input_grad))
+    cot_mine = jnp.concatenate([ours, theirs], 0)
+    far_late, lent_late, returned, new_own, words, side_words, cot_mine, w_other = lax.optimization_barrier(
+        (far_late, lent_late, returned, new_own, words, side_words, cot_mine, w_other)
+    )
+
+    new_own, new_side, words, side_words = momentum_step(
+        place, far_late, core_swap(far_late), key_cot, (cot_side, 0), summed[1], prior, lent_late, cut,
+        [new_own, words, side_words],
+    )
+    is_inner = inner.astype(jnp.int32)[None]
+    words, side_words, cot_mine = lax.optimization_barrier((words, side_words, cot_mine))
+    words = jnp.where(inner, words, outward(side_words))
+    pair = jnp.stack([words, z_flip(words)])
+    quarters = jnp.stack([y, (y + 1) % YS, (y + 3) % YS, (y + 2) % YS]).astype(jnp.int32)
+    ours, theirs = input_step(quarters, cot_mine, w_key, [w_here, w_next, w_before, *w_far])
+    pair, new_side, ours, theirs = lax.optimization_barrier((pair, new_side, ours, theirs))
+
+    votes = [pair, along_y(pair, 1), along_y(pair, -1), along_y(pair, 2)]
+    returned_late = outward(new_side)
+    input_grad = total_step(ours, core_swap(theirs), row_mask.astype(jnp.float32)[:, None])
+    new_own = choose_step(is_inner, new_own, returned, 0)
+    votes_other = [core_swap(piece) for piece in votes]
     rollout_weight = vote_step(core[None], votes, votes_other, w_key, w_other)[None]
+    new_momentum = choose_step(is_inner, new_own, returned_late, cut)[None]
     return (input_grad, new_momentum, rollout_weight)
 
 

time: 192 us -> 175 us (0.911)
  waiting for transfers between devices: 73.4 us -> 52.1 us
  Pallas kernels: 25.7 us -> 39.8 us
  between operations: 14.3 us -> 1 us
  other arithmetic: 10.5 us -> 2.43 us
  starting transfers between devices: 57 us -> 63.1 us
  local copies, waits for them, and re-layouts: 10.7 us -> 15.8 us
    ppermute x29 -> x35, waiting for transfers between devices: 73.3 us -> 52.1 us  [permute(): return lax.ppermute(array, AXES, pairs)]
    pallas_call x1 -> x4, Pallas kernels: 4.69 us -> 13.2 us  [the longest x1 6.65 us: input_step(): pl.pallas_call(input_kernel, grid_spec=pltpu.PrefetchScalarGridSpec(num_s...]
    ppermute x29 -> x35, starting transfers between devices: 57 us -> 63.1 us  [permute(): return lax.ppermute(array, AXES, pairs)]
    slice x2 -> x5, local copies, waits for them, and re-layouts: 1.95 us -> 6.48 us  [the longest x2 3.83 us: per_device(): w_far = [w_next[:quarter // 2], w_before[quarter // 2:]]]
    convert_element_type x1 -> x0, other arithmetic: 3.34 us -> none  [per_device(): (total * row_mask.astype(jnp.float32)[:, None]).astype(jnp.bfloat16)]
    broadcast_in_dim x1 -> x0, other arithmetic: 2.61 us -> none  [per_device(): new_momentum = jnp.where(inner, new_own, jnp.concatenate(returned, 0))[None]]
    pallas_call x1, Pallas kernels: 3.25 us -> 5.73 us  [vote_step(): pl.pallas_call(vote_kernel, grid_spec=pltpu.PrefetchScalarGridSpec(num_sc...]
    pallas_call x2, Pallas kernels: 7.7 us -> 10 us  [momentum_step(): pl.pallas_call(momentum_kernel, grid_spec=pltpu.PrefetchScalarGridSpec(nu...]
  transfers between devices with their start and end apart: 30 -> 35, of which waited for: 11 -> 12; matrix products, arithmetic and copies ran while one was open for 7% -> 7% of each run, Pallas kernels for 12% -> 22%
where the time goes in v3:
time: 175 us; the launch traced here: 174 us
  starting transfers between devices  63.1 us (36%)
  waiting for transfers between devices  52.1 us (30%)
  Pallas kernels  39.8 us (23%)
  local copies, waits for them, and re-layouts  15.8 us (9%)
  other arithmetic  2.43 us (1%)
    ppermute x35, starting transfers between devices, permute(): return lax.ppermute(array, AXES, pairs)  63.1 us
    ppermute x35, waiting for transfers between devices, permute(): return lax.ppermute(array, AXES, pairs)  52.1 us
    pallas_call x2, Pallas kernels, gather_step(): pl.pallas_call(gather_kernel, grid_spec=pltpu.PrefetchScalarGridSpec(num_...  10.9 us
    pallas_call x2, Pallas kernels, momentum_step(): pl.pallas_call(momentum_kernel, grid_spec=pltpu.PrefetchScalarGridSpec(nu...  10 us
    pallas_call x1, Pallas kernels, input_step(): pl.pallas_call(input_kernel, grid_spec=pltpu.PrefetchScalarGridSpec(num_s...  6.65 us
    pallas_call x1, Pallas kernels, vote_step(): pl.pallas_call(vote_kernel, grid_spec=pltpu.PrefetchScalarGridSpec(num_sc...  5.73 us
    pallas_call x2, Pallas kernels, choose_step(): pl.pallas_call(choose_kernel, grid_spec=pltpu.PrefetchScalarGridSpec(num_...  4.88 us
    unnamed x39, local copies, waits for them, and re-layouts  4.51 us
  transfers between devices with their start and end apart: 35, of which 12 were waited for; matrix products, arithmetic and copies ran while one was open for 7% of the time, Pallas kernels for 22%

profile of v3, /device:TPU:1, one launch (start us, length us, event | category | flops | bytes accessed | tf_op | source)
XLA Modules:
  0.0 174.3 jit_solution(15409941545230301154)
XLA Ops:
  0.6 0.7 broadcast_compare_fusion
  1.3 1.6 broadcast_select_fusion.refs_0_
  3.0 1.1 constant_dynamic-slice_fusion.6
  4.1 2.6 %collective-permute-start.2 = (bf16[1280,128]{1,0:T(8,128)(2,1)S(1)}, bf16[1280,128]{1,0:T(8,128)(2,1)S(1)}, u32[]{:S(2)}, u32[]{:S(2)}) collective-permute-start(bf16[1280,128]{1,0:T(8,128)(2,1)S(1)} %constant_dynamic-slice_fusion.6), channel_id=1, source_target_pairs={{0,8},{4,12},{8,0},{12,4},{16,24},{20,28},{24,16},{28,20},{32,40},... | collective-permute-start | bytes 983048 | tf_op jit(solution)/shard_map/ppermute | solution.py:32
  6.6 4.7 %collective-permute-start.3 = (bf16[1280,128]{1,0:T(8,128)(2,1)S(1)}, bf16[1280,128]{1,0:T(8,128)(2,1)S(1)}, u32[]{:S(2)}, u32[]{:S(2)}) collective-permute-start(bf16[1280,128]{1,0:T(8,128)(2,1)S(1)} %constant_dynamic-slice_fusion.6), channel_id=1, source_target_pairs={{0,152},{4,156},{8,16},{12,20},{16,8},{20,12},{24,128},{28,132},{3... | collective-permute-start | bytes 983048 | tf_op jit(solution)/shard_map/ppermute | solution.py:32
  11.3 1.2 collective-permute-start.4
  12.5 1.9 %collective-permute-start = (bf16[160,5120]{1,0:T(8,128)(2,1)S(1)}, bf16[160,5120]{1,0:T(8,128)(2,1)}, u32[]{:S(2)}, u32[]{:S(2)}) collective-permute-start(bf16[160,5120]{1,0:T(8,128)(2,1)S(1)} %broadcast_select_fusion.refs_0_), channel_id=1, source_target_pairs={{8,16},{12,20},{16,8},{20,12},{40,48},{44,52},{48,40},{52,44},{72,... | collective-permute-start | bytes 4915208 | tf_op jit(solution)/shard_map/ppermute | solution.py:32
  14.3 2.8 %collective-permute-start.1 = (bf16[160,5120]{1,0:T(8,128)(2,1)S(1)}, bf16[160,5120]{1,0:T(8,128)(2,1)S(1)}, u32[]{:S(2)}, u32[]{:S(2)}) collective-permute-start(bf16[160,5120]{1,0:T(8,128)(2,1)S(1)} %broadcast_select_fusion.refs_0_), channel_id=1, source_target_pairs={{0,8},{4,12},{24,16},{28,20},{32,40},{36,44},{56,48},{60,52},{64,7... | collective-permute-start | bytes 4915208 | tf_op jit(solution)/shard_map/ppermute | solution.py:32
  17.1 1.9 %collective-permute-start.9 = (bf16[160,5120]{1,0:T(8,128)(2,1)S(1)}, bf16[160,5120]{1,0:T(8,128)(2,1)}, u32[]{:S(2)}, u32[]{:S(2)}) collective-permute-start(bf16[160,5120]{1,0:T(8,128)(2,1)S(1)} %broadcast_select_fusion.refs_0_), channel_id=1, source_target_pairs={{0,4},{4,0},{8,12},{12,8},{16,20},{20,16},{24,28},{28,24},{32,36},... | collective-permute-start | bytes 4915208 | tf_op jit(solution)/shard_map/ppermute | solution.py:32
  19.0 0.8 constant_dynamic-update-slice_fusion.2
  19.8 4.8 %collective-permute-done.3 = bf16[1280,128]{1,0:T(8,128)(2,1)S(1)} collective-permute-done((bf16[1280,128]{1,0:T(8,128)(2,1)S(1)}, bf16[1280,128]{1,0:T(8,128)(2,1)S(1)}, u32[]{:S(2)}, u32[]{:S(2)}) %collective-permute-start.3) | collective-permute-done | bytes 327712 | tf_op jit(solution)/shard_map/ppermute | solution.py:32
  24.6 0.8 constant_dynamic-update-slice_fusion.1
  25.4 6.3 %collective-permute-done.4 = bf16[1280,128]{1,0:T(8,128)(2,1)S(1)} collective-permute-done((bf16[1280,128]{1,0:T(8,128)(2,1)S(1)}, bf16[1280,128]{1,0:T(8,128)(2,1)S(1)}, u32[]{:S(2)}, u32[]{:S(2)}) %collective-permute-start.4) | collective-permute-done | bytes 327712 | tf_op jit(solution)/shard_map/ppermute | solution.py:32
  31.7 0.8 constant_dynamic-update-slice_fusion.here
  32.5 2.7 %collective-permute-start.5 = (bf16[1280,384]{1,0:T(8,128)(2,1)}, bf16[1280,384]{1,0:T(8,128)(2,1)}, u32[]{:S(2)}, u32[]{:S(2)}) collective-permute-start(bf16[1280,384]{1,0:T(8,128)(2,1)} %constant_dynamic-update-slice_fusion.here), channel_id=1, source_target_pairs={{0,96},{4,100},{8,104},{12,108},{16,112},{20,116},{24,120},{28,124... | collective-permute-start | bytes 2949128 | tf_op jit(solution)/shard_map/ppermute | solution.py:32
  35.1 0.9 slice_bitcast_fusion
  36.1 0.8 slice_bitcast_fusion.1
  36.9 1.7 constant_dynamic-slice_fusion.2
  38.6 16.2 %collective-permute-done.5.following = bf16[1280,384]{1,0:T(8,128)(2,1)} collective-permute-done((bf16[1280,384]{1,0:T(8,128)(2,1)}, bf16[1280,384]{1,0:T(8,128)(2,1)}, u32[]{:S(2)}, u32[]{:S(2)}) %collective-permute-start.5) | collective-permute-done | bytes 983072 | tf_op jit(solution)/shard_map/ppermute | solution.py:32
  54.8 3.1 %collective-permute-done.6.before = bf16[1280,384]{1,0:T(8,128)(2,1)} collective-permute-done((bf16[1280,384]{1,0:T(8,128)(2,1)}, bf16[1280,384]{1,0:T(8,128)(2,1)}, u32[]{:S(2)}, u32[]{:S(2)}) %collective-permute-start.6) | collective-permute-done | bytes 983072 | tf_op jit(solution)/shard_map/ppermute | solution.py:32
  58.1 2.7 %collective-permute-start.10 = (bf16[160,5120]{1,0:T(8,128)(2,1)}, bf16[160,5120]{1,0:T(8,128)(2,1)}, u32[]{:S(2)}, u32[]{:S(2)}) collective-permute-start(bf16[160,5120]{1,0:T(8,128)(2,1)} %collective-permute-done.refs_4_), channel_id=1, source_target_pairs={{0,4},{4,0},{8,12},{12,8},{16,20},{20,16},{24,28},{28,24},{32,36},... | collective-permute-start | bytes 4915208 | tf_op jit(solution)/shard_map/ppermute | solution.py:32
  60.9 4.7 %collective-permute-start.12 = (bf16[1280,128]{1,0:T(8,128)(2,1)}, bf16[1280,128]{1,0:T(8,128)(2,1)}, u32[]{:S(2)}, u32[]{:S(2)}) collective-permute-start(bf16[1280,128]{1,0:T(8,128)(2,1)} %refs_2_.1), channel_id=1, source_target_pairs={{0,8},{4,12},{24,16},{28,20},{32,40},{36,44},{56,48},{60,52},{64,7... | collective-permute-start | bytes 983048 | tf_op jit(solution)/shard_map/ppermute | solution.py:32
  65.7 0.9 slice.28
  66.6 1.5 collective-permute-start.7
  68.1 2.5 %collective-permute-start.8 = (bf16[2048,128]{1,0:T(8,128)(2,1)}, bf16[2048,128]{1,0:T(8,128)(2,1)}, u32[]{:S(2)}, u32[]{:S(2)}) collective-permute-start(bf16[2048,128]{1,0:T(8,128)(2,1)} %slice_bitcast_fusion.1), channel_id=1, source_target_pairs={{0,8},{4,12},{24,16},{28,20},{32,40},{36,44},{56,48},{60,52},{64,7... | collective-permute-start | bytes 1572872 | tf_op jit(solution)/shard_map/ppermute | solution.py:32
  70.7 1.9 %slice.29 = bf16[640,384]{1,0:T(8,128)(2,1)} slice(bf16[1280,384]{1,0:T(8,128)(2,1)} %collective-permute-done.5.following), slice={[0:640], [0:384]} | slice | bytes 983040 | tf_op jit(solution)/shard_map/slice | solution.py:386
  72.6 1.9 %slice.30 = bf16[640,384]{1,0:T(8,128)(2,1)} slice(bf16[1280,384]{1,0:T(8,128)(2,1)} %collective-permute-done.6.before), slice={[640:1280], [0:384]} | slice | bytes 983040 | tf_op jit(solution)/shard_map/slice | solution.py:386
  74.6 1.7 collective-permute-start.14
  76.3 0.9 collective-permute-start.15
  77.2 6.3 %gather_step.3.refs_4_ = f32[3072,256]{1,0:T(8,128)} custom-call(s32[8]{0:T(128)S(1)} %stack.59.place, bf16[160,5120]{1,0:T(8,128)(2,1)S(1)} %broadcast_select_fusion.refs_0_, bf16[160,5120]{1,0:T(8,128)(2,1)} %collective-permute-done.9.refs_1_, bf16[160,5120]{1,0:T(8,128)(2,1)S(1)} %collective-permute-done.1.refs_2_, ...), custom_call_target="tpu_custom_call" | custom-call | flops 2000000000 | bytes 10000000 | tf_op jit(solution)/shard_map/gather_step/pallas_call | solution.py:108
  83.5 4.6 %gather_step.2.refs_4_ = f32[2048,256]{1,0:T(8,128)} custom-call(s32[8]{0:T(128)S(1)} %stack.59.place, bf16[160,5120]{1,0:T(8,128)(2,1)S(1)} %broadcast_select_fusion.refs_0_, bf16[160,5120]{1,0:T(8,128)(2,1)} %collective-permute-done.9.refs_1_, bf16[160,5120]{1,0:T(8,128)(2,1)S(1)} %collective-permute-done.1.refs_2_, ...), custom_call_target="tpu_custom_call" | custom-call | flops 2000000000 | bytes 10000000 | tf_op jit(solution)/shard_map/gather_step/pallas_call | solution.py:108
  88.2 0.7 collective-permute-done.14
  88.9 2.2 %collective-permute-start.18 = (bf16[160,2048]{1,0:T(8,128)(2,1)}, bf16[160,2048]{1,0:T(8,128)(2,1)}, u32[]{:S(2)}, u32[]{:S(2)}) collective-permute-start(bf16[160,2048]{1,0:T(8,128)(2,1)} %collective-permute-done.7.refs_0_), channel_id=1, source_target_pairs={{0,4},{4,0},{8,12},{12,8},{16,20},{20,16},{24,28},{28,24},{32,36},... | collective-permute-start | bytes 1966088 | tf_op jit(solution)/shard_map/ppermute | solution.py:32
  91.2 1.0 slice.31
  92.2 0.7 collective-permute-start.16
  93.0 4.9 %collective-permute-start.17 = (bf16[3072,128]{1,0:T(8,128)(2,1)}, bf16[3072,128]{1,0:T(8,128)(2,1)S(1)}, u32[]{:S(2)}, u32[]{:S(2)}) collective-permute-start(bf16[3072,128]{1,0:T(8,128)(2,1)} %slice_bitcast_fusion), channel_id=1, source_target_pairs={{0,8},{4,12},{24,16},{28,20},{32,40},{36,44},{56,48},{60,52},{64,7... | collective-permute-start | bytes 2359304 | tf_op jit(solution)/shard_map/ppermute | solution.py:32
  97.9 4.4 %momentum_step.2 = (bf16[5120,128]{1,0:T(8,128)(2,1)}, bf16[2048,128]{1,0:T(8,128)(2,1)S(1)}, s32[160,128]{1,0:T(8,128)S(1)}, s32[160,128]{1,0:T(8,128)S(1)}) custom-call(s32[8]{0:T(128)S(1)} %stack.59.place, bf16[160,2048]{1,0:T(8,128)(2,1)} %collective-permute-done.7.refs_0_, bf16[160,2048]{1,0:T(8,128)(2,1)} %collective-permute-done.18.refs_1_, ...), custom_call_target="tpu_custom_call" | custom-call | flops 2000000000 | bytes 10000000 | tf_op jit(solution)/shard_map/momentum_step/pallas_call | solution.py:159
  102.3 1.5 collective-permute-start.19
  104.0 10.2 %collective-permute-done.17.refs_6_ = bf16[3072,128]{1,0:T(8,128)(2,1)S(1)} collective-permute-done((bf16[3072,128]{1,0:T(8,128)(2,1)}, bf16[3072,128]{1,0:T(8,128)(2,1)S(1)}, u32[]{:S(2)}, u32[]{:S(2)}) %collective-permute-start.17) | collective-permute-done | bytes 786464 | tf_op jit(solution)/shard_map/ppermute | solution.py:32
  114.2 0.9 copy-done.4
  115.1 1.5 collective-permute-done.19.returned
  116.6 0.8 copy-done.6
  117.4 2.0 %collective-permute-start.21 = (bf16[160,3072]{1,0:T(8,128)(2,1)S(1)}, bf16[160,3072]{1,0:T(8,128)(2,1)}, u32[]{:S(2)}, u32[]{:S(2)}) collective-permute-start(bf16[160,3072]{1,0:T(8,128)(2,1)S(1)} %collective-permute-done.16.refs_0_), channel_id=1, source_target_pairs={{0,4},{4,0},{8,12},{12,8},{16,20},{20,16},{24,28},{28,24},{32,36},... | collective-permute-start | bytes 2949128 | tf_op jit(solution)/shard_map/ppermute | solution.py:32
  119.4 1.9 %collective-permute-start.24 = (bf16[640,384]{1,0:T(8,128)(2,1)}, bf16[640,384]{1,0:T(8,128)(2,1)S(1)}, u32[]{:S(2)}, u32[]{:S(2)}) collective-permute-start(bf16[640,384]{1,0:T(8,128)(2,1)} %slice.29), channel_id=1, source_target_pairs={{0,96},{4,100},{8,104},{12,108},{16,112},{20,116},{24,120},{28,124... | collective-permute-start | bytes 1474568 | tf_op jit(solution)/shard_map/ppermute | solution.py:32
  121.2 0.4 collective-permute-done.21.refs_1_
  121.7 1.1 copy-done.5
  122.8 5.6 %momentum_step.3 = (bf16[5120,128]{1,0:T(8,128)(2,1)}, bf16[3072,128]{1,0:T(8,128)(2,1)}, s32[160,128]{1,0:T(8,128)S(1)}, s32[160,128]{1,0:T(8,128)S(1)}) custom-call(s32[8]{0:T(128)S(1)} %stack.59.place, bf16[160,3072]{1,0:T(8,128)(2,1)S(1)} %collective-permute-done.16.refs_0_, ...), custom_call_target="tpu_custom_call", output_to_operand_aliasing={{0}: (8, {}), {2}: (9, {}), {3}: (10, {})} | custom-call | flops 2000000000 | bytes 10000000 | tf_op jit(solution)/shard_map/momentum_step/pallas_call | solution.py:159
  128.4 1.3 collective-permute-start.22
  129.8 4.2 %collective-permute-done.22 = s32[160,128]{1,0:T(8,128)S(1)} collective-permute-done((s32[160,128]{1,0:T(8,128)S(1)}, s32[160,128]{1,0:T(8,128)S(1)}, u32[]{:S(2)}, u32[]{:S(2)}) %collective-permute-start.22) | collective-permute-done | bytes 81952 | tf_op jit(solution)/shard_map/ppermute | solution.py:32
  134.0 3.8 %collective-permute-start.23 = (s32[160,128]{1,0:T(8,128)S(1)}, s32[160,128]{1,0:T(8,128)S(1)}, u32[]{:S(2)}, u32[]{:S(2)}) collective-permute-start(s32[160,128]{1,0:T(8,128)S(1)} %broadcast_select_fusion.1), channel_id=1, source_target_pairs={{0,128},{4,132},{8,136},{12,140},{16,144},{20,148},{24,152},{28,15... | collective-permute-start | bytes 245768 | tf_op jit(solution)/shard_map/ppermute | solution.py:32
  137.8 6.6 %input_step.1 = (bf16[160,5120]{1,0:T(8,128)(2,1)}, bf16[160,5120]{1,0:T(8,128)(2,1)}) custom-call(s32[4]{0:T(128)S(1)} %pad_add_fusion.1.place, bf16[320,512]{1,0:T(8,128)(2,1)S(1)} %pad_maximum_fusion.cot, bf16[5120,128]{1,0:T(8,128)(2,1)} %refs_8_.1, bf16[1280,384]{1,0:T(8,128)(2,1)} %constant_dynamic-update-slice_fusion.here, ...), custom_call_target="tpu_custom_call" | custom-call | flops 1677721600 | bytes 8519680 | tf_op jit(solution)/shard_map/input_step/pallas_call | solution.py:300
  144.5 1.6 collective-permute-start.26
  146.0 1.3 collective-permute-start.27
  147.3 2.9 %collective-permute-start.28 = (s32[2,160,128]{2,1,0:T(8,128)S(1)}, s32[2,160,128]{2,1,0:T(8,128)S(1)}, u32[]{:S(2)}, u32[]{:S(2)}) collective-permute-start(s32[2,160,128]{2,1,0:T(8,128)S(1)} %pad_add_fusion.refs_0_), channel_id=1, source_target_pairs={{0,96},{4,100},{8,104},{12,108},{16,112},{20,116},{24,120},{28,124... | collective-permute-start | bytes 491528 | tf_op jit(solution)/shard_map/ppermute | solution.py:32
  150.2 1.3 collective-permute-start.30
  151.5 2.3 %collective-permute-done.28.refs_1_ = s32[2,160,128]{2,1,0:T(8,128)S(1)} collective-permute-done((s32[2,160,128]{2,1,0:T(8,128)S(1)}, s32[2,160,128]{2,1,0:T(8,128)S(1)}, u32[]{:S(2)}, u32[]{:S(2)}) %collective-permute-start.28) | collective-permute-done | bytes 163872 | tf_op jit(solution)/shard_map/ppermute | solution.py:32
  153.8 4.3 %collective-permute-start.31 = (s32[2,160,128]{2,1,0:T(8,128)S(1)}, s32[2,160,128]{2,1,0:T(8,128)}, u32[]{:S(2)}, u32[]{:S(2)}) collective-permute-start(s32[2,160,128]{2,1,0:T(8,128)S(1)} %pad_add_fusion.refs_0_), channel_id=1, source_target_pairs={{0,4},{4,0},{8,12},{12,8},{16,20},{20,16},{24,28},{28,24},{32,36},... | collective-permute-start | bytes 491528 | tf_op jit(solution)/shard_map/ppermute | solution.py:32
  158.3 2.1 %collective-permute-done.29.refs_2_ = s32[2,160,128]{2,1,0:T(8,128)S(1)} collective-permute-done((s32[2,160,128]{2,1,0:T(8,128)S(1)}, s32[2,160,128]{2,1,0:T(8,128)S(1)}, u32[]{:S(2)}, u32[]{:S(2)}) %collective-permute-start.29) | collective-permute-done | bytes 163872 | tf_op jit(solution)/shard_map/ppermute | solution.py:32
  160.4 1.1 collective-permute-start.32
  161.5 0.5 collective-permute-start.34
  162.1 1.8 %choose_step.2.own = bf16[5120,128]{1,0:T(8,128)(2,1)} custom-call(s32[1]{0:T(128)} %bitcast.18.inner, bf16[5120,128]{1,0:T(8,128)(2,1)} %get-tuple-element.110.own, bf16[2048,128]{1,0:T(8,128)(2,1)S(1)} %copy-done.7), custom_call_target="tpu_custom_call", output_to_operand_aliasing={{}: (1, {})} | custom-call | flops 2000000000 | bytes 10000000 | tf_op jit(solution)/shard_map/choose_step/pallas_call | solution.py:221
  163.9 5.7 %vote_step.1 = bf16[5120,256]{1,0:T(8,128)(2,1)} custom-call(s32[1]{0:T(128)} %bitcast.20.core, s32[2,160,128]{2,1,0:T(8,128)S(1)} %pad_add_fusion.refs_0_, s32[2,160,128]{2,1,0:T(8,128)S(1)} %collective-permute-done.28.refs_1_, s32[2,160,128]{2,1,0:T(8,128)S(1)} %collective-permute-done.29.refs_2_, s32[2,160,128]{2,1,0:T(8,128)} %collective-permute-done.30.refs_3_, ...), custom_call_target="tpu_custom_call" | custom-call | flops 2000000000 | bytes 10000000 | tf_op jit(solution)/shard_map/vote_step/pallas_call | solution.py:263
  169.6 3.1 %choose_step.3 = bf16[5120,128]{1,0:T(8,128)(2,1)} custom-call(s32[1]{0:T(128)} %bitcast.18.inner, bf16[5120,128]{1,0:T(8,128)(2,1)} %choose_step.2.own, bf16[3072,128]{1,0:T(8,128)(2,1)S(1)} %collective-permute-done.27.returned), custom_call_target="tpu_custom_call", output_to_operand_aliasing={{}: (1, {})} | custom-call | flops 2000000000 | bytes 10000000 | tf_op jit(solution)/shard_map/choose_step/pallas_call | solution.py:221
  172.7 1.7 total_step.1
  (74 shorter events, 1.1 us)
Async XLA Ops:
  2.9 32.2 %copy-start = (bf16[1,5120,128]{2,1,0:T(8,128)(2,1)S(1)}, bf16[1,5120,128]{2,1,0:T(8,128)(2,1)}, u32[]{:S(2)}) copy-start(bf16[1,5120,128]{2,1,0:T(8,128)(2,1)} %param.9) | copy-start | bytes 3932164
  4.1 13.1 %collective-permute-start.2 = (bf16[1280,128]{1,0:T(8,128)(2,1)S(1)}, bf16[1280,128]{1,0:T(8,128)(2,1)S(1)}, u32[]{:S(2)}, u32[]{:S(2)}) collective-permute-start(bf16[1280,128]{1,0:T(8,128)(2,1)S(1)} %constant_dynamic-slice_fusion.6), channel_id=1, source_target_pairs={{0,8},{4,12},{8,0},{12,4},{16,24},{20,28},{24,16},{28,20},{32,40},... | collective-permute-start | bytes 983048 | tf_op jit(solution)/shard_map/ppermute | solution.py:32
  6.6 18.0 %collective-permute-start.3 = (bf16[1280,128]{1,0:T(8,128)(2,1)S(1)}, bf16[1280,128]{1,0:T(8,128)(2,1)S(1)}, u32[]{:S(2)}, u32[]{:S(2)}) collective-permute-start(bf16[1280,128]{1,0:T(8,128)(2,1)S(1)} %constant_dynamic-slice_fusion.6), channel_id=1, source_target_pairs={{0,152},{4,156},{8,16},{12,20},{16,8},{20,12},{24,128},{28,132},{3... | collective-permute-start | bytes 983048 | tf_op jit(solution)/shard_map/ppermute | solution.py:32
  11.3 20.4 %collective-permute-start.4 = (bf16[1280,128]{1,0:T(8,128)(2,1)S(1)}, bf16[1280,128]{1,0:T(8,128)(2,1)S(1)}, u32[]{:S(2)}, u32[]{:S(2)}) collective-permute-start(bf16[1280,128]{1,0:T(8,128)(2,1)S(1)} %constant_dynamic-slice_fusion.6), channel_id=1, source_target_pairs={{0,144},{4,148},{8,152},{12,156},{16,128},{20,132},{24,136},{28,14... | collective-permute-start | bytes 983048 | tf_op jit(solution)/shard_map/ppermute | solution.py:32
  12.5 45.4 %collective-permute-start = (bf16[160,5120]{1,0:T(8,128)(2,1)S(1)}, bf16[160,5120]{1,0:T(8,128)(2,1)}, u32[]{:S(2)}, u32[]{:S(2)}) collective-permute-start(bf16[160,5120]{1,0:T(8,128)(2,1)S(1)} %broadcast_select_fusion.refs_0_), channel_id=1, source_target_pairs={{8,16},{12,20},{16,8},{20,12},{40,48},{44,52},{48,40},{52,44},{72,... | collective-permute-start | bytes 4915208 | tf_op jit(solution)/shard_map/ppermute | solution.py:32
  14.3 43.8 %collective-permute-start.1 = (bf16[160,5120]{1,0:T(8,128)(2,1)S(1)}, bf16[160,5120]{1,0:T(8,128)(2,1)S(1)}, u32[]{:S(2)}, u32[]{:S(2)}) collective-permute-start(bf16[160,5120]{1,0:T(8,128)(2,1)S(1)} %broadcast_select_fusion.refs_0_), channel_id=1, source_target_pairs={{0,8},{4,12},{24,16},{28,20},{32,40},{36,44},{56,48},{60,52},{64,7... | collective-permute-start | bytes 4915208 | tf_op jit(solution)/shard_map/ppermute | solution.py:32
  17.1 50.9 %collective-permute-start.9 = (bf16[160,5120]{1,0:T(8,128)(2,1)S(1)}, bf16[160,5120]{1,0:T(8,128)(2,1)}, u32[]{:S(2)}, u32[]{:S(2)}) collective-permute-start(bf16[160,5120]{1,0:T(8,128)(2,1)S(1)} %broadcast_select_fusion.refs_0_), channel_id=1, source_target_pairs={{0,4},{4,0},{8,12},{12,8},{16,20},{20,16},{24,28},{28,24},{32,36},... | collective-permute-start | bytes 4915208 | tf_op jit(solution)/shard_map/ppermute | solution.py:32
  32.5 22.3 %collective-permute-start.5 = (bf16[1280,384]{1,0:T(8,128)(2,1)}, bf16[1280,384]{1,0:T(8,128)(2,1)}, u32[]{:S(2)}, u32[]{:S(2)}) collective-permute-start(bf16[1280,384]{1,0:T(8,128)(2,1)} %constant_dynamic-update-slice_fusion.here), channel_id=1, source_target_pairs={{0,96},{4,100},{8,104},{12,108},{16,112},{20,116},{24,120},{28,124... | collective-permute-start | bytes 2949128 | tf_op jit(solution)/shard_map/ppermute | solution.py:32
  35.1 22.8 %collective-permute-start.6 = (bf16[1280,384]{1,0:T(8,128)(2,1)}, bf16[1280,384]{1,0:T(8,128)(2,1)}, u32[]{:S(2)}, u32[]{:S(2)}) collective-permute-start(bf16[1280,384]{1,0:T(8,128)(2,1)} %constant_dynamic-update-slice_fusion.here), channel_id=1, source_target_pairs={{0,32},{4,36},{8,40},{12,44},{16,48},{20,52},{24,56},{28,60},{32,6... | collective-permute-start | bytes 2949128 | tf_op jit(solution)/shard_map/ppermute | solution.py:32
  58.1 16.4 %collective-permute-start.10 = (bf16[160,5120]{1,0:T(8,128)(2,1)}, bf16[160,5120]{1,0:T(8,128)(2,1)}, u32[]{:S(2)}, u32[]{:S(2)}) collective-permute-start(bf16[160,5120]{1,0:T(8,128)(2,1)} %collective-permute-done.refs_4_), channel_id=1, source_target_pairs={{0,4},{4,0},{8,12},{12,8},{16,20},{20,16},{24,28},{28,24},{32,36},... | collective-permute-start | bytes 4915208 | tf_op jit(solution)/shard_map/ppermute | solution.py:32
  60.8 13.7 %collective-permute-start.11 = (bf16[160,5120]{1,0:T(8,128)(2,1)S(1)}, bf16[160,5120]{1,0:T(8,128)(2,1)}, u32[]{:S(2)}, u32[]{:S(2)}) collective-permute-start(bf16[160,5120]{1,0:T(8,128)(2,1)S(1)} %collective-permute-done.1.refs_2_), channel_id=1, source_target_pairs={{0,4},{4,0},{8,12},{12,8},{16,20},{20,16},{24,28},{28,24},{32,36},... | collective-permute-start | bytes 4915208 | tf_op jit(solution)/shard_map/ppermute | solution.py:32
  60.9 15.4 %collective-permute-start.12 = (bf16[1280,128]{1,0:T(8,128)(2,1)}, bf16[1280,128]{1,0:T(8,128)(2,1)}, u32[]{:S(2)}, u32[]{:S(2)}) collective-permute-start(bf16[1280,128]{1,0:T(8,128)(2,1)} %refs_2_.1), channel_id=1, source_target_pairs={{0,8},{4,12},{24,16},{28,20},{32,40},{36,44},{56,48},{60,52},{64,7... | collective-permute-start | bytes 983048 | tf_op jit(solution)/shard_map/ppermute | solution.py:32
  66.6 21.6 %collective-permute-start.7 = (bf16[160,2048]{1,0:T(8,128)(2,1)}, bf16[160,2048]{1,0:T(8,128)(2,1)}, u32[]{:S(2)}, u32[]{:S(2)}) collective-permute-start(bf16[160,2048]{1,0:T(8,128)(2,1)} %slice.28), channel_id=1, source_target_pairs={{8,16},{12,20},{16,8},{20,12},{40,48},{44,52},{48,40},{52,44},{72,... | collective-permute-start | bytes 1966088 | tf_op jit(solution)/shard_map/ppermute | solution.py:32
  68.1 20.1 %collective-permute-start.8 = (bf16[2048,128]{1,0:T(8,128)(2,1)}, bf16[2048,128]{1,0:T(8,128)(2,1)}, u32[]{:S(2)}, u32[]{:S(2)}) collective-permute-start(bf16[2048,128]{1,0:T(8,128)(2,1)} %slice_bitcast_fusion.1), channel_id=1, source_target_pairs={{0,8},{4,12},{24,16},{28,20},{32,40},{36,44},{56,48},{60,52},{64,7... | collective-permute-start | bytes 1572872 | tf_op jit(solution)/shard_map/ppermute | solution.py:32
  70.6 3.8 %copy-start.9 = (bf16[320,128]{1,0:T(8,128)(2,1)S(1)}, bf16[320,128]{1,0:T(8,128)(2,1)}, u32[]{:S(2)}) copy-start(bf16[320,128]{1,0:T(8,128)(2,1)} %get-tuple-element.73) | copy-start | bytes 245764
  70.6 6.6 %copy-start.2 = (bf16[1280,128]{1,0:T(8,128)(2,1)S(1)}, bf16[1280,128]{1,0:T(8,128)(2,1)}, u32[]{:S(2)}) copy-start(bf16[1280,128]{1,0:T(8,128)(2,1)} %refs_2_.1) | copy-start | bytes 983044
  74.5 13.7 %collective-permute-start.13 = (bf16[320,128]{1,0:T(8,128)(2,1)S(1)}, bf16[320,128]{1,0:T(8,128)(2,1)S(1)}, u32[]{:S(2)}, u32[]{:S(2)}) collective-permute-start(bf16[320,128]{1,0:T(8,128)(2,1)S(1)} %copy-done.9), channel_id=1, source_target_pairs={{0,8},{4,12},{8,0},{12,4},{16,24},{20,28},{24,16},{28,20},{32,40},... | collective-permute-start | bytes 245768 | tf_op jit(solution)/shard_map/ppermute | solution.py:32
  74.6 14.3 %collective-permute-start.14 = (bf16[320,128]{1,0:T(8,128)(2,1)S(1)}, bf16[320,128]{1,0:T(8,128)(2,1)S(1)}, u32[]{:S(2)}, u32[]{:S(2)}) collective-permute-start(bf16[320,128]{1,0:T(8,128)(2,1)S(1)} %get-tuple-element.74), channel_id=1, source_target_pairs={{0,24},{4,28},{8,16},{12,20},{16,8},{20,12},{24,0},{28,4},{32,56},... | collective-permute-start | bytes 245768 | tf_op jit(solution)/shard_map/ppermute | solution.py:32
  76.3 12.6 %collective-permute-start.15 = (bf16[320,128]{1,0:T(8,128)(2,1)S(1)}, bf16[320,128]{1,0:T(8,128)(2,1)S(1)}, u32[]{:S(2)}, u32[]{:S(2)}) collective-permute-start(bf16[320,128]{1,0:T(8,128)(2,1)S(1)} %get-tuple-element.75), channel_id=1, source_target_pairs={{0,16},{4,20},{8,24},{12,28},{16,0},{20,4},{24,8},{28,12},{32,48},... | collective-permute-start | bytes 245768 | tf_op jit(solution)/shard_map/ppermute | solution.py:32
  88.2 9.7 %copy-start.1 = (bf16[1,5120,128]{2,1,0:T(8,128)(2,1)S(1)}, bf16[1,5120,128]{2,1,0:T(8,128)(2,1)}, u32[]{:S(2)}) copy-start(bf16[1,5120,128]{2,1,0:T(8,128)(2,1)} %param.9) | copy-start | bytes 3932164
  88.2 9.7 %copy-start.3 = (bf16[1280,128]{1,0:T(8,128)(2,1)S(1)}, bf16[1280,128]{1,0:T(8,128)(2,1)}, u32[]{:S(2)}) copy-start(bf16[1280,128]{1,0:T(8,128)(2,1)} %refs_2_.1) | copy-start | bytes 983044
  88.2 4.0 %copy-start.10 = (bf16[320,128]{1,0:T(8,128)(2,1)}, bf16[320,128]{1,0:T(8,128)(2,1)S(1)}, u32[]{:S(2)}) copy-start(bf16[320,128]{1,0:T(8,128)(2,1)S(1)} %collective-permute-done.13) | copy-start | bytes 245764
  88.9 3.3 %copy-start.12 = (bf16[320,128]{1,0:T(8,128)(2,1)}, bf16[320,128]{1,0:T(8,128)(2,1)S(1)}, u32[]{:S(2)}) copy-start(bf16[320,128]{1,0:T(8,128)(2,1)S(1)} %collective-permute-done.14) | copy-start | bytes 245764
  88.9 3.3 %copy-start.14 = (bf16[320,128]{1,0:T(8,128)(2,1)}, bf16[320,128]{1,0:T(8,128)(2,1)S(1)}, u32[]{:S(2)}) copy-start(bf16[320,128]{1,0:T(8,128)(2,1)S(1)} %collective-permute-done.15) | copy-start | bytes 245764
  88.9 9.0 %collective-permute-start.18 = (bf16[160,2048]{1,0:T(8,128)(2,1)}, bf16[160,2048]{1,0:T(8,128)(2,1)}, u32[]{:S(2)}, u32[]{:S(2)}) collective-permute-start(bf16[160,2048]{1,0:T(8,128)(2,1)} %collective-permute-done.7.refs_0_), channel_id=1, source_target_pairs={{0,4},{4,0},{8,12},{12,8},{16,20},{20,16},{24,28},{28,24},{32,36},... | collective-permute-start | bytes 1966088 | tf_op jit(solution)/shard_map/ppermute | solution.py:32
  91.1 12.9 %collective-permute-start.20 = (bf16[5120,128]{1,0:T(8,128)(2,1)}, bf16[5120,128]{1,0:T(8,128)(2,1)}, u32[]{:S(2)}, u32[]{:S(2)}) collective-permute-start(bf16[5120,128]{1,0:T(8,128)(2,1)} %refs_8_.1), channel_id=1, source_target_pairs={{0,4},{4,0},{8,12},{12,8},{16,20},{20,16},{24,28},{28,24},{32,36},... | collective-permute-start | bytes 3932168 | tf_op jit(solution)/shard_map/ppermute | solution.py:32
  92.2 22.8 %collective-permute-start.16 = (bf16[160,3072]{1,0:T(8,128)(2,1)}, bf16[160,3072]{1,0:T(8,128)(2,1)S(1)}, u32[]{:S(2)}, u32[]{:S(2)}) collective-permute-start(bf16[160,3072]{1,0:T(8,128)(2,1)} %slice.31), channel_id=1, source_target_pairs={{8,16},{12,20},{16,8},{20,12},{40,48},{44,52},{48,40},{52,44},{72,... | collective-permute-start | bytes 2949128 | tf_op jit(solution)/shard_map/ppermute | solution.py:32
  93.0 21.2 %collective-permute-start.17 = (bf16[3072,128]{1,0:T(8,128)(2,1)}, bf16[3072,128]{1,0:T(8,128)(2,1)S(1)}, u32[]{:S(2)}, u32[]{:S(2)}) collective-permute-start(bf16[3072,128]{1,0:T(8,128)(2,1)} %slice_bitcast_fusion), channel_id=1, source_target_pairs={{0,8},{4,12},{24,16},{28,20},{32,40},{36,44},{56,48},{60,52},{64,7... | collective-permute-start | bytes 2359304 | tf_op jit(solution)/shard_map/ppermute | solution.py:32
  97.9 5.9 %copy-start.11 = (bf16[320,128]{1,0:T(8,128)(2,1)S(1)}, bf16[320,128]{1,0:T(8,128)(2,1)}, u32[]{:S(2)}) copy-start(bf16[320,128]{1,0:T(8,128)(2,1)} %copy-done.10) | copy-start | bytes 245764
  97.9 5.9 %copy-start.13 = (bf16[320,128]{1,0:T(8,128)(2,1)S(1)}, bf16[320,128]{1,0:T(8,128)(2,1)}, u32[]{:S(2)}) copy-start(bf16[320,128]{1,0:T(8,128)(2,1)} %copy-done.12) | copy-start | bytes 245764
  97.9 6.0 %copy-start.15 = (bf16[320,128]{1,0:T(8,128)(2,1)S(1)}, bf16[320,128]{1,0:T(8,128)(2,1)}, u32[]{:S(2)}) copy-start(bf16[320,128]{1,0:T(8,128)(2,1)} %copy-done.14) | copy-start | bytes 245764
  102.3 14.2 %collective-permute-start.19 = (bf16[2048,128]{1,0:T(8,128)(2,1)S(1)}, bf16[2048,128]{1,0:T(8,128)(2,1)S(1)}, u32[]{:S(2)}, u32[]{:S(2)}) collective-permute-start(bf16[2048,128]{1,0:T(8,128)(2,1)S(1)} %get-tuple-element.83), channel_id=1, source_target_pairs={{8,0},{12,4},{16,24},{20,28},{40,32},{44,36},{48,56},{52,60},{72,6... | collective-permute-start | bytes 1572872 | tf_op jit(solution)/shard_map/ppermute | solution.py:32
  114.2 0.9 copy-start.4
  116.6 0.8 copy-start.6
  117.4 4.3 %collective-permute-start.21 = (bf16[160,3072]{1,0:T(8,128)(2,1)S(1)}, bf16[160,3072]{1,0:T(8,128)(2,1)}, u32[]{:S(2)}, u32[]{:S(2)}) collective-permute-start(bf16[160,3072]{1,0:T(8,128)(2,1)S(1)} %collective-permute-done.16.refs_0_), channel_id=1, source_target_pairs={{0,4},{4,0},{8,12},{12,8},{16,20},{20,16},{24,28},{28,24},{32,36},... | collective-permute-start | bytes 2949128 | tf_op jit(solution)/shard_map/ppermute | solution.py:32
  119.4 18.4 %collective-permute-start.24 = (bf16[640,384]{1,0:T(8,128)(2,1)}, bf16[640,384]{1,0:T(8,128)(2,1)S(1)}, u32[]{:S(2)}, u32[]{:S(2)}) collective-permute-start(bf16[640,384]{1,0:T(8,128)(2,1)} %slice.29), channel_id=1, source_target_pairs={{0,96},{4,100},{8,104},{12,108},{16,112},{20,116},{24,120},{28,124... | collective-permute-start | bytes 1474568 | tf_op jit(solution)/shard_map/ppermute | solution.py:32
  121.2 16.6 %collective-permute-start.25 = (bf16[640,384]{1,0:T(8,128)(2,1)}, bf16[640,384]{1,0:T(8,128)(2,1)S(1)}, u32[]{:S(2)}, u32[]{:S(2)}) collective-permute-start(bf16[640,384]{1,0:T(8,128)(2,1)} %slice.30), channel_id=1, source_target_pairs={{0,32},{4,36},{8,40},{12,44},{16,48},{20,52},{24,56},{28,60},{32,6... | collective-permute-start | bytes 1474568 | tf_op jit(solution)/shard_map/ppermute | solution.py:32
  121.7 1.1 copy-start.5
  128.4 5.5 %collective-permute-start.22 = (s32[160,128]{1,0:T(8,128)S(1)}, s32[160,128]{1,0:T(8,128)S(1)}, u32[]{:S(2)}, u32[]{:S(2)}) collective-permute-start(s32[160,128]{1,0:T(8,128)S(1)} %get-tuple-element.101), channel_id=1, source_target_pairs={{8,0},{12,4},{16,24},{20,28},{40,32},{44,36},{48,56},{52,60},{72,6... | collective-permute-start | bytes 245768 | tf_op jit(solution)/shard_map/ppermute | solution.py:32
  134.0 24.2 %copy-start.16 = (s32[160]{0:T(256)S(1)}, s32[160]{0:T(256)}, u32[]{:S(2)}) copy-start(s32[160]{0:T(256)} %param.7) | copy-start | bytes 1924
  134.0 28.1 %copy-start.7 = (bf16[2048,128]{1,0:T(8,128)(2,1)S(1)}, bf16[2048,128]{1,0:T(8,128)(2,1)}, u32[]{:S(2)}) copy-start(bf16[2048,128]{1,0:T(8,128)(2,1)} %copy-done.6) | copy-start | bytes 1572868
  134.0 10.4 %collective-permute-start.23 = (s32[160,128]{1,0:T(8,128)S(1)}, s32[160,128]{1,0:T(8,128)S(1)}, u32[]{:S(2)}, u32[]{:S(2)}) collective-permute-start(s32[160,128]{1,0:T(8,128)S(1)} %broadcast_select_fusion.1), channel_id=1, source_target_pairs={{0,128},{4,132},{8,136},{12,140},{16,144},{20,148},{24,152},{28,15... | collective-permute-start | bytes 245768 | tf_op jit(solution)/shard_map/ppermute | solution.py:32
  144.5 28.2 %collective-permute-start.26 = (bf16[160,5120]{1,0:T(8,128)(2,1)}, bf16[160,5120]{1,0:T(8,128)(2,1)S(1)}, u32[]{:S(2)}, u32[]{:S(2)}) collective-permute-start(bf16[160,5120]{1,0:T(8,128)(2,1)} %get-tuple-element.109), channel_id=1, source_target_pairs={{0,4},{4,0},{8,12},{12,8},{16,20},{20,16},{24,28},{28,24},{32,36},... | collective-permute-start | bytes 4915208 | tf_op jit(solution)/shard_map/ppermute | solution.py:32
  146.0 23.6 %collective-permute-start.27 = (bf16[3072,128]{1,0:T(8,128)(2,1)}, bf16[3072,128]{1,0:T(8,128)(2,1)S(1)}, u32[]{:S(2)}, u32[]{:S(2)}) collective-permute-start(bf16[3072,128]{1,0:T(8,128)(2,1)} %get-tuple-element.112), channel_id=1, source_target_pairs={{8,0},{12,4},{16,24},{20,28},{40,32},{44,36},{48,56},{52,60},{72,6... | collective-permute-start | bytes 2359304 | tf_op jit(solution)/shard_map/ppermute | solution.py:32
  147.3 6.5 %collective-permute-start.28 = (s32[2,160,128]{2,1,0:T(8,128)S(1)}, s32[2,160,128]{2,1,0:T(8,128)S(1)}, u32[]{:S(2)}, u32[]{:S(2)}) collective-permute-start(s32[2,160,128]{2,1,0:T(8,128)S(1)} %pad_add_fusion.refs_0_), channel_id=1, source_target_pairs={{0,96},{4,100},{8,104},{12,108},{16,112},{20,116},{24,120},{28,124... | collective-permute-start | bytes 491528 | tf_op jit(solution)/shard_map/ppermute | solution.py:32
  150.2 10.2 %collective-permute-start.29 = (s32[2,160,128]{2,1,0:T(8,128)S(1)}, s32[2,160,128]{2,1,0:T(8,128)S(1)}, u32[]{:S(2)}, u32[]{:S(2)}) collective-permute-start(s32[2,160,128]{2,1,0:T(8,128)S(1)} %pad_add_fusion.refs_0_), channel_id=1, source_target_pairs={{0,32},{4,36},{8,40},{12,44},{16,48},{20,52},{24,56},{28,60},{32,6... | collective-permute-start | bytes 491528 | tf_op jit(solution)/shard_map/ppermute | solution.py:32
  150.2 11.3 %collective-permute-start.30 = (s32[2,160,128]{2,1,0:T(8,128)S(1)}, s32[2,160,128]{2,1,0:T(8,128)}, u32[]{:S(2)}, u32[]{:S(2)}) collective-permute-start(s32[2,160,128]{2,1,0:T(8,128)S(1)} %pad_add_fusion.refs_0_), channel_id=1, source_target_pairs={{0,64},{4,68},{8,72},{12,76},{16,80},{20,84},{24,88},{28,92},{32,9... | collective-permute-start | bytes 491528 | tf_op jit(solution)/shard_map/ppermute | solution.py:32
  153.8 7.7 %collective-permute-start.31 = (s32[2,160,128]{2,1,0:T(8,128)S(1)}, s32[2,160,128]{2,1,0:T(8,128)}, u32[]{:S(2)}, u32[]{:S(2)}) collective-permute-start(s32[2,160,128]{2,1,0:T(8,128)S(1)} %pad_add_fusion.refs_0_), channel_id=1, source_target_pairs={{0,4},{4,0},{8,12},{12,8},{16,20},{20,16},{24,28},{28,24},{32,36},... | collective-permute-start | bytes 491528 | tf_op jit(solution)/shard_map/ppermute | solution.py:32
  160.4 3.5 %collective-permute-start.32 = (s32[2,160,128]{2,1,0:T(8,128)S(1)}, s32[2,160,128]{2,1,0:T(8,128)S(1)}, u32[]{:S(2)}, u32[]{:S(2)}) collective-permute-start(s32[2,160,128]{2,1,0:T(8,128)S(1)} %collective-permute-done.28.refs_1_), channel_id=1, source_target_pairs={{0,4},{4,0},{8,12},{12,8},{16,20},{20,16},{24,28},{28,24},{32,36},... | collective-permute-start | bytes 491528 | tf_op jit(solution)/shard_map/ppermute | solution.py:32
  161.5 2.3 %collective-permute-start.33 = (s32[2,160,128]{2,1,0:T(8,128)S(1)}, s32[2,160,128]{2,1,0:T(8,128)S(1)}, u32[]{:S(2)}, u32[]{:S(2)}) collective-permute-start(s32[2,160,128]{2,1,0:T(8,128)S(1)} %collective-permute-done.29.refs_2_), channel_id=1, source_target_pairs={{0,4},{4,0},{8,12},{12,8},{16,20},{20,16},{24,28},{28,24},{32,36},... | collective-permute-start | bytes 491528 | tf_op jit(solution)/shard_map/ppermute | solution.py:32
  161.5 2.3 %collective-permute-start.34 = (s32[2,160,128]{2,1,0:T(8,128)}, s32[2,160,128]{2,1,0:T(8,128)S(1)}, u32[]{:S(2)}, u32[]{:S(2)}) collective-permute-start(s32[2,160,128]{2,1,0:T(8,128)} %collective-permute-done.30.refs_3_), channel_id=1, source_target_pairs={{0,4},{4,0},{8,12},{12,8},{16,20},{20,16},{24,28},{28,24},{32,36},... | collective-permute-start | bytes 491528 | tf_op jit(solution)/shard_map/ppermute | solution.py:32
  169.6 3.1 %copy-start.8 = (bf16[160,5120]{1,0:T(8,128)(2,1)S(1)}, bf16[160,5120]{1,0:T(8,128)(2,1)}, u32[]{:S(2)}) copy-start(bf16[160,5120]{1,0:T(8,128)(2,1)} %get-tuple-element.108.ours) | copy-start | bytes 4915204

commit v4 on v3

--- a/solution.py
+++ b/solution.py
@@ -12,6 +12,7 @@
 AXES = ("dp", "tensor")
 HI, YS, LINE, CORES = 2, 4, 4, 2
 WIDTH = 1024
+PACK = 512
 CUT = 2048
 COST = pl.CostEstimate(flops=2_000_000_000, bytes_accessed=10_000_000, transcendentals=0)
 VMEM = 48 * 1024 * 1024
@@ -139,11 +140,13 @@
         before = prior[...].astype(jnp.float32)
         new[...] = (beta_slow * before + (1.0 - beta_slow) * part).astype(jnp.bfloat16)
         positive = (beta_vote * before + (1.0 - beta_vote) * part > 0).astype(jnp.int32)
-        step = WIDTH // 32
-        packed = positive[:step]
-        for bit in range(1, 32):
-            packed = packed | (positive[bit * step : (bit + 1) * step] << bit)
-        words[...] = packed
+        step = PACK // 32
+        for block in range(WIDTH // PACK):
+            start = block * PACK
+            packed = positive[start : start + step]
+            for bit in range(1, 32):
+                packed = packed | (positive[start + bit * step : start + (bit + 1) * step] << bit)
+            words[block * step : (block + 1) * step, :] = packed
 
 
 def momentum_step(place, first, second, cot_own, cot_side, early, prior_own, prior_side, start, buffers):
@@ -211,35 +214,44 @@
     return more, fewer
 
 
-def choose_kernel(inner, own, returned, out):
-    out[...] = jnp.where(inner[0] == 1, own[...], returned[...])
-
-
-def choose_step(inner, own, returned, start):
-    skip = start // WIDTH
-    there = pl.BlockSpec((WIDTH, 128), lambda i, inner: (i + skip, 0))
-    return pl.pallas_call(
-        choose_kernel,
+def fill_kernel(inner, low, high, own, out, sems):
+    @pl.when(inner[0] == 0)
+    def _():
+        copies = [
+            pltpu.make_async_copy(ref, out.at[pl.ds(start, ref.shape[0])], sems.at[i])
+            for i, (ref, start) in enumerate(((low, 0), (high, low.shape[0])))
+        ]
+        for copy in copies:
+            copy.start()
+        for copy in copies:
+            copy.wait()
+
+
+def fill_step(inner, low, high, own):
+    anywhere = pl.BlockSpec(memory_space=pl.ANY)
+    return pl.pallas_call(
+        fill_kernel,
         grid_spec=pltpu.PrefetchScalarGridSpec(
             num_scalar_prefetch=1,
-            grid=(returned.shape[0] // WIDTH,),
-            in_specs=[there, pl.BlockSpec((WIDTH, 128), lambda i, inner: (i, 0))],
-            out_specs=there,
+            grid=(1,),
+            in_specs=[anywhere] * 3,
+            out_specs=anywhere,
+            scratch_shapes=[pltpu.SemaphoreType.DMA((2,))],
         ),
         out_shape=jax.ShapeDtypeStruct(own.shape, own.dtype),
-        input_output_aliases={1: 0},
+        input_output_aliases={3: 0},
         compiler_params=params(),
         cost_estimate=COST,
-        name="choose_step",
-    )(inner, own, returned)
+        name="fill_step",
+    )(inner, low, high, own)
 
 
 def vote_kernel(core, *refs):
     words_own, words_other, (w_own, w_other, out) = refs[:4], refs[4:8], refs[8:]
     is_low = core[0] == 0
-    step = WIDTH // 32
-    for block in range(out.shape[0] // WIDTH):
-        rows = slice(block * WIDTH, (block + 1) * WIDTH)
+    step = PACK // 32
+    for block in range(out.shape[0] // PACK):
+        rows = slice(block * PACK, (block + 1) * PACK)
         updated = []
         for words, weights in ((words_own, w_own), (words_other, w_other)):
             more, fewer = majority(
@@ -257,7 +269,7 @@
 
 def vote_step(core, words_own, words_other, w_own, w_other):
     features = w_own.shape[0]
-    size = WIDTH
+    size = features // 2
     word_spec = pl.BlockSpec((2, size // 32, 128), lambda i, core: (0, i, 0))
     weight_spec = pl.BlockSpec((size, 128), lambda i, core: (i, 0))
     return pl.pallas_call(
@@ -425,11 +437,12 @@
     votes = [pair, along_y(pair, 1), along_y(pair, -1), along_y(pair, 2)]
     returned_late = outward(new_side)
     input_grad = total_step(ours, core_swap(theirs), row_mask.astype(jnp.float32)[:, None])
-    new_own = choose_step(is_inner, new_own, returned, 0)
+    votes, input_grad = lax.optimization_barrier((votes, input_grad))
     votes_other = [core_swap(piece) for piece in votes]
-    rollout_weight = vote_step(core[None], votes, votes_other, w_key, w_other)[None]
-    new_momentum = choose_step(is_inner, new_own, returned_late, cut)[None]
-    return (input_grad, new_momentum, rollout_weight)
+    rollout_weight = vote_step(core[None], votes, votes_other, w_key, w_other)
+    returned_late, rollout_weight = lax.optimization_barrier((returned_late, rollout_weight))
+    new_momentum = fill_step(is_inner, returned, returned_late, new_own)
+    return (input_grad, new_momentum[None], rollout_weight[None])
 
 
 def solution(mesh):

time: 175 us -> 170 us (0.971)
  Pallas kernels: 39.8 us -> 34.8 us
  starting transfers between devices: 63.1 us -> 58.8 us
  waiting for transfers between devices: 52.1 us -> 54.9 us
    ppermute x35, starting transfers between devices: 63.1 us -> 58.8 us  [permute(): return lax.ppermute(array, AXES, pairs)]
    pallas_call x2 -> x1, Pallas kernels: 4.88 us -> 1.07 us  [fill_step(): pl.pallas_call(fill_kernel, grid_spec=pltpu.PrefetchScalarGridSpec(num_sc...]
    ppermute x35, waiting for transfers between devices: 52.1 us -> 54.9 us  [permute(): return lax.ppermute(array, AXES, pairs)]
  transfers between devices with their start and end apart: 35 -> 35, of which waited for: 12 -> 15; matrix products, arithmetic and copies ran while one was open for 7% -> 7% of each run, Pallas kernels for 22% -> 20%
where the time goes in v4:
time: 170 us; the launch traced here: 169 us
  starting transfers between devices  58.8 us (35%)
  waiting for transfers between devices  54.9 us (32%)
  Pallas kernels  34.8 us (20%)
  local copies, waits for them, and re-layouts  17.3 us (10%)
  other arithmetic  2.42 us (1%)
    ppermute x35, starting transfers between devices, permute(): return lax.ppermute(array, AXES, pairs)  58.8 us
    ppermute x35, waiting for transfers between devices, permute(): return lax.ppermute(array, AXES, pairs)  54.9 us
    pallas_call x2, Pallas kernels, gather_step(): pl.pallas_call(gather_kernel, grid_spec=pltpu.PrefetchScalarGridSpec(num_...  10.9 us
    pallas_call x2, Pallas kernels, momentum_step(): pl.pallas_call(momentum_kernel, grid_spec=pltpu.PrefetchScalarGridSpec(nu...  10 us
    pallas_call x1, Pallas kernels, input_step(): pl.pallas_call(input_kernel, grid_spec=pltpu.PrefetchScalarGridSpec(num_s...  6.62 us
    unnamed x39, local copies, waits for them, and re-layouts  5.94 us
    pallas_call x1, Pallas kernels, vote_step(): pl.pallas_call(vote_kernel, grid_spec=pltpu.PrefetchScalarGridSpec(num_sc...  4.52 us
    slice x2, local copies, waits for them, and re-layouts, per_device(): w_far = [w_next[:quarter // 2], w_before[quarter // 2:]]  3.83 us
  transfers between devices with their start and end apart: 35, of which 15 were waited for; matrix products, arithmetic and copies ran while one was open for 7% of the time, Pallas kernels for 20%

profile of v4, /device:TPU:1, one launch (start us, length us, event | category | flops | bytes accessed | tf_op | source)
XLA Modules:
  0.0 169.3 jit_solution(8080275520916566026)
XLA Ops:
  0.6 0.7 broadcast_compare_fusion
  1.3 1.6 broadcast_select_fusion.refs_0_
  3.0 1.1 constant_dynamic-slice_fusion.6
  4.1 2.6 %collective-permute-start.2 = (bf16[1280,128]{1,0:T(8,128)(2,1)S(1)}, bf16[1280,128]{1,0:T(8,128)(2,1)S(1)}, u32[]{:S(2)}, u32[]{:S(2)}) collective-permute-start(bf16[1280,128]{1,0:T(8,128)(2,1)S(1)} %constant_dynamic-slice_fusion.6), channel_id=1, source_target_pairs={{0,8},{4,12},{8,0},{12,4},{16,24},{20,28},{24,16},{28,20},{32,40},... | collective-permute-start | bytes 983048 | tf_op jit(solution)/shard_map/ppermute | solution.py:33
  6.6 4.7 %collective-permute-start.3 = (bf16[1280,128]{1,0:T(8,128)(2,1)S(1)}, bf16[1280,128]{1,0:T(8,128)(2,1)S(1)}, u32[]{:S(2)}, u32[]{:S(2)}) collective-permute-start(bf16[1280,128]{1,0:T(8,128)(2,1)S(1)} %constant_dynamic-slice_fusion.6), channel_id=1, source_target_pairs={{0,152},{4,156},{8,16},{12,20},{16,8},{20,12},{24,128},{28,132},{3... | collective-permute-start | bytes 983048 | tf_op jit(solution)/shard_map/ppermute | solution.py:33
  11.3 1.2 collective-permute-start.4
  12.5 1.9 %collective-permute-start = (bf16[160,5120]{1,0:T(8,128)(2,1)S(1)}, bf16[160,5120]{1,0:T(8,128)(2,1)}, u32[]{:S(2)}, u32[]{:S(2)}) collective-permute-start(bf16[160,5120]{1,0:T(8,128)(2,1)S(1)} %broadcast_select_fusion.refs_0_), channel_id=1, source_target_pairs={{8,16},{12,20},{16,8},{20,12},{40,48},{44,52},{48,40},{52,44},{72,... | collective-permute-start | bytes 4915208 | tf_op jit(solution)/shard_map/ppermute | solution.py:33
  14.3 2.8 %collective-permute-start.1 = (bf16[160,5120]{1,0:T(8,128)(2,1)S(1)}, bf16[160,5120]{1,0:T(8,128)(2,1)S(1)}, u32[]{:S(2)}, u32[]{:S(2)}) collective-permute-start(bf16[160,5120]{1,0:T(8,128)(2,1)S(1)} %broadcast_select_fusion.refs_0_), channel_id=1, source_target_pairs={{0,8},{4,12},{24,16},{28,20},{32,40},{36,44},{56,48},{60,52},{64,7... | collective-permute-start | bytes 4915208 | tf_op jit(solution)/shard_map/ppermute | solution.py:33
  17.1 1.9 %collective-permute-start.9 = (bf16[160,5120]{1,0:T(8,128)(2,1)S(1)}, bf16[160,5120]{1,0:T(8,128)(2,1)}, u32[]{:S(2)}, u32[]{:S(2)}) collective-permute-start(bf16[160,5120]{1,0:T(8,128)(2,1)S(1)} %broadcast_select_fusion.refs_0_), channel_id=1, source_target_pairs={{0,4},{4,0},{8,12},{12,8},{16,20},{20,16},{24,28},{28,24},{32,36},... | collective-permute-start | bytes 4915208 | tf_op jit(solution)/shard_map/ppermute | solution.py:33
  19.0 0.8 constant_dynamic-update-slice_fusion.2
  19.8 4.8 %collective-permute-done.3 = bf16[1280,128]{1,0:T(8,128)(2,1)S(1)} collective-permute-done((bf16[1280,128]{1,0:T(8,128)(2,1)S(1)}, bf16[1280,128]{1,0:T(8,128)(2,1)S(1)}, u32[]{:S(2)}, u32[]{:S(2)}) %collective-permute-start.3) | collective-permute-done | bytes 327712 | tf_op jit(solution)/shard_map/ppermute | solution.py:33
  24.6 0.8 constant_dynamic-update-slice_fusion.1
  25.4 6.3 %collective-permute-done.4 = bf16[1280,128]{1,0:T(8,128)(2,1)S(1)} collective-permute-done((bf16[1280,128]{1,0:T(8,128)(2,1)S(1)}, bf16[1280,128]{1,0:T(8,128)(2,1)S(1)}, u32[]{:S(2)}, u32[]{:S(2)}) %collective-permute-start.4) | collective-permute-done | bytes 327712 | tf_op jit(solution)/shard_map/ppermute | solution.py:33
  31.7 0.8 constant_dynamic-update-slice_fusion.here
  32.5 2.7 %collective-permute-start.5 = (bf16[1280,384]{1,0:T(8,128)(2,1)}, bf16[1280,384]{1,0:T(8,128)(2,1)}, u32[]{:S(2)}, u32[]{:S(2)}) collective-permute-start(bf16[1280,384]{1,0:T(8,128)(2,1)} %constant_dynamic-update-slice_fusion.here), channel_id=1, source_target_pairs={{0,96},{4,100},{8,104},{12,108},{16,112},{20,116},{24,120},{28,124... | collective-permute-start | bytes 2949128 | tf_op jit(solution)/shard_map/ppermute | solution.py:33
  35.1 0.9 slice_bitcast_fusion
  36.1 0.8 slice_bitcast_fusion.1
  36.9 1.7 constant_dynamic-slice_fusion.2
  38.6 16.2 %collective-permute-done.5.following = bf16[1280,384]{1,0:T(8,128)(2,1)} collective-permute-done((bf16[1280,384]{1,0:T(8,128)(2,1)}, bf16[1280,384]{1,0:T(8,128)(2,1)}, u32[]{:S(2)}, u32[]{:S(2)}) %collective-permute-start.5) | collective-permute-done | bytes 983072 | tf_op jit(solution)/shard_map/ppermute | solution.py:33
  54.8 3.1 %collective-permute-done.6.before = bf16[1280,384]{1,0:T(8,128)(2,1)} collective-permute-done((bf16[1280,384]{1,0:T(8,128)(2,1)}, bf16[1280,384]{1,0:T(8,128)(2,1)}, u32[]{:S(2)}, u32[]{:S(2)}) %collective-permute-start.6) | collective-permute-done | bytes 983072 | tf_op jit(solution)/shard_map/ppermute | solution.py:33
  58.1 2.7 %collective-permute-start.10 = (bf16[160,5120]{1,0:T(8,128)(2,1)}, bf16[160,5120]{1,0:T(8,128)(2,1)}, u32[]{:S(2)}, u32[]{:S(2)}) collective-permute-start(bf16[160,5120]{1,0:T(8,128)(2,1)} %collective-permute-done.refs_4_), channel_id=1, source_target_pairs={{0,4},{4,0},{8,12},{12,8},{16,20},{20,16},{24,28},{28,24},{32,36},... | collective-permute-start | bytes 4915208 | tf_op jit(solution)/shard_map/ppermute | solution.py:33
  60.9 4.7 %collective-permute-start.12 = (bf16[1280,128]{1,0:T(8,128)(2,1)}, bf16[1280,128]{1,0:T(8,128)(2,1)}, u32[]{:S(2)}, u32[]{:S(2)}) collective-permute-start(bf16[1280,128]{1,0:T(8,128)(2,1)} %refs_2_.1), channel_id=1, source_target_pairs={{0,8},{4,12},{24,16},{28,20},{32,40},{36,44},{56,48},{60,52},{64,7... | collective-permute-start | bytes 983048 | tf_op jit(solution)/shard_map/ppermute | solution.py:33
  65.7 0.9 slice.28
  66.6 1.5 collective-permute-start.7
  68.1 2.5 %collective-permute-start.8 = (bf16[2048,128]{1,0:T(8,128)(2,1)}, bf16[2048,128]{1,0:T(8,128)(2,1)}, u32[]{:S(2)}, u32[]{:S(2)}) collective-permute-start(bf16[2048,128]{1,0:T(8,128)(2,1)} %slice_bitcast_fusion.1), channel_id=1, source_target_pairs={{0,8},{4,12},{24,16},{28,20},{32,40},{36,44},{56,48},{60,52},{64,7... | collective-permute-start | bytes 1572872 | tf_op jit(solution)/shard_map/ppermute | solution.py:33
  70.7 1.9 %slice.29 = bf16[640,384]{1,0:T(8,128)(2,1)} slice(bf16[1280,384]{1,0:T(8,128)(2,1)} %collective-permute-done.5.following), slice={[0:640], [0:384]} | slice | bytes 983040 | tf_op jit(solution)/shard_map/slice | solution.py:398
  72.6 1.9 %slice.30 = bf16[640,384]{1,0:T(8,128)(2,1)} slice(bf16[1280,384]{1,0:T(8,128)(2,1)} %collective-permute-done.6.before), slice={[640:1280], [0:384]} | slice | bytes 983040 | tf_op jit(solution)/shard_map/slice | solution.py:398
  74.6 1.7 %collective-permute-start.14 = (bf16[320,128]{1,0:T(8,128)(2,1)S(1)}, bf16[320,128]{1,0:T(8,128)(2,1)S(1)}, u32[]{:S(2)}, u32[]{:S(2)}) collective-permute-start(bf16[320,128]{1,0:T(8,128)(2,1)S(1)} %get-tuple-element.81), channel_id=1, source_target_pairs={{0,24},{4,28},{8,16},{12,20},{16,8},{20,12},{24,0},{28,4},{32,56},... | collective-permute-start | bytes 245768 | tf_op jit(solution)/shard_map/ppermute | solution.py:33
  76.3 0.9 collective-permute-start.15
  77.2 6.3 %gather_step.3.refs_4_ = f32[3072,256]{1,0:T(8,128)} custom-call(s32[8]{0:T(128)S(1)} %stack.59.place, bf16[160,5120]{1,0:T(8,128)(2,1)S(1)} %broadcast_select_fusion.refs_0_, bf16[160,5120]{1,0:T(8,128)(2,1)} %collective-permute-done.9.refs_1_, bf16[160,5120]{1,0:T(8,128)(2,1)S(1)} %collective-permute-done.1.refs_2_, ...), custom_call_target="tpu_custom_call" | custom-call | flops 2000000000 | bytes 10000000 | tf_op jit(solution)/shard_map/gather_step/pallas_call | solution.py:109
  83.5 4.6 %gather_step.2.refs_4_ = f32[2048,256]{1,0:T(8,128)} custom-call(s32[8]{0:T(128)S(1)} %stack.59.place, bf16[160,5120]{1,0:T(8,128)(2,1)S(1)} %broadcast_select_fusion.refs_0_, bf16[160,5120]{1,0:T(8,128)(2,1)} %collective-permute-done.9.refs_1_, bf16[160,5120]{1,0:T(8,128)(2,1)S(1)} %collective-permute-done.1.refs_2_, ...), custom_call_target="tpu_custom_call" | custom-call | flops 2000000000 | bytes 10000000 | tf_op jit(solution)/shard_map/gather_step/pallas_call | solution.py:109
  88.2 0.7 collective-permute-done.14
  88.9 2.2 %collective-permute-start.18 = (bf16[160,2048]{1,0:T(8,128)(2,1)}, bf16[160,2048]{1,0:T(8,128)(2,1)}, u32[]{:S(2)}, u32[]{:S(2)}) collective-permute-start(bf16[160,2048]{1,0:T(8,128)(2,1)} %collective-permute-done.7.refs_0_), channel_id=1, source_target_pairs={{0,4},{4,0},{8,12},{12,8},{16,20},{20,16},{24,28},{28,24},{32,36},... | collective-permute-start | bytes 1966088 | tf_op jit(solution)/shard_map/ppermute | solution.py:33
  91.2 1.0 slice.31
  92.2 0.7 collective-permute-start.16
  93.0 4.9 %collective-permute-start.17 = (bf16[3072,128]{1,0:T(8,128)(2,1)}, bf16[3072,128]{1,0:T(8,128)(2,1)S(1)}, u32[]{:S(2)}, u32[]{:S(2)}) collective-permute-start(bf16[3072,128]{1,0:T(8,128)(2,1)} %slice_bitcast_fusion), channel_id=1, source_target_pairs={{0,8},{4,12},{24,16},{28,20},{32,40},{36,44},{56,48},{60,52},{64,7... | collective-permute-start | bytes 2359304 | tf_op jit(solution)/shard_map/ppermute | solution.py:33
  97.9 4.4 %momentum_step.2 = (bf16[5120,128]{1,0:T(8,128)(2,1)}, bf16[2048,128]{1,0:T(8,128)(2,1)S(1)}, s32[160,128]{1,0:T(8,128)S(1)}, s32[160,128]{1,0:T(8,128)S(1)}) custom-call(s32[8]{0:T(128)S(1)} %stack.59.place, bf16[160,2048]{1,0:T(8,128)(2,1)} %collective-permute-done.7.refs_0_, bf16[160,2048]{1,0:T(8,128)(2,1)} %collective-permute-done.18.refs_1_, ...), custom_call_target="tpu_custom_call" | custom-call | flops 2000000000 | bytes 10000000 | tf_op jit(solution)/shard_map/momentum_step/pallas_call | solution.py:162
  102.3 1.5 collective-permute-start.19
  104.0 10.2 %collective-permute-done.17.refs_6_ = bf16[3072,128]{1,0:T(8,128)(2,1)S(1)} collective-permute-done((bf16[3072,128]{1,0:T(8,128)(2,1)}, bf16[3072,128]{1,0:T(8,128)(2,1)S(1)}, u32[]{:S(2)}, u32[]{:S(2)}) %collective-permute-start.17) | collective-permute-done | bytes 786464 | tf_op jit(solution)/shard_map/ppermute | solution.py:33
  114.2 0.9 copy-done.4
  115.1 1.5 collective-permute-done.19.low
  116.6 0.8 copy-done.6
  117.4 2.0 %collective-permute-start.21 = (bf16[160,3072]{1,0:T(8,128)(2,1)S(1)}, bf16[160,3072]{1,0:T(8,128)(2,1)}, u32[]{:S(2)}, u32[]{:S(2)}) collective-permute-start(bf16[160,3072]{1,0:T(8,128)(2,1)S(1)} %collective-permute-done.16.refs_0_), channel_id=1, source_target_pairs={{0,4},{4,0},{8,12},{12,8},{16,20},{20,16},{24,28},{28,24},{32,36},... | collective-permute-start | bytes 2949128 | tf_op jit(solution)/shard_map/ppermute | solution.py:33
  119.4 1.9 %collective-permute-start.24 = (bf16[640,384]{1,0:T(8,128)(2,1)}, bf16[640,384]{1,0:T(8,128)(2,1)S(1)}, u32[]{:S(2)}, u32[]{:S(2)}) collective-permute-start(bf16[640,384]{1,0:T(8,128)(2,1)} %slice.29), channel_id=1, source_target_pairs={{0,96},{4,100},{8,104},{12,108},{16,112},{20,116},{24,120},{28,124... | collective-permute-start | bytes 1474568 | tf_op jit(solution)/shard_map/ppermute | solution.py:33
  121.3 0.4 collective-permute-done.21.refs_1_
  121.7 1.1 copy-done.5
  122.8 5.6 %momentum_step.3 = (bf16[5120,128]{1,0:T(8,128)(2,1)}, bf16[3072,128]{1,0:T(8,128)(2,1)}, s32[160,128]{1,0:T(8,128)S(1)}, s32[160,128]{1,0:T(8,128)S(1)}) custom-call(s32[8]{0:T(128)S(1)} %stack.59.place, bf16[160,3072]{1,0:T(8,128)(2,1)S(1)} %collective-permute-done.16.refs_0_, ...), custom_call_target="tpu_custom_call", output_to_operand_aliasing={{0}: (8, {}), {2}: (9, {}), {3}: (10, {})} | custom-call | flops 2000000000 | bytes 10000000 | tf_op jit(solution)/shard_map/momentum_step/pallas_call | solution.py:162
  128.5 1.3 collective-permute-start.22
  129.8 4.2 %collective-permute-done.22 = s32[160,128]{1,0:T(8,128)S(1)} collective-permute-done((s32[160,128]{1,0:T(8,128)S(1)}, s32[160,128]{1,0:T(8,128)S(1)}, u32[]{:S(2)}, u32[]{:S(2)}) %collective-permute-start.22) | collective-permute-done | bytes 81952 | tf_op jit(solution)/shard_map/ppermute | solution.py:33
  134.0 3.8 %collective-permute-start.23 = (s32[160,128]{1,0:T(8,128)S(1)}, s32[160,128]{1,0:T(8,128)S(1)}, u32[]{:S(2)}, u32[]{:S(2)}) collective-permute-start(s32[160,128]{1,0:T(8,128)S(1)} %broadcast_select_fusion.1), channel_id=1, source_target_pairs={{0,128},{4,132},{8,136},{12,140},{16,144},{20,148},{24,152},{28,15... | collective-permute-start | bytes 245768 | tf_op jit(solution)/shard_map/ppermute | solution.py:33
  137.8 6.6 %input_step.1 = (bf16[160,5120]{1,0:T(8,128)(2,1)}, bf16[160,5120]{1,0:T(8,128)(2,1)}) custom-call(s32[4]{0:T(128)S(1)} %pad_add_fusion.1.place, bf16[320,512]{1,0:T(8,128)(2,1)S(1)} %pad_maximum_fusion.cot, bf16[5120,128]{1,0:T(8,128)(2,1)} %refs_8_.1, bf16[1280,384]{1,0:T(8,128)(2,1)} %constant_dynamic-update-slice_fusion.here, ...), custom_call_target="tpu_custom_call" | custom-call | flops 1677721600 | bytes 8519680 | tf_op jit(solution)/shard_map/input_step/pallas_call | solution.py:312
  144.5 1.6 collective-permute-start.29
  146.0 1.3 collective-permute-start.30
  147.4 2.9 %collective-permute-start.26 = (s32[2,160,128]{2,1,0:T(8,128)S(1)}, s32[2,160,128]{2,1,0:T(8,128)S(1)}, u32[]{:S(2)}, u32[]{:S(2)}) collective-permute-start(s32[2,160,128]{2,1,0:T(8,128)S(1)} %pad_add_fusion.refs_0_), channel_id=1, source_target_pairs={{0,96},{4,100},{8,104},{12,108},{16,112},{20,116},{24,120},{28,124... | collective-permute-start | bytes 491528 | tf_op jit(solution)/shard_map/ppermute | solution.py:33
  150.3 1.3 collective-permute-start.28
  151.6 1.4 copy-done.8
  153.0 1.6 total_step.1
  154.7 5.8 %collective-permute-done.27.refs_2_ = s32[2,160,128]{2,1,0:T(8,128)S(1)} collective-permute-done((s32[2,160,128]{2,1,0:T(8,128)S(1)}, s32[2,160,128]{2,1,0:T(8,128)S(1)}, u32[]{:S(2)}, u32[]{:S(2)}) %collective-permute-start.27) | collective-permute-done | bytes 163872 | tf_op jit(solution)/shard_map/ppermute | solution.py:33
  160.5 1.1 collective-permute-start.31
  161.7 0.5 collective-permute-start.33
  162.2 0.5 collective-permute-done.31.refs_4_
  162.7 0.4 collective-permute-done.32.refs_5_
  163.6 4.5 %vote_step.1 = bf16[5120,256]{1,0:T(8,128)(2,1)} custom-call(s32[1]{0:T(128)} %bitcast.19.core, s32[2,160,128]{2,1,0:T(8,128)S(1)} %pad_add_fusion.refs_0_, s32[2,160,128]{2,1,0:T(8,128)S(1)} %collective-permute-done.26.refs_1_, s32[2,160,128]{2,1,0:T(8,128)S(1)} %collective-permute-done.27.refs_2_, s32[2,160,128]{2,1,0:T(8,128)S(1)} %collective-permute-done.28.refs_3_, ...), custom_call_target="tpu_custom_call" | custom-call | flops 2000000000 | bytes 10000000 | tf_op jit(solution)/shard_map/vote_step/pallas_call | solution.py:275
  168.1 1.1 fill_step.1
  (73 shorter events, 1.6 us)
Async XLA Ops:
  2.9 32.2 %copy-start = (bf16[1,5120,128]{2,1,0:T(8,128)(2,1)S(1)}, bf16[1,5120,128]{2,1,0:T(8,128)(2,1)}, u32[]{:S(2)}) copy-start(bf16[1,5120,128]{2,1,0:T(8,128)(2,1)} %param.9) | copy-start | bytes 3932164
  4.1 13.1 %collective-permute-start.2 = (bf16[1280,128]{1,0:T(8,128)(2,1)S(1)}, bf16[1280,128]{1,0:T(8,128)(2,1)S(1)}, u32[]{:S(2)}, u32[]{:S(2)}) collective-permute-start(bf16[1280,128]{1,0:T(8,128)(2,1)S(1)} %constant_dynamic-slice_fusion.6), channel_id=1, source_target_pairs={{0,8},{4,12},{8,0},{12,4},{16,24},{20,28},{24,16},{28,20},{32,40},... | collective-permute-start | bytes 983048 | tf_op jit(solution)/shard_map/ppermute | solution.py:33
  6.6 18.0 %collective-permute-start.3 = (bf16[1280,128]{1,0:T(8,128)(2,1)S(1)}, bf16[1280,128]{1,0:T(8,128)(2,1)S(1)}, u32[]{:S(2)}, u32[]{:S(2)}) collective-permute-start(bf16[1280,128]{1,0:T(8,128)(2,1)S(1)} %constant_dynamic-slice_fusion.6), channel_id=1, source_target_pairs={{0,152},{4,156},{8,16},{12,20},{16,8},{20,12},{24,128},{28,132},{3... | collective-permute-start | bytes 983048 | tf_op jit(solution)/shard_map/ppermute | solution.py:33
  11.3 20.4 %collective-permute-start.4 = (bf16[1280,128]{1,0:T(8,128)(2,1)S(1)}, bf16[1280,128]{1,0:T(8,128)(2,1)S(1)}, u32[]{:S(2)}, u32[]{:S(2)}) collective-permute-start(bf16[1280,128]{1,0:T(8,128)(2,1)S(1)} %constant_dynamic-slice_fusion.6), channel_id=1, source_target_pairs={{0,144},{4,148},{8,152},{12,156},{16,128},{20,132},{24,136},{28,14... | collective-permute-start | bytes 983048 | tf_op jit(solution)/shard_map/ppermute | solution.py:33
  12.5 45.4 %collective-permute-start = (bf16[160,5120]{1,0:T(8,128)(2,1)S(1)}, bf16[160,5120]{1,0:T(8,128)(2,1)}, u32[]{:S(2)}, u32[]{:S(2)}) collective-permute-start(bf16[160,5120]{1,0:T(8,128)(2,1)S(1)} %broadcast_select_fusion.refs_0_), channel_id=1, source_target_pairs={{8,16},{12,20},{16,8},{20,12},{40,48},{44,52},{48,40},{52,44},{72,... | collective-permute-start | bytes 4915208 | tf_op jit(solution)/shard_map/ppermute | solution.py:33
  14.3 43.8 %collective-permute-start.1 = (bf16[160,5120]{1,0:T(8,128)(2,1)S(1)}, bf16[160,5120]{1,0:T(8,128)(2,1)S(1)}, u32[]{:S(2)}, u32[]{:S(2)}) collective-permute-start(bf16[160,5120]{1,0:T(8,128)(2,1)S(1)} %broadcast_select_fusion.refs_0_), channel_id=1, source_target_pairs={{0,8},{4,12},{24,16},{28,20},{32,40},{36,44},{56,48},{60,52},{64,7... | collective-permute-start | bytes 4915208 | tf_op jit(solution)/shard_map/ppermute | solution.py:33
  17.1 50.9 %collective-permute-start.9 = (bf16[160,5120]{1,0:T(8,128)(2,1)S(1)}, bf16[160,5120]{1,0:T(8,128)(2,1)}, u32[]{:S(2)}, u32[]{:S(2)}) collective-permute-start(bf16[160,5120]{1,0:T(8,128)(2,1)S(1)} %broadcast_select_fusion.refs_0_), channel_id=1, source_target_pairs={{0,4},{4,0},{8,12},{12,8},{16,20},{20,16},{24,28},{28,24},{32,36},... | collective-permute-start | bytes 4915208 | tf_op jit(solution)/shard_map/ppermute | solution.py:33
  32.5 22.3 %collective-permute-start.5 = (bf16[1280,384]{1,0:T(8,128)(2,1)}, bf16[1280,384]{1,0:T(8,128)(2,1)}, u32[]{:S(2)}, u32[]{:S(2)}) collective-permute-start(bf16[1280,384]{1,0:T(8,128)(2,1)} %constant_dynamic-update-slice_fusion.here), channel_id=1, source_target_pairs={{0,96},{4,100},{8,104},{12,108},{16,112},{20,116},{24,120},{28,124... | collective-permute-start | bytes 2949128 | tf_op jit(solution)/shard_map/ppermute | solution.py:33
  35.1 22.8 %collective-permute-start.6 = (bf16[1280,384]{1,0:T(8,128)(2,1)}, bf16[1280,384]{1,0:T(8,128)(2,1)}, u32[]{:S(2)}, u32[]{:S(2)}) collective-permute-start(bf16[1280,384]{1,0:T(8,128)(2,1)} %constant_dynamic-update-slice_fusion.here), channel_id=1, source_target_pairs={{0,32},{4,36},{8,40},{12,44},{16,48},{20,52},{24,56},{28,60},{32,6... | collective-permute-start | bytes 2949128 | tf_op jit(solution)/shard_map/ppermute | solution.py:33
  58.1 16.4 %collective-permute-start.10 = (bf16[160,5120]{1,0:T(8,128)(2,1)}, bf16[160,5120]{1,0:T(8,128)(2,1)}, u32[]{:S(2)}, u32[]{:S(2)}) collective-permute-start(bf16[160,5120]{1,0:T(8,128)(2,1)} %collective-permute-done.refs_4_), channel_id=1, source_target_pairs={{0,4},{4,0},{8,12},{12,8},{16,20},{20,16},{24,28},{28,24},{32,36},... | collective-permute-start | bytes 4915208 | tf_op jit(solution)/shard_map/ppermute | solution.py:33
  60.8 13.7 %collective-permute-start.11 = (bf16[160,5120]{1,0:T(8,128)(2,1)S(1)}, bf16[160,5120]{1,0:T(8,128)(2,1)}, u32[]{:S(2)}, u32[]{:S(2)}) collective-permute-start(bf16[160,5120]{1,0:T(8,128)(2,1)S(1)} %collective-permute-done.1.refs_2_), channel_id=1, source_target_pairs={{0,4},{4,0},{8,12},{12,8},{16,20},{20,16},{24,28},{28,24},{32,36},... | collective-permute-start | bytes 4915208 | tf_op jit(solution)/shard_map/ppermute | solution.py:33
  60.9 15.4 %collective-permute-start.12 = (bf16[1280,128]{1,0:T(8,128)(2,1)}, bf16[1280,128]{1,0:T(8,128)(2,1)}, u32[]{:S(2)}, u32[]{:S(2)}) collective-permute-start(bf16[1280,128]{1,0:T(8,128)(2,1)} %refs_2_.1), channel_id=1, source_target_pairs={{0,8},{4,12},{24,16},{28,20},{32,40},{36,44},{56,48},{60,52},{64,7... | collective-permute-start | bytes 983048 | tf_op jit(solution)/shard_map/ppermute | solution.py:33
  66.6 21.6 %collective-permute-start.7 = (bf16[160,2048]{1,0:T(8,128)(2,1)}, bf16[160,2048]{1,0:T(8,128)(2,1)}, u32[]{:S(2)}, u32[]{:S(2)}) collective-permute-start(bf16[160,2048]{1,0:T(8,128)(2,1)} %slice.28), channel_id=1, source_target_pairs={{8,16},{12,20},{16,8},{20,12},{40,48},{44,52},{48,40},{52,44},{72,... | collective-permute-start | bytes 1966088 | tf_op jit(solution)/shard_map/ppermute | solution.py:33
  68.1 20.1 %collective-permute-start.8 = (bf16[2048,128]{1,0:T(8,128)(2,1)}, bf16[2048,128]{1,0:T(8,128)(2,1)}, u32[]{:S(2)}, u32[]{:S(2)}) collective-permute-start(bf16[2048,128]{1,0:T(8,128)(2,1)} %slice_bitcast_fusion.1), channel_id=1, source_target_pairs={{0,8},{4,12},{24,16},{28,20},{32,40},{36,44},{56,48},{60,52},{64,7... | collective-permute-start | bytes 1572872 | tf_op jit(solution)/shard_map/ppermute | solution.py:33
  70.6 3.8 %copy-start.9 = (bf16[320,128]{1,0:T(8,128)(2,1)S(1)}, bf16[320,128]{1,0:T(8,128)(2,1)}, u32[]{:S(2)}) copy-start(bf16[320,128]{1,0:T(8,128)(2,1)} %get-tuple-element.80) | copy-start | bytes 245764
  70.6 6.6 %copy-start.2 = (bf16[1280,128]{1,0:T(8,128)(2,1)S(1)}, bf16[1280,128]{1,0:T(8,128)(2,1)}, u32[]{:S(2)}) copy-start(bf16[1280,128]{1,0:T(8,128)(2,1)} %refs_2_.1) | copy-start | bytes 983044
  74.5 13.7 %collective-permute-start.13 = (bf16[320,128]{1,0:T(8,128)(2,1)S(1)}, bf16[320,128]{1,0:T(8,128)(2,1)S(1)}, u32[]{:S(2)}, u32[]{:S(2)}) collective-permute-start(bf16[320,128]{1,0:T(8,128)(2,1)S(1)} %copy-done.9), channel_id=1, source_target_pairs={{0,8},{4,12},{8,0},{12,4},{16,24},{20,28},{24,16},{28,20},{32,40},... | collective-permute-start | bytes 245768 | tf_op jit(solution)/shard_map/ppermute | solution.py:33
  74.6 14.3 %collective-permute-start.14 = (bf16[320,128]{1,0:T(8,128)(2,1)S(1)}, bf16[320,128]{1,0:T(8,128)(2,1)S(1)}, u32[]{:S(2)}, u32[]{:S(2)}) collective-permute-start(bf16[320,128]{1,0:T(8,128)(2,1)S(1)} %get-tuple-element.81), channel_id=1, source_target_pairs={{0,24},{4,28},{8,16},{12,20},{16,8},{20,12},{24,0},{28,4},{32,56},... | collective-permute-start | bytes 245768 | tf_op jit(solution)/shard_map/ppermute | solution.py:33
  76.3 12.6 %collective-permute-start.15 = (bf16[320,128]{1,0:T(8,128)(2,1)S(1)}, bf16[320,128]{1,0:T(8,128)(2,1)S(1)}, u32[]{:S(2)}, u32[]{:S(2)}) collective-permute-start(bf16[320,128]{1,0:T(8,128)(2,1)S(1)} %get-tuple-element.82), channel_id=1, source_target_pairs={{0,16},{4,20},{8,24},{12,28},{16,0},{20,4},{24,8},{28,12},{32,48},... | collective-permute-start | bytes 245768 | tf_op jit(solution)/shard_map/ppermute | solution.py:33
  88.2 9.7 %copy-start.1 = (bf16[1,5120,128]{2,1,0:T(8,128)(2,1)S(1)}, bf16[1,5120,128]{2,1,0:T(8,128)(2,1)}, u32[]{:S(2)}) copy-start(bf16[1,5120,128]{2,1,0:T(8,128)(2,1)} %param.9) | copy-start | bytes 3932164
  88.2 9.7 %copy-start.3 = (bf16[1280,128]{1,0:T(8,128)(2,1)S(1)}, bf16[1280,128]{1,0:T(8,128)(2,1)}, u32[]{:S(2)}) copy-start(bf16[1280,128]{1,0:T(8,128)(2,1)} %refs_2_.1) | copy-start | bytes 983044
  88.2 4.0 %copy-start.10 = (bf16[320,128]{1,0:T(8,128)(2,1)}, bf16[320,128]{1,0:T(8,128)(2,1)S(1)}, u32[]{:S(2)}) copy-start(bf16[320,128]{1,0:T(8,128)(2,1)S(1)} %collective-permute-done.13) | copy-start | bytes 245764
  88.9 3.3 %copy-start.12 = (bf16[320,128]{1,0:T(8,128)(2,1)}, bf16[320,128]{1,0:T(8,128)(2,1)S(1)}, u32[]{:S(2)}) copy-start(bf16[320,128]{1,0:T(8,128)(2,1)S(1)} %collective-permute-done.14) | copy-start | bytes 245764
  88.9 3.3 %copy-start.14 = (bf16[320,128]{1,0:T(8,128)(2,1)}, bf16[320,128]{1,0:T(8,128)(2,1)S(1)}, u32[]{:S(2)}) copy-start(bf16[320,128]{1,0:T(8,128)(2,1)S(1)} %collective-permute-done.15) | copy-start | bytes 245764
  88.9 9.0 %collective-permute-start.18 = (bf16[160,2048]{1,0:T(8,128)(2,1)}, bf16[160,2048]{1,0:T(8,128)(2,1)}, u32[]{:S(2)}, u32[]{:S(2)}) collective-permute-start(bf16[160,2048]{1,0:T(8,128)(2,1)} %collective-permute-done.7.refs_0_), channel_id=1, source_target_pairs={{0,4},{4,0},{8,12},{12,8},{16,20},{20,16},{24,28},{28,24},{32,36},... | collective-permute-start | bytes 1966088 | tf_op jit(solution)/shard_map/ppermute | solution.py:33
  91.1 12.9 %collective-permute-start.20 = (bf16[5120,128]{1,0:T(8,128)(2,1)}, bf16[5120,128]{1,0:T(8,128)(2,1)}, u32[]{:S(2)}, u32[]{:S(2)}) collective-permute-start(bf16[5120,128]{1,0:T(8,128)(2,1)} %refs_8_.1), channel_id=1, source_target_pairs={{0,4},{4,0},{8,12},{12,8},{16,20},{20,16},{24,28},{28,24},{32,36},... | collective-permute-start | bytes 3932168 | tf_op jit(solution)/shard_map/ppermute | solution.py:33
  92.2 22.8 %collective-permute-start.16 = (bf16[160,3072]{1,0:T(8,128)(2,1)}, bf16[160,3072]{1,0:T(8,128)(2,1)S(1)}, u32[]{:S(2)}, u32[]{:S(2)}) collective-permute-start(bf16[160,3072]{1,0:T(8,128)(2,1)} %slice.31), channel_id=1, source_target_pairs={{8,16},{12,20},{16,8},{20,12},{40,48},{44,52},{48,40},{52,44},{72,... | collective-permute-start | bytes 2949128 | tf_op jit(solution)/shard_map/ppermute | solution.py:33
  93.0 21.2 %collective-permute-start.17 = (bf16[3072,128]{1,0:T(8,128)(2,1)}, bf16[3072,128]{1,0:T(8,128)(2,1)S(1)}, u32[]{:S(2)}, u32[]{:S(2)}) collective-permute-start(bf16[3072,128]{1,0:T(8,128)(2,1)} %slice_bitcast_fusion), channel_id=1, source_target_pairs={{0,8},{4,12},{24,16},{28,20},{32,40},{36,44},{56,48},{60,52},{64,7... | collective-permute-start | bytes 2359304 | tf_op jit(solution)/shard_map/ppermute | solution.py:33
  97.9 5.9 %copy-start.11 = (bf16[320,128]{1,0:T(8,128)(2,1)S(1)}, bf16[320,128]{1,0:T(8,128)(2,1)}, u32[]{:S(2)}) copy-start(bf16[320,128]{1,0:T(8,128)(2,1)} %copy-done.10) | copy-start | bytes 245764
  97.9 5.9 %copy-start.13 = (bf16[320,128]{1,0:T(8,128)(2,1)S(1)}, bf16[320,128]{1,0:T(8,128)(2,1)}, u32[]{:S(2)}) copy-start(bf16[320,128]{1,0:T(8,128)(2,1)} %copy-done.12) | copy-start | bytes 245764
  97.9 6.0 %copy-start.15 = (bf16[320,128]{1,0:T(8,128)(2,1)S(1)}, bf16[320,128]{1,0:T(8,128)(2,1)}, u32[]{:S(2)}) copy-start(bf16[320,128]{1,0:T(8,128)(2,1)} %copy-done.14) | copy-start | bytes 245764
  102.3 14.2 %collective-permute-start.19 = (bf16[2048,128]{1,0:T(8,128)(2,1)S(1)}, bf16[2048,128]{1,0:T(8,128)(2,1)S(1)}, u32[]{:S(2)}, u32[]{:S(2)}) collective-permute-start(bf16[2048,128]{1,0:T(8,128)(2,1)S(1)} %get-tuple-element.90), channel_id=1, source_target_pairs={{8,0},{12,4},{16,24},{20,28},{40,32},{44,36},{48,56},{52,60},{72,6... | collective-permute-start | bytes 1572872 | tf_op jit(solution)/shard_map/ppermute | solution.py:33
  114.2 0.9 copy-start.4
  116.6 0.8 copy-start.6
  117.4 4.3 %collective-permute-start.21 = (bf16[160,3072]{1,0:T(8,128)(2,1)S(1)}, bf16[160,3072]{1,0:T(8,128)(2,1)}, u32[]{:S(2)}, u32[]{:S(2)}) collective-permute-start(bf16[160,3072]{1,0:T(8,128)(2,1)S(1)} %collective-permute-done.16.refs_0_), channel_id=1, source_target_pairs={{0,4},{4,0},{8,12},{12,8},{16,20},{20,16},{24,28},{28,24},{32,36},... | collective-permute-start | bytes 2949128 | tf_op jit(solution)/shard_map/ppermute | solution.py:33
  119.4 18.5 %collective-permute-start.24 = (bf16[640,384]{1,0:T(8,128)(2,1)}, bf16[640,384]{1,0:T(8,128)(2,1)S(1)}, u32[]{:S(2)}, u32[]{:S(2)}) collective-permute-start(bf16[640,384]{1,0:T(8,128)(2,1)} %slice.29), channel_id=1, source_target_pairs={{0,96},{4,100},{8,104},{12,108},{16,112},{20,116},{24,120},{28,124... | collective-permute-start | bytes 1474568 | tf_op jit(solution)/shard_map/ppermute | solution.py:33
  121.3 16.6 %collective-permute-start.25 = (bf16[640,384]{1,0:T(8,128)(2,1)}, bf16[640,384]{1,0:T(8,128)(2,1)S(1)}, u32[]{:S(2)}, u32[]{:S(2)}) collective-permute-start(bf16[640,384]{1,0:T(8,128)(2,1)} %slice.30), channel_id=1, source_target_pairs={{0,32},{4,36},{8,40},{12,44},{16,48},{20,52},{24,56},{28,60},{32,6... | collective-permute-start | bytes 1474568 | tf_op jit(solution)/shard_map/ppermute | solution.py:33
  121.7 1.1 copy-start.5
  128.5 5.5 %collective-permute-start.22 = (s32[160,128]{1,0:T(8,128)S(1)}, s32[160,128]{1,0:T(8,128)S(1)}, u32[]{:S(2)}, u32[]{:S(2)}) collective-permute-start(s32[160,128]{1,0:T(8,128)S(1)} %get-tuple-element.108), channel_id=1, source_target_pairs={{8,0},{12,4},{16,24},{20,28},{40,32},{44,36},{48,56},{52,60},{72,6... | collective-permute-start | bytes 245768 | tf_op jit(solution)/shard_map/ppermute | solution.py:33
  134.0 13.3 %copy-start.16 = (s32[160]{0:T(256)S(1)}, s32[160]{0:T(256)}, u32[]{:S(2)}) copy-start(s32[160]{0:T(256)} %param.7) | copy-start | bytes 1924
  134.0 10.4 %collective-permute-start.23 = (s32[160,128]{1,0:T(8,128)S(1)}, s32[160,128]{1,0:T(8,128)S(1)}, u32[]{:S(2)}, u32[]{:S(2)}) collective-permute-start(s32[160,128]{1,0:T(8,128)S(1)} %broadcast_select_fusion.1), channel_id=1, source_target_pairs={{0,128},{4,132},{8,136},{12,140},{16,144},{20,148},{24,152},{28,15... | collective-permute-start | bytes 245768 | tf_op jit(solution)/shard_map/ppermute | solution.py:33
  144.5 7.1 %collective-permute-start.29 = (bf16[160,5120]{1,0:T(8,128)(2,1)}, bf16[160,5120]{1,0:T(8,128)(2,1)S(1)}, u32[]{:S(2)}, u32[]{:S(2)}) collective-permute-start(bf16[160,5120]{1,0:T(8,128)(2,1)} %get-tuple-element.117), channel_id=1, source_target_pairs={{0,4},{4,0},{8,12},{12,8},{16,20},{20,16},{24,28},{28,24},{32,36},... | collective-permute-start | bytes 4915208 | tf_op jit(solution)/shard_map/ppermute | solution.py:33
  146.0 22.1 %collective-permute-start.30 = (bf16[3072,128]{1,0:T(8,128)(2,1)}, bf16[3072,128]{1,0:T(8,128)(2,1)S(1)}, u32[]{:S(2)}, u32[]{:S(2)}) collective-permute-start(bf16[3072,128]{1,0:T(8,128)(2,1)} %get-tuple-element.120), channel_id=1, source_target_pairs={{8,0},{12,4},{16,24},{20,28},{40,32},{44,36},{48,56},{52,60},{72,6... | collective-permute-start | bytes 2359304 | tf_op jit(solution)/shard_map/ppermute | solution.py:33
  147.4 7.2 %collective-permute-start.26 = (s32[2,160,128]{2,1,0:T(8,128)S(1)}, s32[2,160,128]{2,1,0:T(8,128)S(1)}, u32[]{:S(2)}, u32[]{:S(2)}) collective-permute-start(s32[2,160,128]{2,1,0:T(8,128)S(1)} %pad_add_fusion.refs_0_), channel_id=1, source_target_pairs={{0,96},{4,100},{8,104},{12,108},{16,112},{20,116},{24,120},{28,124... | collective-permute-start | bytes 491528 | tf_op jit(solution)/shard_map/ppermute | solution.py:33
  150.3 10.2 %collective-permute-start.27 = (s32[2,160,128]{2,1,0:T(8,128)S(1)}, s32[2,160,128]{2,1,0:T(8,128)S(1)}, u32[]{:S(2)}, u32[]{:S(2)}) collective-permute-start(s32[2,160,128]{2,1,0:T(8,128)S(1)} %pad_add_fusion.refs_0_), channel_id=1, source_target_pairs={{0,32},{4,36},{8,40},{12,44},{16,48},{20,52},{24,56},{28,60},{32,6... | collective-permute-start | bytes 491528 | tf_op jit(solution)/shard_map/ppermute | solution.py:33
  150.3 10.2 %collective-permute-start.28 = (s32[2,160,128]{2,1,0:T(8,128)S(1)}, s32[2,160,128]{2,1,0:T(8,128)S(1)}, u32[]{:S(2)}, u32[]{:S(2)}) collective-permute-start(s32[2,160,128]{2,1,0:T(8,128)S(1)} %pad_add_fusion.refs_0_), channel_id=1, source_target_pairs={{0,64},{4,68},{8,72},{12,76},{16,80},{20,84},{24,88},{28,92},{32,9... | collective-permute-start | bytes 491528 | tf_op jit(solution)/shard_map/ppermute | solution.py:33
  151.6 1.4 copy-start.8
  160.5 2.2 %collective-permute-start.31 = (s32[2,160,128]{2,1,0:T(8,128)S(1)}, s32[2,160,128]{2,1,0:T(8,128)S(1)}, u32[]{:S(2)}, u32[]{:S(2)}) collective-permute-start(s32[2,160,128]{2,1,0:T(8,128)S(1)} %pad_add_fusion.refs_0_), channel_id=1, source_target_pairs={{0,4},{4,0},{8,12},{12,8},{16,20},{20,16},{24,28},{28,24},{32,36},... | collective-permute-start | bytes 491528 | tf_op jit(solution)/shard_map/ppermute | solution.py:33
  161.7 1.4 collective-permute-start.32
  161.7 1.6 collective-permute-start.33
  162.2 1.4 collective-permute-start.34
  163.6 4.5 %copy-start.7 = (bf16[2048,128]{1,0:T(8,128)(2,1)S(1)}, bf16[2048,128]{1,0:T(8,128)(2,1)}, u32[]{:S(2)}) copy-start(bf16[2048,128]{1,0:T(8,128)(2,1)} %copy-done.6) | copy-start | bytes 1572868

commit v5 on v4

--- a/solution.py
+++ b/solution.py
@@ -131,8 +131,13 @@
 
 def momentum_kernel(place, *refs):
     first, second, cot_own, cot_side, early, prior_own, prior_side = refs[:7]
-    new_own, new_side, words_own, words_side = refs[-4:]
-    grad = early[...] + multiply((first, second), cot_rows(place, 6, 2, cot_own, cot_side))
+    new_own, new_side, words_own, words_side, cot = refs[-5:]
+
+    @pl.when(pl.program_id(0) == 0)
+    def _():
+        cot[...] = cot_rows(place, 6, 2, cot_own, cot_side)
+
+    grad = early[...] + multiply((first, second), cot[...])
     for i, (prior, new, words) in enumerate(
         ((prior_own, new_own, words_own), (prior_side, new_side, words_side))
     ):
@@ -180,6 +185,7 @@
                 word_spec,
                 word_spec,
             ],
+            scratch_shapes=[pltpu.VMEM((2 * share, 256), jnp.bfloat16)],
         ),
         out_shape=[
             jax.ShapeDtypeStruct((features, 128), jnp.bfloat16),

time: 170 us -> 170 us (level)
  no operation moved by 1% of the time
where the time goes in v5:
time: 170 us; the launch traced here: 169 us
  starting transfers between devices  58.8 us (35%)
  waiting for transfers between devices  54.9 us (32%)
  Pallas kernels  34.9 us (21%)
  local copies, waits for them, and re-layouts  17.3 us (10%)
  other arithmetic  2.42 us (1%)
    ppermute x35, starting transfers between devices, permute(): return lax.ppermute(array, AXES, pairs)  58.8 us
    ppermute x35, waiting for transfers between devices, permute(): return lax.ppermute(array, AXES, pairs)  54.9 us
    pallas_call x2, Pallas kernels, gather_step(): pl.pallas_call(gather_kernel, grid_spec=pltpu.PrefetchScalarGridSpec(num_...  10.9 us
    pallas_call x2, Pallas kernels, momentum_step(): pl.pallas_call(momentum_kernel, grid_spec=pltpu.PrefetchScalarGridSpec(nu...  10.1 us
    pallas_call x1, Pallas kernels, input_step(): pl.pallas_call(input_kernel, grid_spec=pltpu.PrefetchScalarGridSpec(num_s...  6.61 us
    unnamed x39, local copies, waits for them, and re-layouts  5.94 us
    pallas_call x1, Pallas kernels, vote_step(): pl.pallas_call(vote_kernel, grid_spec=pltpu.PrefetchScalarGridSpec(num_sc...  4.52 us
    slice x2, local copies, waits for them, and re-layouts, per_device(): w_far = [w_next[:quarter // 2], w_before[quarter // 2:]]  3.83 us
  transfers between devices with their start and end apart: 35, of which 15 were waited for; matrix products, arithmetic and copies ran while one was open for 7% of the time, Pallas kernels for 20%

profile of v5, /device:TPU:1, one launch (start us, length us, event | category | flops | bytes accessed | tf_op | source)
XLA Modules:
  0.0 169.4 jit_solution(260500048309026381)
XLA Ops:
  0.6 0.7 broadcast_compare_fusion
  1.3 1.6 broadcast_select_fusion.refs_0_
  3.0 1.1 constant_dynamic-slice_fusion.6
  4.1 2.6 %collective-permute-start.2 = (bf16[1280,128]{1,0:T(8,128)(2,1)S(1)}, bf16[1280,128]{1,0:T(8,128)(2,1)S(1)}, u32[]{:S(2)}, u32[]{:S(2)}) collective-permute-start(bf16[1280,128]{1,0:T(8,128)(2,1)S(1)} %constant_dynamic-slice_fusion.6), channel_id=1, source_target_pairs={{0,8},{4,12},{8,0},{12,4},{16,24},{20,28},{24,16},{28,20},{32,40},... | collective-permute-start | bytes 983048 | tf_op jit(solution)/shard_map/ppermute | solution.py:33
  6.6 4.7 %collective-permute-start.3 = (bf16[1280,128]{1,0:T(8,128)(2,1)S(1)}, bf16[1280,128]{1,0:T(8,128)(2,1)S(1)}, u32[]{:S(2)}, u32[]{:S(2)}) collective-permute-start(bf16[1280,128]{1,0:T(8,128)(2,1)S(1)} %constant_dynamic-slice_fusion.6), channel_id=1, source_target_pairs={{0,152},{4,156},{8,16},{12,20},{16,8},{20,12},{24,128},{28,132},{3... | collective-permute-start | bytes 983048 | tf_op jit(solution)/shard_map/ppermute | solution.py:33
  11.3 1.2 collective-permute-start.4
  12.5 1.9 %collective-permute-start = (bf16[160,5120]{1,0:T(8,128)(2,1)S(1)}, bf16[160,5120]{1,0:T(8,128)(2,1)}, u32[]{:S(2)}, u32[]{:S(2)}) collective-permute-start(bf16[160,5120]{1,0:T(8,128)(2,1)S(1)} %broadcast_select_fusion.refs_0_), channel_id=1, source_target_pairs={{8,16},{12,20},{16,8},{20,12},{40,48},{44,52},{48,40},{52,44},{72,... | collective-permute-start | bytes 4915208 | tf_op jit(solution)/shard_map/ppermute | solution.py:33
  14.3 2.8 %collective-permute-start.1 = (bf16[160,5120]{1,0:T(8,128)(2,1)S(1)}, bf16[160,5120]{1,0:T(8,128)(2,1)S(1)}, u32[]{:S(2)}, u32[]{:S(2)}) collective-permute-start(bf16[160,5120]{1,0:T(8,128)(2,1)S(1)} %broadcast_select_fusion.refs_0_), channel_id=1, source_target_pairs={{0,8},{4,12},{24,16},{28,20},{32,40},{36,44},{56,48},{60,52},{64,7... | collective-permute-start | bytes 4915208 | tf_op jit(solution)/shard_map/ppermute | solution.py:33
  17.1 1.9 %collective-permute-start.9 = (bf16[160,5120]{1,0:T(8,128)(2,1)S(1)}, bf16[160,5120]{1,0:T(8,128)(2,1)}, u32[]{:S(2)}, u32[]{:S(2)}) collective-permute-start(bf16[160,5120]{1,0:T(8,128)(2,1)S(1)} %broadcast_select_fusion.refs_0_), channel_id=1, source_target_pairs={{0,4},{4,0},{8,12},{12,8},{16,20},{20,16},{24,28},{28,24},{32,36},... | collective-permute-start | bytes 4915208 | tf_op jit(solution)/shard_map/ppermute | solution.py:33
  19.0 0.8 constant_dynamic-update-slice_fusion.2
  19.8 4.8 %collective-permute-done.3 = bf16[1280,128]{1,0:T(8,128)(2,1)S(1)} collective-permute-done((bf16[1280,128]{1,0:T(8,128)(2,1)S(1)}, bf16[1280,128]{1,0:T(8,128)(2,1)S(1)}, u32[]{:S(2)}, u32[]{:S(2)}) %collective-permute-start.3) | collective-permute-done | bytes 327712 | tf_op jit(solution)/shard_map/ppermute | solution.py:33
  24.6 0.8 constant_dynamic-update-slice_fusion.1
  25.4 6.3 %collective-permute-done.4 = bf16[1280,128]{1,0:T(8,128)(2,1)S(1)} collective-permute-done((bf16[1280,128]{1,0:T(8,128)(2,1)S(1)}, bf16[1280,128]{1,0:T(8,128)(2,1)S(1)}, u32[]{:S(2)}, u32[]{:S(2)}) %collective-permute-start.4) | collective-permute-done | bytes 327712 | tf_op jit(solution)/shard_map/ppermute | solution.py:33
  31.7 0.8 constant_dynamic-update-slice_fusion.here
  32.5 2.7 %collective-permute-start.5 = (bf16[1280,384]{1,0:T(8,128)(2,1)}, bf16[1280,384]{1,0:T(8,128)(2,1)}, u32[]{:S(2)}, u32[]{:S(2)}) collective-permute-start(bf16[1280,384]{1,0:T(8,128)(2,1)} %constant_dynamic-update-slice_fusion.here), channel_id=1, source_target_pairs={{0,96},{4,100},{8,104},{12,108},{16,112},{20,116},{24,120},{28,124... | collective-permute-start | bytes 2949128 | tf_op jit(solution)/shard_map/ppermute | solution.py:33
  35.1 0.9 slice_bitcast_fusion
  36.1 0.8 slice_bitcast_fusion.1
  36.9 1.7 constant_dynamic-slice_fusion.2
  38.6 16.2 %collective-permute-done.5.following = bf16[1280,384]{1,0:T(8,128)(2,1)} collective-permute-done((bf16[1280,384]{1,0:T(8,128)(2,1)}, bf16[1280,384]{1,0:T(8,128)(2,1)}, u32[]{:S(2)}, u32[]{:S(2)}) %collective-permute-start.5) | collective-permute-done | bytes 983072 | tf_op jit(solution)/shard_map/ppermute | solution.py:33
  54.8 3.1 %collective-permute-done.6.before = bf16[1280,384]{1,0:T(8,128)(2,1)} collective-permute-done((bf16[1280,384]{1,0:T(8,128)(2,1)}, bf16[1280,384]{1,0:T(8,128)(2,1)}, u32[]{:S(2)}, u32[]{:S(2)}) %collective-permute-start.6) | collective-permute-done | bytes 983072 | tf_op jit(solution)/shard_map/ppermute | solution.py:33
  58.1 2.7 %collective-permute-start.10 = (bf16[160,5120]{1,0:T(8,128)(2,1)}, bf16[160,5120]{1,0:T(8,128)(2,1)}, u32[]{:S(2)}, u32[]{:S(2)}) collective-permute-start(bf16[160,5120]{1,0:T(8,128)(2,1)} %collective-permute-done.refs_4_), channel_id=1, source_target_pairs={{0,4},{4,0},{8,12},{12,8},{16,20},{20,16},{24,28},{28,24},{32,36},... | collective-permute-start | bytes 4915208 | tf_op jit(solution)/shard_map/ppermute | solution.py:33
  60.9 4.7 %collective-permute-start.12 = (bf16[1280,128]{1,0:T(8,128)(2,1)}, bf16[1280,128]{1,0:T(8,128)(2,1)}, u32[]{:S(2)}, u32[]{:S(2)}) collective-permute-start(bf16[1280,128]{1,0:T(8,128)(2,1)} %refs_2_.1), channel_id=1, source_target_pairs={{0,8},{4,12},{24,16},{28,20},{32,40},{36,44},{56,48},{60,52},{64,7... | collective-permute-start | bytes 983048 | tf_op jit(solution)/shard_map/ppermute | solution.py:33
  65.7 0.9 slice.28
  66.6 1.5 collective-permute-start.7
  68.1 2.5 %collective-permute-start.8 = (bf16[2048,128]{1,0:T(8,128)(2,1)}, bf16[2048,128]{1,0:T(8,128)(2,1)}, u32[]{:S(2)}, u32[]{:S(2)}) collective-permute-start(bf16[2048,128]{1,0:T(8,128)(2,1)} %slice_bitcast_fusion.1), channel_id=1, source_target_pairs={{0,8},{4,12},{24,16},{28,20},{32,40},{36,44},{56,48},{60,52},{64,7... | collective-permute-start | bytes 1572872 | tf_op jit(solution)/shard_map/ppermute | solution.py:33
  70.7 1.9 %slice.29 = bf16[640,384]{1,0:T(8,128)(2,1)} slice(bf16[1280,384]{1,0:T(8,128)(2,1)} %collective-permute-done.5.following), slice={[0:640], [0:384]} | slice | bytes 983040 | tf_op jit(solution)/shard_map/slice | solution.py:404
  72.6 1.9 %slice.30 = bf16[640,384]{1,0:T(8,128)(2,1)} slice(bf16[1280,384]{1,0:T(8,128)(2,1)} %collective-permute-done.6.before), slice={[640:1280], [0:384]} | slice | bytes 983040 | tf_op jit(solution)/shard_map/slice | solution.py:404
  74.6 1.7 %collective-permute-start.14 = (bf16[320,128]{1,0:T(8,128)(2,1)S(1)}, bf16[320,128]{1,0:T(8,128)(2,1)S(1)}, u32[]{:S(2)}, u32[]{:S(2)}) collective-permute-start(bf16[320,128]{1,0:T(8,128)(2,1)S(1)} %get-tuple-element.81), channel_id=1, source_target_pairs={{0,24},{4,28},{8,16},{12,20},{16,8},{20,12},{24,0},{28,4},{32,56},... | collective-permute-start | bytes 245768 | tf_op jit(solution)/shard_map/ppermute | solution.py:33
  76.3 0.9 collective-permute-start.15
  77.2 6.3 %gather_step.3.refs_4_ = f32[3072,256]{1,0:T(8,128)} custom-call(s32[8]{0:T(128)S(1)} %stack.59.place, bf16[160,5120]{1,0:T(8,128)(2,1)S(1)} %broadcast_select_fusion.refs_0_, bf16[160,5120]{1,0:T(8,128)(2,1)} %collective-permute-done.9.refs_1_, bf16[160,5120]{1,0:T(8,128)(2,1)S(1)} %collective-permute-done.1.refs_2_, ...), custom_call_target="tpu_custom_call" | custom-call | flops 2000000000 | bytes 10000000 | tf_op jit(solution)/shard_map/gather_step/pallas_call | solution.py:109
  83.5 4.6 %gather_step.2.refs_4_ = f32[2048,256]{1,0:T(8,128)} custom-call(s32[8]{0:T(128)S(1)} %stack.59.place, bf16[160,5120]{1,0:T(8,128)(2,1)S(1)} %broadcast_select_fusion.refs_0_, bf16[160,5120]{1,0:T(8,128)(2,1)} %collective-permute-done.9.refs_1_, bf16[160,5120]{1,0:T(8,128)(2,1)S(1)} %collective-permute-done.1.refs_2_, ...), custom_call_target="tpu_custom_call" | custom-call | flops 2000000000 | bytes 10000000 | tf_op jit(solution)/shard_map/gather_step/pallas_call | solution.py:109
  88.2 0.7 collective-permute-done.14
  88.9 2.2 %collective-permute-start.18 = (bf16[160,2048]{1,0:T(8,128)(2,1)}, bf16[160,2048]{1,0:T(8,128)(2,1)}, u32[]{:S(2)}, u32[]{:S(2)}) collective-permute-start(bf16[160,2048]{1,0:T(8,128)(2,1)} %collective-permute-done.7.refs_0_), channel_id=1, source_target_pairs={{0,4},{4,0},{8,12},{12,8},{16,20},{20,16},{24,28},{28,24},{32,36},... | collective-permute-start | bytes 1966088 | tf_op jit(solution)/shard_map/ppermute | solution.py:33
  91.2 1.0 slice.31
  92.2 0.7 collective-permute-start.16
  93.0 4.9 %collective-permute-start.17 = (bf16[3072,128]{1,0:T(8,128)(2,1)}, bf16[3072,128]{1,0:T(8,128)(2,1)S(1)}, u32[]{:S(2)}, u32[]{:S(2)}) collective-permute-start(bf16[3072,128]{1,0:T(8,128)(2,1)} %slice_bitcast_fusion), channel_id=1, source_target_pairs={{0,8},{4,12},{24,16},{28,20},{32,40},{36,44},{56,48},{60,52},{64,7... | collective-permute-start | bytes 2359304 | tf_op jit(solution)/shard_map/ppermute | solution.py:33
  97.9 4.4 %momentum_step.2 = (bf16[5120,128]{1,0:T(8,128)(2,1)}, bf16[2048,128]{1,0:T(8,128)(2,1)S(1)}, s32[160,128]{1,0:T(8,128)S(1)}, s32[160,128]{1,0:T(8,128)S(1)}) custom-call(s32[8]{0:T(128)S(1)} %stack.59.place, bf16[160,2048]{1,0:T(8,128)(2,1)} %collective-permute-done.7.refs_0_, bf16[160,2048]{1,0:T(8,128)(2,1)} %collective-permute-done.18.refs_1_, ...), custom_call_target="tpu_custom_call" | custom-call | flops 2000000000 | bytes 10000000 | tf_op jit(solution)/shard_map/momentum_step/pallas_call | solution.py:167
  102.4 1.5 collective-permute-start.19
  104.0 10.1 %collective-permute-done.17.refs_6_ = bf16[3072,128]{1,0:T(8,128)(2,1)S(1)} collective-permute-done((bf16[3072,128]{1,0:T(8,128)(2,1)}, bf16[3072,128]{1,0:T(8,128)(2,1)S(1)}, u32[]{:S(2)}, u32[]{:S(2)}) %collective-permute-start.17) | collective-permute-done | bytes 786464 | tf_op jit(solution)/shard_map/ppermute | solution.py:33
  114.2 0.9 copy-done.4
  115.1 1.5 collective-permute-done.19.low
  116.6 0.8 copy-done.6
  117.4 2.0 %collective-permute-start.21 = (bf16[160,3072]{1,0:T(8,128)(2,1)S(1)}, bf16[160,3072]{1,0:T(8,128)(2,1)}, u32[]{:S(2)}, u32[]{:S(2)}) collective-permute-start(bf16[160,3072]{1,0:T(8,128)(2,1)S(1)} %collective-permute-done.16.refs_0_), channel_id=1, source_target_pairs={{0,4},{4,0},{8,12},{12,8},{16,20},{20,16},{24,28},{28,24},{32,36},... | collective-permute-start | bytes 2949128 | tf_op jit(solution)/shard_map/ppermute | solution.py:33
  119.4 1.9 %collective-permute-start.24 = (bf16[640,384]{1,0:T(8,128)(2,1)}, bf16[640,384]{1,0:T(8,128)(2,1)S(1)}, u32[]{:S(2)}, u32[]{:S(2)}) collective-permute-start(bf16[640,384]{1,0:T(8,128)(2,1)} %slice.29), channel_id=1, source_target_pairs={{0,96},{4,100},{8,104},{12,108},{16,112},{20,116},{24,120},{28,124... | collective-permute-start | bytes 1474568 | tf_op jit(solution)/shard_map/ppermute | solution.py:33
  121.3 0.4 collective-permute-done.21.refs_1_
  121.7 1.1 copy-done.5
  122.9 5.7 %momentum_step.3 = (bf16[5120,128]{1,0:T(8,128)(2,1)}, bf16[3072,128]{1,0:T(8,128)(2,1)}, s32[160,128]{1,0:T(8,128)S(1)}, s32[160,128]{1,0:T(8,128)S(1)}) custom-call(s32[8]{0:T(128)S(1)} %stack.59.place, bf16[160,3072]{1,0:T(8,128)(2,1)S(1)} %collective-permute-done.16.refs_0_, ...), custom_call_target="tpu_custom_call", output_to_operand_aliasing={{0}: (8, {}), {2}: (9, {}), {3}: (10, {})} | custom-call | flops 2000000000 | bytes 10000000 | tf_op jit(solution)/shard_map/momentum_step/pallas_call | solution.py:167
  128.5 1.3 collective-permute-start.22
  129.9 4.2 %collective-permute-done.22 = s32[160,128]{1,0:T(8,128)S(1)} collective-permute-done((s32[160,128]{1,0:T(8,128)S(1)}, s32[160,128]{1,0:T(8,128)S(1)}, u32[]{:S(2)}, u32[]{:S(2)}) %collective-permute-start.22) | collective-permute-done | bytes 81952 | tf_op jit(solution)/shard_map/ppermute | solution.py:33
  134.1 3.8 %collective-permute-start.23 = (s32[160,128]{1,0:T(8,128)S(1)}, s32[160,128]{1,0:T(8,128)S(1)}, u32[]{:S(2)}, u32[]{:S(2)}) collective-permute-start(s32[160,128]{1,0:T(8,128)S(1)} %broadcast_select_fusion.1), channel_id=1, source_target_pairs={{0,128},{4,132},{8,136},{12,140},{16,144},{20,148},{24,152},{28,15... | collective-permute-start | bytes 245768 | tf_op jit(solution)/shard_map/ppermute | solution.py:33
  137.9 6.6 %input_step.1 = (bf16[160,5120]{1,0:T(8,128)(2,1)}, bf16[160,5120]{1,0:T(8,128)(2,1)}) custom-call(s32[4]{0:T(128)S(1)} %pad_add_fusion.1.place, bf16[320,512]{1,0:T(8,128)(2,1)S(1)} %pad_maximum_fusion.cot, bf16[5120,128]{1,0:T(8,128)(2,1)} %refs_8_.1, bf16[1280,384]{1,0:T(8,128)(2,1)} %constant_dynamic-update-slice_fusion.here, ...), custom_call_target="tpu_custom_call" | custom-call | flops 1677721600 | bytes 8519680 | tf_op jit(solution)/shard_map/input_step/pallas_call | solution.py:318
  144.5 1.6 collective-permute-start.29
  146.1 1.3 collective-permute-start.30
  147.5 2.9 %collective-permute-start.26 = (s32[2,160,128]{2,1,0:T(8,128)S(1)}, s32[2,160,128]{2,1,0:T(8,128)S(1)}, u32[]{:S(2)}, u32[]{:S(2)}) collective-permute-start(s32[2,160,128]{2,1,0:T(8,128)S(1)} %pad_add_fusion.refs_0_), channel_id=1, source_target_pairs={{0,96},{4,100},{8,104},{12,108},{16,112},{20,116},{24,120},{28,124... | collective-permute-start | bytes 491528 | tf_op jit(solution)/shard_map/ppermute | solution.py:33
  150.3 1.3 collective-permute-start.28
  151.6 1.4 copy-done.8
  153.0 1.6 total_step.1
  154.7 5.8 %collective-permute-done.27.refs_2_ = s32[2,160,128]{2,1,0:T(8,128)S(1)} collective-permute-done((s32[2,160,128]{2,1,0:T(8,128)S(1)}, s32[2,160,128]{2,1,0:T(8,128)S(1)}, u32[]{:S(2)}, u32[]{:S(2)}) %collective-permute-start.27) | collective-permute-done | bytes 163872 | tf_op jit(solution)/shard_map/ppermute | solution.py:33
  160.6 1.1 collective-permute-start.31
  161.7 0.5 collective-permute-start.33
  162.2 0.5 collective-permute-done.31.refs_4_
  162.7 0.4 collective-permute-done.32.refs_5_
  163.6 4.5 %vote_step.1 = bf16[5120,256]{1,0:T(8,128)(2,1)} custom-call(s32[1]{0:T(128)} %bitcast.19.core, s32[2,160,128]{2,1,0:T(8,128)S(1)} %pad_add_fusion.refs_0_, s32[2,160,128]{2,1,0:T(8,128)S(1)} %collective-permute-done.26.refs_1_, s32[2,160,128]{2,1,0:T(8,128)S(1)} %collective-permute-done.27.refs_2_, s32[2,160,128]{2,1,0:T(8,128)S(1)} %collective-permute-done.28.refs_3_, ...), custom_call_target="tpu_custom_call" | custom-call | flops 2000000000 | bytes 10000000 | tf_op jit(solution)/shard_map/vote_step/pallas_call | solution.py:281
  168.1 1.1 fill_step.1
  (73 shorter events, 1.6 us)
Async XLA Ops:
  2.9 32.2 %copy-start = (bf16[1,5120,128]{2,1,0:T(8,128)(2,1)S(1)}, bf16[1,5120,128]{2,1,0:T(8,128)(2,1)}, u32[]{:S(2)}) copy-start(bf16[1,5120,128]{2,1,0:T(8,128)(2,1)} %param.9) | copy-start | bytes 3932164
  4.1 13.1 %collective-permute-start.2 = (bf16[1280,128]{1,0:T(8,128)(2,1)S(1)}, bf16[1280,128]{1,0:T(8,128)(2,1)S(1)}, u32[]{:S(2)}, u32[]{:S(2)}) collective-permute-start(bf16[1280,128]{1,0:T(8,128)(2,1)S(1)} %constant_dynamic-slice_fusion.6), channel_id=1, source_target_pairs={{0,8},{4,12},{8,0},{12,4},{16,24},{20,28},{24,16},{28,20},{32,40},... | collective-permute-start | bytes 983048 | tf_op jit(solution)/shard_map/ppermute | solution.py:33
  6.6 18.0 %collective-permute-start.3 = (bf16[1280,128]{1,0:T(8,128)(2,1)S(1)}, bf16[1280,128]{1,0:T(8,128)(2,1)S(1)}, u32[]{:S(2)}, u32[]{:S(2)}) collective-permute-start(bf16[1280,128]{1,0:T(8,128)(2,1)S(1)} %constant_dynamic-slice_fusion.6), channel_id=1, source_target_pairs={{0,152},{4,156},{8,16},{12,20},{16,8},{20,12},{24,128},{28,132},{3... | collective-permute-start | bytes 983048 | tf_op jit(solution)/shard_map/ppermute | solution.py:33
  11.3 20.4 %collective-permute-start.4 = (bf16[1280,128]{1,0:T(8,128)(2,1)S(1)}, bf16[1280,128]{1,0:T(8,128)(2,1)S(1)}, u32[]{:S(2)}, u32[]{:S(2)}) collective-permute-start(bf16[1280,128]{1,0:T(8,128)(2,1)S(1)} %constant_dynamic-slice_fusion.6), channel_id=1, source_target_pairs={{0,144},{4,148},{8,152},{12,156},{16,128},{20,132},{24,136},{28,14... | collective-permute-start | bytes 983048 | tf_op jit(solution)/shard_map/ppermute | solution.py:33
  12.5 45.4 %collective-permute-start = (bf16[160,5120]{1,0:T(8,128)(2,1)S(1)}, bf16[160,5120]{1,0:T(8,128)(2,1)}, u32[]{:S(2)}, u32[]{:S(2)}) collective-permute-start(bf16[160,5120]{1,0:T(8,128)(2,1)S(1)} %broadcast_select_fusion.refs_0_), channel_id=1, source_target_pairs={{8,16},{12,20},{16,8},{20,12},{40,48},{44,52},{48,40},{52,44},{72,... | collective-permute-start | bytes 4915208 | tf_op jit(solution)/shard_map/ppermute | solution.py:33
  14.3 43.8 %collective-permute-start.1 = (bf16[160,5120]{1,0:T(8,128)(2,1)S(1)}, bf16[160,5120]{1,0:T(8,128)(2,1)S(1)}, u32[]{:S(2)}, u32[]{:S(2)}) collective-permute-start(bf16[160,5120]{1,0:T(8,128)(2,1)S(1)} %broadcast_select_fusion.refs_0_), channel_id=1, source_target_pairs={{0,8},{4,12},{24,16},{28,20},{32,40},{36,44},{56,48},{60,52},{64,7... | collective-permute-start | bytes 4915208 | tf_op jit(solution)/shard_map/ppermute | solution.py:33
  17.1 50.9 %collective-permute-start.9 = (bf16[160,5120]{1,0:T(8,128)(2,1)S(1)}, bf16[160,5120]{1,0:T(8,128)(2,1)}, u32[]{:S(2)}, u32[]{:S(2)}) collective-permute-start(bf16[160,5120]{1,0:T(8,128)(2,1)S(1)} %broadcast_select_fusion.refs_0_), channel_id=1, source_target_pairs={{0,4},{4,0},{8,12},{12,8},{16,20},{20,16},{24,28},{28,24},{32,36},... | collective-permute-start | bytes 4915208 | tf_op jit(solution)/shard_map/ppermute | solution.py:33
  32.5 22.3 %collective-permute-start.5 = (bf16[1280,384]{1,0:T(8,128)(2,1)}, bf16[1280,384]{1,0:T(8,128)(2,1)}, u32[]{:S(2)}, u32[]{:S(2)}) collective-permute-start(bf16[1280,384]{1,0:T(8,128)(2,1)} %constant_dynamic-update-slice_fusion.here), channel_id=1, source_target_pairs={{0,96},{4,100},{8,104},{12,108},{16,112},{20,116},{24,120},{28,124... | collective-permute-start | bytes 2949128 | tf_op jit(solution)/shard_map/ppermute | solution.py:33
  35.1 22.8 %collective-permute-start.6 = (bf16[1280,384]{1,0:T(8,128)(2,1)}, bf16[1280,384]{1,0:T(8,128)(2,1)}, u32[]{:S(2)}, u32[]{:S(2)}) collective-permute-start(bf16[1280,384]{1,0:T(8,128)(2,1)} %constant_dynamic-update-slice_fusion.here), channel_id=1, source_target_pairs={{0,32},{4,36},{8,40},{12,44},{16,48},{20,52},{24,56},{28,60},{32,6... | collective-permute-start | bytes 2949128 | tf_op jit(solution)/shard_map/ppermute | solution.py:33
  58.1 16.4 %collective-permute-start.10 = (bf16[160,5120]{1,0:T(8,128)(2,1)}, bf16[160,5120]{1,0:T(8,128)(2,1)}, u32[]{:S(2)}, u32[]{:S(2)}) collective-permute-start(bf16[160,5120]{1,0:T(8,128)(2,1)} %collective-permute-done.refs_4_), channel_id=1, source_target_pairs={{0,4},{4,0},{8,12},{12,8},{16,20},{20,16},{24,28},{28,24},{32,36},... | collective-permute-start | bytes 4915208 | tf_op jit(solution)/shard_map/ppermute | solution.py:33
  60.8 13.7 %collective-permute-start.11 = (bf16[160,5120]{1,0:T(8,128)(2,1)S(1)}, bf16[160,5120]{1,0:T(8,128)(2,1)}, u32[]{:S(2)}, u32[]{:S(2)}) collective-permute-start(bf16[160,5120]{1,0:T(8,128)(2,1)S(1)} %collective-permute-done.1.refs_2_), channel_id=1, source_target_pairs={{0,4},{4,0},{8,12},{12,8},{16,20},{20,16},{24,28},{28,24},{32,36},... | collective-permute-start | bytes 4915208 | tf_op jit(solution)/shard_map/ppermute | solution.py:33
  60.9 15.4 %collective-permute-start.12 = (bf16[1280,128]{1,0:T(8,128)(2,1)}, bf16[1280,128]{1,0:T(8,128)(2,1)}, u32[]{:S(2)}, u32[]{:S(2)}) collective-permute-start(bf16[1280,128]{1,0:T(8,128)(2,1)} %refs_2_.1), channel_id=1, source_target_pairs={{0,8},{4,12},{24,16},{28,20},{32,40},{36,44},{56,48},{60,52},{64,7... | collective-permute-start | bytes 983048 | tf_op jit(solution)/shard_map/ppermute | solution.py:33
  66.6 21.6 %collective-permute-start.7 = (bf16[160,2048]{1,0:T(8,128)(2,1)}, bf16[160,2048]{1,0:T(8,128)(2,1)}, u32[]{:S(2)}, u32[]{:S(2)}) collective-permute-start(bf16[160,2048]{1,0:T(8,128)(2,1)} %slice.28), channel_id=1, source_target_pairs={{8,16},{12,20},{16,8},{20,12},{40,48},{44,52},{48,40},{52,44},{72,... | collective-permute-start | bytes 1966088 | tf_op jit(solution)/shard_map/ppermute | solution.py:33
  68.1 20.1 %collective-permute-start.8 = (bf16[2048,128]{1,0:T(8,128)(2,1)}, bf16[2048,128]{1,0:T(8,128)(2,1)}, u32[]{:S(2)}, u32[]{:S(2)}) collective-permute-start(bf16[2048,128]{1,0:T(8,128)(2,1)} %slice_bitcast_fusion.1), channel_id=1, source_target_pairs={{0,8},{4,12},{24,16},{28,20},{32,40},{36,44},{56,48},{60,52},{64,7... | collective-permute-start | bytes 1572872 | tf_op jit(solution)/shard_map/ppermute | solution.py:33
  70.6 3.8 %copy-start.9 = (bf16[320,128]{1,0:T(8,128)(2,1)S(1)}, bf16[320,128]{1,0:T(8,128)(2,1)}, u32[]{:S(2)}) copy-start(bf16[320,128]{1,0:T(8,128)(2,1)} %get-tuple-element.80) | copy-start | bytes 245764
  70.6 6.6 %copy-start.2 = (bf16[1280,128]{1,0:T(8,128)(2,1)S(1)}, bf16[1280,128]{1,0:T(8,128)(2,1)}, u32[]{:S(2)}) copy-start(bf16[1280,128]{1,0:T(8,128)(2,1)} %refs_2_.1) | copy-start | bytes 983044
  74.5 13.7 %collective-permute-start.13 = (bf16[320,128]{1,0:T(8,128)(2,1)S(1)}, bf16[320,128]{1,0:T(8,128)(2,1)S(1)}, u32[]{:S(2)}, u32[]{:S(2)}) collective-permute-start(bf16[320,128]{1,0:T(8,128)(2,1)S(1)} %copy-done.9), channel_id=1, source_target_pairs={{0,8},{4,12},{8,0},{12,4},{16,24},{20,28},{24,16},{28,20},{32,40},... | collective-permute-start | bytes 245768 | tf_op jit(solution)/shard_map/ppermute | solution.py:33
  74.6 14.3 %collective-permute-start.14 = (bf16[320,128]{1,0:T(8,128)(2,1)S(1)}, bf16[320,128]{1,0:T(8,128)(2,1)S(1)}, u32[]{:S(2)}, u32[]{:S(2)}) collective-permute-start(bf16[320,128]{1,0:T(8,128)(2,1)S(1)} %get-tuple-element.81), channel_id=1, source_target_pairs={{0,24},{4,28},{8,16},{12,20},{16,8},{20,12},{24,0},{28,4},{32,56},... | collective-permute-start | bytes 245768 | tf_op jit(solution)/shard_map/ppermute | solution.py:33
  76.3 12.6 %collective-permute-start.15 = (bf16[320,128]{1,0:T(8,128)(2,1)S(1)}, bf16[320,128]{1,0:T(8,128)(2,1)S(1)}, u32[]{:S(2)}, u32[]{:S(2)}) collective-permute-start(bf16[320,128]{1,0:T(8,128)(2,1)S(1)} %get-tuple-element.82), channel_id=1, source_target_pairs={{0,16},{4,20},{8,24},{12,28},{16,0},{20,4},{24,8},{28,12},{32,48},... | collective-permute-start | bytes 245768 | tf_op jit(solution)/shard_map/ppermute | solution.py:33
  88.2 9.7 %copy-start.1 = (bf16[1,5120,128]{2,1,0:T(8,128)(2,1)S(1)}, bf16[1,5120,128]{2,1,0:T(8,128)(2,1)}, u32[]{:S(2)}) copy-start(bf16[1,5120,128]{2,1,0:T(8,128)(2,1)} %param.9) | copy-start | bytes 3932164
  88.2 9.7 %copy-start.3 = (bf16[1280,128]{1,0:T(8,128)(2,1)S(1)}, bf16[1280,128]{1,0:T(8,128)(2,1)}, u32[]{:S(2)}) copy-start(bf16[1280,128]{1,0:T(8,128)(2,1)} %refs_2_.1) | copy-start | bytes 983044
  88.2 4.0 %copy-start.10 = (bf16[320,128]{1,0:T(8,128)(2,1)}, bf16[320,128]{1,0:T(8,128)(2,1)S(1)}, u32[]{:S(2)}) copy-start(bf16[320,128]{1,0:T(8,128)(2,1)S(1)} %collective-permute-done.13) | copy-start | bytes 245764
  88.9 3.3 %copy-start.12 = (bf16[320,128]{1,0:T(8,128)(2,1)}, bf16[320,128]{1,0:T(8,128)(2,1)S(1)}, u32[]{:S(2)}) copy-start(bf16[320,128]{1,0:T(8,128)(2,1)S(1)} %collective-permute-done.14) | copy-start | bytes 245764
  88.9 3.3 %copy-start.14 = (bf16[320,128]{1,0:T(8,128)(2,1)}, bf16[320,128]{1,0:T(8,128)(2,1)S(1)}, u32[]{:S(2)}) copy-start(bf16[320,128]{1,0:T(8,128)(2,1)S(1)} %collective-permute-done.15) | copy-start | bytes 245764
  88.9 9.0 %collective-permute-start.18 = (bf16[160,2048]{1,0:T(8,128)(2,1)}, bf16[160,2048]{1,0:T(8,128)(2,1)}, u32[]{:S(2)}, u32[]{:S(2)}) collective-permute-start(bf16[160,2048]{1,0:T(8,128)(2,1)} %collective-permute-done.7.refs_0_), channel_id=1, source_target_pairs={{0,4},{4,0},{8,12},{12,8},{16,20},{20,16},{24,28},{28,24},{32,36},... | collective-permute-start | bytes 1966088 | tf_op jit(solution)/shard_map/ppermute | solution.py:33
  91.1 12.9 %collective-permute-start.20 = (bf16[5120,128]{1,0:T(8,128)(2,1)}, bf16[5120,128]{1,0:T(8,128)(2,1)}, u32[]{:S(2)}, u32[]{:S(2)}) collective-permute-start(bf16[5120,128]{1,0:T(8,128)(2,1)} %refs_8_.1), channel_id=1, source_target_pairs={{0,4},{4,0},{8,12},{12,8},{16,20},{20,16},{24,28},{28,24},{32,36},... | collective-permute-start | bytes 3932168 | tf_op jit(solution)/shard_map/ppermute | solution.py:33
  92.2 22.8 %collective-permute-start.16 = (bf16[160,3072]{1,0:T(8,128)(2,1)}, bf16[160,3072]{1,0:T(8,128)(2,1)S(1)}, u32[]{:S(2)}, u32[]{:S(2)}) collective-permute-start(bf16[160,3072]{1,0:T(8,128)(2,1)} %slice.31), channel_id=1, source_target_pairs={{8,16},{12,20},{16,8},{20,12},{40,48},{44,52},{48,40},{52,44},{72,... | collective-permute-start | bytes 2949128 | tf_op jit(solution)/shard_map/ppermute | solution.py:33
  93.0 21.2 %collective-permute-start.17 = (bf16[3072,128]{1,0:T(8,128)(2,1)}, bf16[3072,128]{1,0:T(8,128)(2,1)S(1)}, u32[]{:S(2)}, u32[]{:S(2)}) collective-permute-start(bf16[3072,128]{1,0:T(8,128)(2,1)} %slice_bitcast_fusion), channel_id=1, source_target_pairs={{0,8},{4,12},{24,16},{28,20},{32,40},{36,44},{56,48},{60,52},{64,7... | collective-permute-start | bytes 2359304 | tf_op jit(solution)/shard_map/ppermute | solution.py:33
  97.9 5.9 %copy-start.11 = (bf16[320,128]{1,0:T(8,128)(2,1)S(1)}, bf16[320,128]{1,0:T(8,128)(2,1)}, u32[]{:S(2)}) copy-start(bf16[320,128]{1,0:T(8,128)(2,1)} %copy-done.10) | copy-start | bytes 245764
  97.9 6.0 %copy-start.13 = (bf16[320,128]{1,0:T(8,128)(2,1)S(1)}, bf16[320,128]{1,0:T(8,128)(2,1)}, u32[]{:S(2)}) copy-start(bf16[320,128]{1,0:T(8,128)(2,1)} %copy-done.12) | copy-start | bytes 245764
  97.9 6.0 %copy-start.15 = (bf16[320,128]{1,0:T(8,128)(2,1)S(1)}, bf16[320,128]{1,0:T(8,128)(2,1)}, u32[]{:S(2)}) copy-start(bf16[320,128]{1,0:T(8,128)(2,1)} %copy-done.14) | copy-start | bytes 245764
  102.4 14.2 %collective-permute-start.19 = (bf16[2048,128]{1,0:T(8,128)(2,1)S(1)}, bf16[2048,128]{1,0:T(8,128)(2,1)S(1)}, u32[]{:S(2)}, u32[]{:S(2)}) collective-permute-start(bf16[2048,128]{1,0:T(8,128)(2,1)S(1)} %get-tuple-element.90), channel_id=1, source_target_pairs={{8,0},{12,4},{16,24},{20,28},{40,32},{44,36},{48,56},{52,60},{72,6... | collective-permute-start | bytes 1572872 | tf_op jit(solution)/shard_map/ppermute | solution.py:33
  114.2 0.9 copy-start.4
  116.6 0.8 copy-start.6
  117.4 4.3 %collective-permute-start.21 = (bf16[160,3072]{1,0:T(8,128)(2,1)S(1)}, bf16[160,3072]{1,0:T(8,128)(2,1)}, u32[]{:S(2)}, u32[]{:S(2)}) collective-permute-start(bf16[160,3072]{1,0:T(8,128)(2,1)S(1)} %collective-permute-done.16.refs_0_), channel_id=1, source_target_pairs={{0,4},{4,0},{8,12},{12,8},{16,20},{20,16},{24,28},{28,24},{32,36},... | collective-permute-start | bytes 2949128 | tf_op jit(solution)/shard_map/ppermute | solution.py:33
  119.4 18.5 %collective-permute-start.24 = (bf16[640,384]{1,0:T(8,128)(2,1)}, bf16[640,384]{1,0:T(8,128)(2,1)S(1)}, u32[]{:S(2)}, u32[]{:S(2)}) collective-permute-start(bf16[640,384]{1,0:T(8,128)(2,1)} %slice.29), channel_id=1, source_target_pairs={{0,96},{4,100},{8,104},{12,108},{16,112},{20,116},{24,120},{28,124... | collective-permute-start | bytes 1474568 | tf_op jit(solution)/shard_map/ppermute | solution.py:33
  121.3 16.6 %collective-permute-start.25 = (bf16[640,384]{1,0:T(8,128)(2,1)}, bf16[640,384]{1,0:T(8,128)(2,1)S(1)}, u32[]{:S(2)}, u32[]{:S(2)}) collective-permute-start(bf16[640,384]{1,0:T(8,128)(2,1)} %slice.30), channel_id=1, source_target_pairs={{0,32},{4,36},{8,40},{12,44},{16,48},{20,52},{24,56},{28,60},{32,6... | collective-permute-start | bytes 1474568 | tf_op jit(solution)/shard_map/ppermute | solution.py:33
  121.7 1.1 copy-start.5
  128.5 5.5 %collective-permute-start.22 = (s32[160,128]{1,0:T(8,128)S(1)}, s32[160,128]{1,0:T(8,128)S(1)}, u32[]{:S(2)}, u32[]{:S(2)}) collective-permute-start(s32[160,128]{1,0:T(8,128)S(1)} %get-tuple-element.108), channel_id=1, source_target_pairs={{8,0},{12,4},{16,24},{20,28},{40,32},{44,36},{48,56},{52,60},{72,6... | collective-permute-start | bytes 245768 | tf_op jit(solution)/shard_map/ppermute | solution.py:33
  134.1 13.3 %copy-start.16 = (s32[160]{0:T(256)S(1)}, s32[160]{0:T(256)}, u32[]{:S(2)}) copy-start(s32[160]{0:T(256)} %param.7) | copy-start | bytes 1924
  134.1 10.4 %collective-permute-start.23 = (s32[160,128]{1,0:T(8,128)S(1)}, s32[160,128]{1,0:T(8,128)S(1)}, u32[]{:S(2)}, u32[]{:S(2)}) collective-permute-start(s32[160,128]{1,0:T(8,128)S(1)} %broadcast_select_fusion.1), channel_id=1, source_target_pairs={{0,128},{4,132},{8,136},{12,140},{16,144},{20,148},{24,152},{28,15... | collective-permute-start | bytes 245768 | tf_op jit(solution)/shard_map/ppermute | solution.py:33
  144.5 7.1 %collective-permute-start.29 = (bf16[160,5120]{1,0:T(8,128)(2,1)}, bf16[160,5120]{1,0:T(8,128)(2,1)S(1)}, u32[]{:S(2)}, u32[]{:S(2)}) collective-permute-start(bf16[160,5120]{1,0:T(8,128)(2,1)} %get-tuple-element.117), channel_id=1, source_target_pairs={{0,4},{4,0},{8,12},{12,8},{16,20},{20,16},{24,28},{28,24},{32,36},... | collective-permute-start | bytes 4915208 | tf_op jit(solution)/shard_map/ppermute | solution.py:33
  146.1 22.1 %collective-permute-start.30 = (bf16[3072,128]{1,0:T(8,128)(2,1)}, bf16[3072,128]{1,0:T(8,128)(2,1)S(1)}, u32[]{:S(2)}, u32[]{:S(2)}) collective-permute-start(bf16[3072,128]{1,0:T(8,128)(2,1)} %get-tuple-element.120), channel_id=1, source_target_pairs={{8,0},{12,4},{16,24},{20,28},{40,32},{44,36},{48,56},{52,60},{72,6... | collective-permute-start | bytes 2359304 | tf_op jit(solution)/shard_map/ppermute | solution.py:33
  147.5 7.2 %collective-permute-start.26 = (s32[2,160,128]{2,1,0:T(8,128)S(1)}, s32[2,160,128]{2,1,0:T(8,128)S(1)}, u32[]{:S(2)}, u32[]{:S(2)}) collective-permute-start(s32[2,160,128]{2,1,0:T(8,128)S(1)} %pad_add_fusion.refs_0_), channel_id=1, source_target_pairs={{0,96},{4,100},{8,104},{12,108},{16,112},{20,116},{24,120},{28,124... | collective-permute-start | bytes 491528 | tf_op jit(solution)/shard_map/ppermute | solution.py:33
  150.3 10.2 %collective-permute-start.27 = (s32[2,160,128]{2,1,0:T(8,128)S(1)}, s32[2,160,128]{2,1,0:T(8,128)S(1)}, u32[]{:S(2)}, u32[]{:S(2)}) collective-permute-start(s32[2,160,128]{2,1,0:T(8,128)S(1)} %pad_add_fusion.refs_0_), channel_id=1, source_target_pairs={{0,32},{4,36},{8,40},{12,44},{16,48},{20,52},{24,56},{28,60},{32,6... | collective-permute-start | bytes 491528 | tf_op jit(solution)/shard_map/ppermute | solution.py:33
  150.3 10.2 %collective-permute-start.28 = (s32[2,160,128]{2,1,0:T(8,128)S(1)}, s32[2,160,128]{2,1,0:T(8,128)S(1)}, u32[]{:S(2)}, u32[]{:S(2)}) collective-permute-start(s32[2,160,128]{2,1,0:T(8,128)S(1)} %pad_add_fusion.refs_0_), channel_id=1, source_target_pairs={{0,64},{4,68},{8,72},{12,76},{16,80},{20,84},{24,88},{28,92},{32,9... | collective-permute-start | bytes 491528 | tf_op jit(solution)/shard_map/ppermute | solution.py:33
  151.6 1.4 copy-start.8
  160.6 2.2 %collective-permute-start.31 = (s32[2,160,128]{2,1,0:T(8,128)S(1)}, s32[2,160,128]{2,1,0:T(8,128)S(1)}, u32[]{:S(2)}, u32[]{:S(2)}) collective-permute-start(s32[2,160,128]{2,1,0:T(8,128)S(1)} %pad_add_fusion.refs_0_), channel_id=1, source_target_pairs={{0,4},{4,0},{8,12},{12,8},{16,20},{20,16},{24,28},{28,24},{32,36},... | collective-permute-start | bytes 491528 | tf_op jit(solution)/shard_map/ppermute | solution.py:33
  161.7 1.4 collective-permute-start.32
  161.7 1.6 collective-permute-start.33
  162.2 1.4 collective-permute-start.34
  163.6 4.5 %copy-start.7 = (bf16[2048,128]{1,0:T(8,128)(2,1)S(1)}, bf16[2048,128]{1,0:T(8,128)(2,1)}, u32[]{:S(2)}) copy-start(bf16[2048,128]{1,0:T(8,128)(2,1)} %copy-done.6) | copy-start | bytes 1572868
